TPU v7x, 256 devices: a whole 4x4x8 slice. The times are simulated.
256 devices in a mesh: chan: 8 (over z), win: 4 (over x), freq: 8 (over y, core).
Axes of the slice: x: 4, y: 4, z: 8, core: 2. Of those that a mesh axis runs over, the one named last changes fastest.
Arguments:
- spectrogram: bfloat16 [16384, 32, 1024], P('chan', 'win', 'freq'), may hold values from 0 to 200, as said below
- window_factor: bfloat16 [32, 128], P(('win', 'freq')), may hold values from 0.099609375 to 1
- freq_factor: bfloat16 [1024, 128], P('freq'), may hold values from 0.099609375 to 1
- channel_factor: float32 [16384, 128], P(('chan', 'win', 'freq')), may hold values from 0 to 0.06
Outputs:
- channel_out: float32 [16384, 128], P(('chan', 'win', 'freq'))
- column_scale: float32 [128], replicated
Inputs may be any that keep to these rules, and one draw needn't show every extreme that they name: `spectrogram`: nonnegative.
All inputs are finite; a program needn't handle non-finite values.
Results may differ from a plain program's by a relative error of at most 0.0022.
Values may be sent and summed in bfloat16 or wider, within the bound.
No kernel may reach another device: no remote copies, remote signals or barrier semaphores. Data moves between devices by JAX's collectives and lax.ppermute only.
A program may use at most 64 MiB of HBM per device.

v0:
```python
import jax
import jax.numpy as jnp
from jax import lax
from jax.sharding import PartitionSpec as P


def gram_of(factor):
    return lax.dot_general(
        factor, factor, (((0,), (0,)), ((), ())), preferred_element_type=jnp.float32
    )


def body(spectrogram, window_factor, freq_factor, channel_factor):
    chan_rows, win_rows, freq_rows = spectrogram.shape
    rank_cols = freq_factor.shape[1]
    block = lax.all_gather(window_factor, "freq", axis=0, tiled=True)
    window_gram = lax.psum(gram_of(block), "win")
    freq_gram = lax.psum(gram_of(freq_factor), "freq")
    gram = window_gram * freq_gram
    product = block.astype(jnp.float32)[:, None, :] * freq_factor.astype(jnp.float32)[None, :, :]
    khatri_rao = product.astype(jnp.bfloat16).reshape(win_rows * freq_rows, rank_cols)
    flat = spectrogram.reshape(
        lax.axis_size(("win", "freq")) * channel_factor.shape[0], win_rows * freq_rows
    )
    mttkrp = lax.psum_scatter(
        jnp.dot(flat, khatri_rao, preferred_element_type=jnp.float32),
        ("win", "freq"),
        scatter_dimension=0,
        tiled=True,
    )
    factor = channel_factor
    for index in range(rank_cols):
        fitted = jnp.dot(factor, gram[:, index], precision=lax.Precision.HIGHEST)
        fresh = jnp.maximum(
            factor[:, index] + (mttkrp[:, index] - fitted) / gram[index, index], 0.0
        )
        factor = factor.at[:, index].set(fresh)
    squares = lax.psum(jnp.sum(factor * factor, axis=0), ("chan", "win", "freq"))
    total_rows = (
        factor.shape[0] * lax.axis_size("chan") * lax.axis_size("win") * lax.axis_size("freq")
    )
    column_scale = jnp.sqrt(squares / total_rows + 1e-06)
    return (factor / column_scale[None, :], column_scale)


def solution(mesh):
    placed = (
        P("chan", "win", "freq"),
        P(("win", "freq"), None),
        P("freq", None),
        P(("chan", "win", "freq"), None),
    )
    return jax.shard_map(
        body,
        mesh=mesh,
        in_specs=placed,
        out_specs=(P(("chan", "win", "freq"), None), P()),
        check_vma=False,
    )
```

profile of v0, /device:TPU:2, one launch (start us, length us, event | category | flops | bytes accessed | tf_op | source)
XLA Modules:
  0.0 421.7 jit_solution(13966255076985883434)
XLA Ops:
  8.0 1.6 fusion.920
  9.8 10.9 %all-gather = bf16[8,1,128]{2,1,0:T(2,128)(2,1)S(1)} all-gather(bf16[1,1,128]{2,1,0:T(2,128)(2,1)} %bitcast.3466), channel_id=1, replica_groups=mesh['chan'=8,'win'=4,'freq'=8] {'freq'}, dimensions={0}, use_global_device_ids=true | all-gather | bytes 2304 | tf_op jit(solution)/shard_map/all_gather | solution.py:16
  22.5 3.7 fusion.2
  112.7 11.5 %all-reduce.3.cloned.1.call-done = f32[128,128]{1,0:T(8,128)} async-done(((f32[128,128]{1,0:T(8,128)}), f32[128,128]{1,0:T(8,128)}) %all-reduce.3.cloned.1.call-update) | async-done | bytes 65552 | tf_op jit(solution)/shard_map/psum | solution.py:17
  135.5 1.8 fusion.919
  138.4 2.3 fusion.918
  142.2 2.3 fusion.917
  153.1 1.5 fusion.771
  167.4 1.5 fusion.761
  180.3 1.5 fusion.752
  183.2 1.5 fusion.750
  188.9 1.5 fusion.746
  210.5 1.5 fusion.731
  212.2 1.5 fusion.730
  215.1 1.5 fusion.728
  216.7 1.6 fusion.727
  218.2 1.5 fusion.726
  224.1 1.5 fusion.722
  239.9 1.5 fusion.711
  254.3 1.5 fusion.701
  257.3 1.5 fusion.699
  268.8 1.5 fusion.691
  271.7 1.5 fusion.689
  290.4 1.5 fusion.676
  294.8 1.5 fusion.673
  300.6 1.5 fusion.669
  302.2 1.5 fusion.668
  305.2 1.5 fusion.666
  308.1 1.5 fusion.664
  331.0 1.5 fusion.648
  332.5 1.5 fusion.647
  337.9 75.6 %psum.23 = f32[128]{0:T(128)S(1)} all-reduce(f32[128]{0:T(128)S(1)} %multiply_reduce_fusion), channel_id=1, replica_groups=mesh['chan'=8,'win'=4,'freq'=8] {'chan','win','freq'}, use_global_device_ids=true, to_apply=%region_131.0 | all-reduce | flops 128 | bytes 1024 | tf_op jit(solution)/shard_map/psum | solution.py:38
  (529 shorter events, 258.7 us)
Async XLA Ops:
  8.0 104.7 %all-reduce.5.cloned.1.call-start = ((), (), s32[]{:S(2)}) async-start(), calls=%async_computation.2 | async-start | bytes 131072 | tf_op jit(solution)/shard_map/psum | solution.py:18
  9.7 114.5 %all-reduce.3.cloned.1.call-start = ((), (), s32[]{:S(2)}) async-start(), calls=%async_computation.1 | async-start | bytes 131072 | tf_op jit(solution)/shard_map/psum | solution.py:17
  21.5 114.0 %reduce-scatter.4.cloned.1.call-start = ((), (), s32[]{:S(2)}) async-start(), calls=%async_computation.3 | async-start | bytes 1081344
  22.4 90.2 %copy-start.1 = (f32[64,128]{1,0:T(8,128)S(1)}, f32[64,128]{1,0:T(8,128)}, u32[]{:S(2)}) copy-start(f32[64,128]{1,0:T(8,128)} %param.263) | copy-start | bytes 98308
  135.5 10.5 %copy-start = (f32[64,128]{1,0:T(8,128)S(1)}, f32[64,128]{1,0:T(8,128)}, u32[]{:S(2)}) copy-start(f32[64,128]{1,0:T(8,128)} %reduce-scatter.4.cloned.1.call-done) | copy-start | bytes 98308
  413.5 0.8 copy-start.2
Sparse Core Ops, SparseCore 0:
  11.1 66.8 all-reduce.4
  80.4 43.7 all-reduce.2
Sparse Core Ops, SparseCore 1:
  27.6 85.6 reduce-scatter.3
where the time goes:
time: 427 us; the launch traced here: 422 us
  matrix products  186 us (44%)
  blocking collectives  86.5 us (20%)
  other arithmetic  86.1 us (20%)
  local copies, waits for them, and re-layouts  33.8 us (8%)
  between operations  17.2 us (4%)
  waiting for transfers between devices  11.6 us (3%)
    dot_general x128, matrix products, body(): fitted = jnp.dot(factor, gram[:, index], precision=lax.Precision.HIGHEST)  180 us
    another operation x127, other arithmetic  85 us
    psum x1, blocking collectives, body(): lax.psum(jnp.sum(factor * factor, axis=0), ('chan', 'win', 'freq'))  75.6 us
    psum x1, waiting for transfers between devices, body(): window_gram = lax.psum(gram_of(block), 'win')  11.5 us
    unnamed x137, local copies, waits for them, and re-layouts  11.3 us
    all_gather x1, blocking collectives, body(): block = lax.all_gather(window_factor, 'freq', axis=0, tiled=True)  10.9 us
  transfers between devices with their start and end apart: 3, of which 1 were waited for; matrix products, arithmetic and copies ran while one was open for 24% of the time, Pallas kernels for 0%

commit v1 on v0

v1 whole, which is shorter than its diff:
```python
import jax
import jax.numpy as jnp
from jax import lax
from jax.experimental import pallas as pl
from jax.experimental.pallas import tpu as pltpu
from jax.sharding import Mesh, PartitionSpec as P

f32 = jnp.float32
DOWN = 0.125


def on_vmem(kernel, outs, *args):
    place = pl.BlockSpec(memory_space=pltpu.VMEM)
    return pl.pallas_call(
        kernel,
        out_shape=outs,
        in_specs=[place] * len(args),
        out_specs=jax.tree.map(lambda _: place, outs),
        compiler_params=pltpu.CompilerParams(vmem_limit_bytes=48 * 2**20),
    )(*args)


def swap(value, axis, distance):
    count = lax.axis_size(axis)
    return lax.ppermute(value, axis, [(i, i ^ distance) for i in range(count)])


def gram_kernel(own_ref, far_ref, window_ref, factor_ref, lower_ref, upper_ref, inverse_ref):
    def gram_of(block):
        return lax.dot_general(
            block, block, (((0,), (0,)), ((), ())), preferred_element_type=f32
        )

    rank = own_ref.shape[-1]
    gram = (gram_of(own_ref[...]) + gram_of(far_ref[...])) * gram_of(window_ref[...])
    row = lax.broadcasted_iota(jnp.int32, (rank, rank), 0)
    col = lax.broadcasted_iota(jnp.int32, (rank, rank), 1)
    inverse = 1.0 / jnp.sum(jnp.where(row == col, gram, 0.0), axis=1, keepdims=True)
    lower_ref[...] = jnp.where(row > col, gram, 0.0) * inverse
    upper = jnp.where(row < col, gram, 0.0) * inverse
    upper_ref[...] = lax.dot_general(
        upper,
        factor_ref[...],
        (((1,), (1,)), ((), ())),
        precision=lax.Precision.HIGHEST,
        preferred_element_type=f32,
    )
    inverse_ref[...] = jnp.broadcast_to(inverse, inverse_ref.shape)


def sweep_kernel(a_ref, b_ref, c_ref, d_ref, lower_ref, upper_ref, inverse_ref, out_ref, square_ref):
    mttkrp = (a_ref[...] + b_ref[...]) + (c_ref[...] + d_ref[...])
    start = mttkrp.T * inverse_ref[...] - upper_ref[...]
    rank, rows = start.shape
    parts = [start[8 * i : 8 * i + 8] for i in range(rank // 8)]
    for j in range(rank):
        block, lane = divmod(j, 8)
        fresh = jnp.maximum(parts[block], 0.0)[lane : lane + 1, :]
        fresh = jnp.broadcast_to(fresh, (8, rows))
        for i in range(block, rank // 8):
            column = jnp.broadcast_to(lower_ref[8 * i : 8 * i + 8, j : j + 1], (8, rows))
            parts[i] = parts[i] - column * fresh
    updated = jnp.maximum(jnp.concatenate(parts, axis=0), 0.0).T
    out_ref[...] = updated
    square_ref[...] = jnp.sum(updated * updated, axis=0, keepdims=True)


def body(spectrogram, window_factor, freq_factor, channel_factor):
    chan_rows, win_rows, freq_rows = spectrogram.shape
    rows, rank = channel_factor.shape
    xs, ys = lax.axis_size("x"), lax.axis_size("y")
    x, y, c = lax.axis_index("x"), lax.axis_index("y"), lax.axis_index("c")

    line = [window_factor] + [swap(window_factor, "y", k) for k in (1, 3, 2)]
    line = jnp.concatenate(line, axis=0)
    pair = swap(line, "c", 1)
    slot = jnp.arange(win_rows)[:, None]
    block = jnp.zeros((win_rows, rank), f32)
    for i, k in enumerate((0, 1, 3, 2)):
        block = jnp.where(slot == 2 * (y ^ k) + c, line[i : i + 1].astype(f32), block)
        block = jnp.where(slot == 2 * (y ^ k) + 1 - c, pair[i : i + 1].astype(f32), block)
    product = block[:, None, :] * freq_factor.astype(f32)[None, :, :]
    khatri_rao = product.astype(jnp.bfloat16).reshape(win_rows * freq_rows, rank)
    flat = spectrogram.reshape(chan_rows, win_rows * freq_rows)
    part = jnp.dot(flat, khatri_rao, preferred_element_type=f32)

    freqs = [freq_factor] + [swap(freq_factor, "y", k) for k in (1, 3, 2)]
    freqs = jnp.concatenate(freqs, axis=0)
    freqs_far = swap(freqs, "c", 1)
    block = block.astype(jnp.bfloat16)
    windows = jnp.concatenate([block] + [swap(block, "x", k) for k in (1, 3, 2)], axis=0)
    like = jax.ShapeDtypeStruct((rank, rows), f32)
    lower, upper, inverse = on_vmem(
        gram_kernel,
        (jax.ShapeDtypeStruct((rank, rank), f32), like, like),
        freqs,
        freqs_far,
        windows,
        channel_factor,
    )

    part = part.reshape(xs, ys, 2, rows, rank)
    mine = lax.dynamic_index_in_dim(part, c, 2, keepdims=False)
    other = lax.dynamic_index_in_dim(part, 1 - c, 2, keepdims=False)
    part = mine + swap(other, "c", 1)
    total = lax.dynamic_index_in_dim(part, y, 1, keepdims=False)
    small = (part * DOWN).astype(jnp.float16)
    for k in (1, 3, 2):
        piece = lax.dynamic_index_in_dim(small, y ^ k, 1, keepdims=False)
        total = total + swap(piece, "y", k).astype(f32) * (1.0 / DOWN)
    pieces = [lax.dynamic_index_in_dim(total, x, 0, keepdims=False)]
    for k in (1, 3, 2):
        piece = lax.dynamic_index_in_dim(total, x ^ k, 0, keepdims=False)
        pieces.append(swap(piece, "x", k))

    updated, squares = on_vmem(
        sweep_kernel,
        (jax.ShapeDtypeStruct((rows, rank), f32), jax.ShapeDtypeStruct((1, rank), f32)),
        *pieces,
        lower,
        upper,
        inverse,
    )
    squares = squares + swap(squares, "c", 1)
    chips = xs * ys * lax.axis_size("z")
    squares = lax.all_to_all(
        jnp.broadcast_to(squares, (chips, rank)), ("z", "x", "y"), 0, 0, tiled=True
    ).sum(axis=0)
    column_scale = jnp.sqrt(squares / (chips * 2 * rows) + 1e-06)
    return (updated / column_scale[None, :], column_scale)


def solution(mesh):
    chan, win, freq = mesh.devices.shape
    fine = Mesh(mesh.devices.reshape(chan, win, freq // 2, 2), ("z", "x", "y", "c"))
    placed = (
        P("z", "x", ("y", "c")),
        P(("x", "y", "c"), None),
        P(("y", "c"), None),
        P(("z", "x", "y", "c"), None),
    )
    return jax.shard_map(
        body,
        mesh=fine,
        in_specs=placed,
        out_specs=(P(("z", "x", "y", "c"), None), P()),
        check_vma=False,
    )
```

time: 427 us -> 67.9 us (0.16); the launches traced: 422 us -> 67 us
  matrix products: 186 us -> 3.71 us
  other arithmetic: 86.1 us -> 2.31 us
  blocking collectives: 86.5 us -> 26.1 us
  local copies, waits for them, and re-layouts: 33.8 us -> 1.38 us
  starting transfers between devices: 0.12 us -> 21.5 us
  between operations: 17.2 us -> 0.82 us
    dot_general x131 -> x1, matrix products: 186 us -> 3.71 us  [body(): part = jnp.dot(flat, khatri_rao, preferred_element_type=f32)]
    another operation x127 -> x0, other arithmetic: 85 us -> none
    psum x1 -> x0, blocking collectives: 75.6 us -> none  [body(): lax.psum(jnp.sum(factor * factor, axis=0), ('chan', 'win', 'freq'))]
    all_to_all x0 -> x1, blocking collectives: none -> 26.1 us  [body(): lax.all_to_all(jnp.broadcast_to(squares, (chips, rank)), ('z', 'x', 'y'),...]
    ppermute x0 -> x19, starting transfers between devices: none -> 21.5 us  [swap(): return lax.ppermute(value, axis, [(i, i ^ distance) for i in range(count)])]
    slice x21 -> x0, local copies, waits for them, and re-layouts: 18 us -> none  [the longest x7 7.65 us: body(): mttkrp[:, index] - fitted]
    psum x2 -> x0, waiting for transfers between devices: 11.5 us -> none  [the longest x1 11.5 us: body(): window_gram = lax.psum(gram_of(block), 'win')]
    unnamed x137 -> x9, local copies, waits for them, and re-layouts: 11.3 us -> 0.04 us
  transfers between devices with their start and end apart: 3 -> 19, of which waited for: 1 -> 9; matrix products, arithmetic and copies ran while one was open for 24% -> 3% of each run, Pallas kernels for 0% -> 1%
where the time goes in v1:
time: 67.9 us; the launch traced here: 67 us
  blocking collectives  26.1 us (38%)
  starting transfers between devices  21.5 us (32%)
  waiting for transfers between devices  9.11 us (13%)
  matrix products  3.71 us (5%)
  other arithmetic  2.31 us (3%)
  Pallas kernels  2.12 us (3%)
  local copies, waits for them, and re-layouts  1.38 us (2%)
  between operations  0.82 us (1%)
    all_to_all x1, blocking collectives, body(): lax.all_to_all(jnp.broadcast_to(squares, (chips, rank)), ('z', 'x', 'y'),...  26.1 us
    ppermute x19, starting transfers between devices, swap(): return lax.ppermute(value, axis, [(i, i ^ distance) for i in range(count)])  21.5 us
    ppermute x19, waiting for transfers between devices, swap(): return lax.ppermute(value, axis, [(i, i ^ distance) for i in range(count)])  9.11 us
    dot_general x1, matrix products, body(): part = jnp.dot(flat, khatri_rao, preferred_element_type=f32)  3.71 us
    pallas_call x2, Pallas kernels, on_vmem(): pl.pallas_call(kernel, out_shape=outs, in_specs=[place] * len(args), out_...  2.12 us
  transfers between devices with their start and end apart: 19, of which 9 were waited for; matrix products, arithmetic and copies ran while one was open for 3% of the time, Pallas kernels for 1%

profile of v1, /device:TPU:2, one launch (start us, length us, event | category | flops | bytes accessed | tf_op | source)
XLA Modules:
  0.0 67.0 jit_solution(10001525803643184515)
XLA Ops:
  0.6 1.7 %collective-permute-start = (bf16[1,128]{1,0:T(2,128)(2,1)}, bf16[1,128]{1,0:T(2,128)(2,1)S(1)}, u32[]{:S(2)}, u32[]{:S(2)}) collective-permute-start(bf16[1,128]{1,0:T(2,128)(2,1)} %param.5), channel_id=1, source_target_pairs={{0,2},{2,0},{4,6},{6,4},{1,3},{3,1},{5,7},{7,5},{8,10},{10,8},{12,... | collective-permute-start | bytes 776 | tf_op jit(solution)/shard_map/ppermute | solution.py:25
  2.3 2.2 %collective-permute-start.1 = (bf16[1,128]{1,0:T(2,128)(2,1)}, bf16[1,128]{1,0:T(2,128)(2,1)S(1)}, u32[]{:S(2)}, u32[]{:S(2)}) collective-permute-start(bf16[1,128]{1,0:T(2,128)(2,1)} %param.5), channel_id=1, source_target_pairs={{0,6},{2,4},{4,2},{6,0},{1,7},{3,5},{5,3},{7,1},{8,14},{10,12},{12... | collective-permute-start | bytes 776 | tf_op jit(solution)/shard_map/ppermute | solution.py:25
  4.5 0.7 %collective-permute-start.2 = (bf16[1,128]{1,0:T(2,128)(2,1)}, bf16[1,128]{1,0:T(2,128)(2,1)S(1)}, u32[]{:S(2)}, u32[]{:S(2)}) collective-permute-start(bf16[1,128]{1,0:T(2,128)(2,1)} %param.5), channel_id=1, source_target_pairs={{0,4},{2,6},{4,0},{6,2},{1,5},{3,7},{5,1},{7,3},{8,12},{10,14},{12... | collective-permute-start | bytes 776 | tf_op jit(solution)/shard_map/ppermute | solution.py:25
  5.2 0.7 %bitcast_convert_fusion = f32[128]{0:T(128)S(1)} fusion(bf16[1,128]{1,0:T(2,128)(2,1)} %param.5), kind=kLoop, calls=%fused_computation.27 | loop fusion | flops 128 | bytes 768 | tf_op jit(solution)/shard_map/jit(_where)/broadcast_in_dim | solution.py:80
  5.9 0.8 %copy.14 = f32[128,128]{0,1:T(8,128)S(1)} copy(bf16[128,128]{1,0:T(8,128)(2,1)} %param.6) | data formatting | bytes 98304 | tf_op jit(solution)/shard_map/convert_element_type | solution.py:82
  6.8 0.4 collective-permute-done.1
  7.2 2.5 %collective-permute-done.2 = bf16[1,128]{1,0:T(2,128)(2,1)S(1)} collective-permute-done((bf16[1,128]{1,0:T(2,128)(2,1)}, bf16[1,128]{1,0:T(2,128)(2,1)S(1)}, u32[]{:S(2)}, u32[]{:S(2)}) %collective-permute-start.2) | collective-permute-done | bytes 288 | tf_op jit(solution)/shard_map/ppermute | solution.py:25
  9.7 0.7 pad_maximum_fusion.1
  10.4 1.1 %collective-permute-done.3 = bf16[4,128]{1,0:T(4,128)(2,1)S(1)} collective-permute-done((bf16[4,128]{1,0:T(4,128)(2,1)S(1)}, bf16[4,128]{1,0:T(4,128)(2,1)S(1)}, u32[]{:S(2)}, u32[]{:S(2)}) %collective-permute-start.3) | collective-permute-done | bytes 1056 | tf_op jit(solution)/shard_map/ppermute | solution.py:25
  11.6 3.7 %fusion.2 = f32[2048,128]{0,1:T(8,128)S(1)} fusion(bf16[2048,8,128]{2,1,0:T(8,128)(2,1)} %param.4, f32[128,128]{0,1:T(8,128)S(1)} %copy.14, f32[8,128]{1,0:T(8,128)S(1)} %get-tuple-element.13), kind=kOutput, calls=%fused_computation.2 | convolution fusion | flops 537133056 | bytes 5312512 | tf_op jit(solution)/shard_map/dot_general | solution.py:85
  15.3 0.3 copy.16
  16.0 0.7 %collective-permute-start.11 = (bf16[128,128]{1,0:T(8,128)(2,1)S(1)}, bf16[128,128]{1,0:T(8,128)(2,1)S(1)}, u32[]{:S(2)}, u32[]{:S(2)}) collective-permute-start(bf16[128,128]{1,0:T(8,128)(2,1)S(1)} %copy-done.1), channel_id=1, source_target_pairs={{0,2},{2,0},{4,6},{6,4},{1,3},{3,1},{5,7},{7,5},{8,10},{10,8},{12,... | collective-permute-start | bytes 98312 | tf_op jit(solution)/shard_map/ppermute | solution.py:25
  16.6 0.6 collective-permute-start.12
  17.2 2.8 %collective-permute-start.13 = (bf16[128,128]{1,0:T(8,128)(2,1)S(1)}, bf16[128,128]{1,0:T(8,128)(2,1)S(1)}, u32[]{:S(2)}, u32[]{:S(2)}) collective-permute-start(bf16[128,128]{1,0:T(8,128)(2,1)S(1)} %copy-done.1), channel_id=1, source_target_pairs={{0,4},{2,6},{4,0},{6,2},{1,5},{3,7},{5,1},{7,3},{8,12},{10,14},{12... | collective-permute-start | bytes 98312 | tf_op jit(solution)/shard_map/ppermute | solution.py:25
  20.1 0.5 collective-permute-start.15
  20.6 2.2 %collective-permute-start.16 = (bf16[8,128]{1,0:T(8,128)(2,1)S(1)}, bf16[8,128]{1,0:T(8,128)(2,1)S(1)}, u32[]{:S(2)}, u32[]{:S(2)}) collective-permute-start(bf16[8,128]{1,0:T(8,128)(2,1)S(1)} %get-tuple-element.12), channel_id=1, source_target_pairs={{0,24},{8,16},{16,8},{24,0},{1,25},{9,17},{17,9},{25,1},{2,26},{10... | collective-permute-start | bytes 6152 | tf_op jit(solution)/shard_map/ppermute | solution.py:25
  23.0 0.8 %collective-permute-start.5 = (f16[4,64,128]{2,1,0:T(8,128)(2,1)S(1)}, f16[4,64,128]{2,1,0:T(8,128)(2,1)S(1)}, u32[]{:S(2)}, u32[]{:S(2)}) collective-permute-start(f16[4,64,128]{2,1,0:T(8,128)(2,1)S(1)} %get-tuple-element.16), channel_id=1, source_target_pairs={{0,2},{2,0},{4,6},{6,4},{1,3},{3,1},{5,7},{7,5},{8,10},{10,8},{12,... | collective-permute-start | bytes 196616 | tf_op jit(solution)/shard_map/ppermute | solution.py:25
  23.7 0.6 collective-permute-start.6
  24.3 2.8 %collective-permute-start.7 = (f16[4,64,128]{2,1,0:T(8,128)(2,1)S(1)}, f16[4,64,128]{2,1,0:T(8,128)(2,1)S(1)}, u32[]{:S(2)}, u32[]{:S(2)}) collective-permute-start(f16[4,64,128]{2,1,0:T(8,128)(2,1)S(1)} %get-tuple-element.17), channel_id=1, source_target_pairs={{0,4},{2,6},{4,0},{6,2},{1,5},{3,7},{5,1},{7,3},{8,12},{10,14},{12... | collective-permute-start | bytes 196616 | tf_op jit(solution)/shard_map/ppermute | solution.py:25
  27.1 0.7 %collective-permute-done.5 = f16[4,64,128]{2,1,0:T(8,128)(2,1)S(1)} collective-permute-done((f16[4,64,128]{2,1,0:T(8,128)(2,1)S(1)}, f16[4,64,128]{2,1,0:T(8,128)(2,1)S(1)}, u32[]{:S(2)}, u32[]{:S(2)}) %collective-permute-start.5) | collective-permute-done | bytes 65568 | tf_op jit(solution)/shard_map/ppermute | solution.py:25
  27.9 1.4 %collective-permute-start.17 = (bf16[8,128]{1,0:T(8,128)(2,1)S(1)}, bf16[8,128]{1,0:T(8,128)(2,1)S(1)}, u32[]{:S(2)}, u32[]{:S(2)}) collective-permute-start(bf16[8,128]{1,0:T(8,128)(2,1)S(1)} %get-tuple-element.12), channel_id=1, source_target_pairs={{0,16},{8,24},{16,0},{24,8},{1,17},{9,25},{17,1},{25,9},{2,18},{10... | collective-permute-start | bytes 6152 | tf_op jit(solution)/shard_map/ppermute | solution.py:25
  29.3 0.8 %collective-permute-done.7 = f16[4,64,128]{2,1,0:T(8,128)(2,1)S(1)} collective-permute-done((f16[4,64,128]{2,1,0:T(8,128)(2,1)S(1)}, f16[4,64,128]{2,1,0:T(8,128)(2,1)S(1)}, u32[]{:S(2)}, u32[]{:S(2)}) %collective-permute-start.7) | collective-permute-done | bytes 65568 | tf_op jit(solution)/shard_map/ppermute | solution.py:25
  30.2 1.5 %collective-permute-start.10 = (f32[64,128]{1,0:T(8,128)S(1)}, f32[64,128]{1,0:T(8,128)S(1)}, u32[]{:S(2)}, u32[]{:S(2)}) collective-permute-start(f32[64,128]{1,0:T(8,128)S(1)} %get-tuple-element.19), channel_id=1, source_target_pairs={{0,16},{8,24},{16,0},{24,8},{1,17},{9,25},{17,1},{25,9},{2,18},{10... | collective-permute-start | bytes 98312 | tf_op jit(solution)/shard_map/ppermute | solution.py:25
  31.7 1.9 %collective-permute-start.8 = (f32[64,128]{1,0:T(8,128)S(1)}, f32[64,128]{1,0:T(8,128)S(1)}, u32[]{:S(2)}, u32[]{:S(2)}) collective-permute-start(f32[64,128]{1,0:T(8,128)S(1)} %get-tuple-element.21), channel_id=1, source_target_pairs={{0,8},{8,0},{16,24},{24,16},{1,9},{9,1},{17,25},{25,17},{2,10},{10... | collective-permute-start | bytes 98312 | tf_op jit(solution)/shard_map/ppermute | solution.py:25
  33.6 0.8 %collective-permute-start.9 = (f32[64,128]{1,0:T(8,128)S(1)}, f32[64,128]{1,0:T(8,128)S(1)}, u32[]{:S(2)}, u32[]{:S(2)}) collective-permute-start(f32[64,128]{1,0:T(8,128)S(1)} %get-tuple-element.20), channel_id=1, source_target_pairs={{0,24},{8,16},{16,8},{24,0},{1,25},{9,17},{17,9},{25,1},{2,26},{10... | collective-permute-start | bytes 98312 | tf_op jit(solution)/shard_map/ppermute | solution.py:25
  34.4 0.6 shard_map.59
  35.0 0.7 %collective-permute-done.10.d_ref = f32[64,128]{1,0:T(8,128)S(1)} collective-permute-done((f32[64,128]{1,0:T(8,128)S(1)}, f32[64,128]{1,0:T(8,128)S(1)}, u32[]{:S(2)}, u32[]{:S(2)}) %collective-permute-start.10) | collective-permute-done | bytes 32800 | tf_op jit(solution)/shard_map/ppermute | solution.py:25
  35.8 1.7 %collective-permute-done.9.c_ref = f32[64,128]{1,0:T(8,128)S(1)} collective-permute-done((f32[64,128]{1,0:T(8,128)S(1)}, f32[64,128]{1,0:T(8,128)S(1)}, u32[]{:S(2)}, u32[]{:S(2)}) %collective-permute-start.9) | collective-permute-done | bytes 32800 | tf_op jit(solution)/shard_map/ppermute | solution.py:25
  37.5 1.5 %shard_map.60 = (f32[64,128]{1,0:T(8,128)S(1)}, f32[1,128]{1,0:T(1,128)S(1)}) custom-call(f32[64,128]{1,0:T(8,128)S(1)} %get-tuple-element.22.a_ref, f32[64,128]{1,0:T(8,128)S(1)} %collective-permute-done.8.b_ref, f32[64,128]{1,0:T(8,128)S(1)} %collective-permute-done.9.c_ref, f32[64,128]{1,0:T(8,128)S(1)} %collective-permute-done.10.d_ref, ...), custom_call_target="tpu_custom_call" | custom-call | tf_op jit(solution)/shard_map/pallas_call | solution.py:14
  39.1 1.1 %collective-permute-done.18 = f32[1,128]{1,0:T(1,128)S(1)} collective-permute-done((f32[1,128]{1,0:T(1,128)S(1)}, f32[1,128]{1,0:T(1,128)S(1)}, u32[]{:S(2)}, u32[]{:S(2)}) %collective-permute-start.18) | collective-permute-done | bytes 544 | tf_op jit(solution)/shard_map/ppermute | solution.py:25
  40.3 26.1 %all_to_all.6 = f32[128,1,128]{2,1,0:T(1,128)S(1)} all-to-all(f32[128,1,128]{2,1,0:T(1,128)S(1)} %broadcast_in_dim.163), channel_id=1, replica_groups=mesh['z'=8,'x'=4,'y'=4,'c'=2] {'z','x','y'}, dimensions={0} | all-to-all | bytes 131072 | tf_op jit(solution)/shard_map/all_to_all | solution.py:126
  66.4 0.6 broadcast_divide_fusion
  (44 shorter events, 1.0 us)
Async XLA Ops:
  0.6 6.2 %collective-permute-start = (bf16[1,128]{1,0:T(2,128)(2,1)}, bf16[1,128]{1,0:T(2,128)(2,1)S(1)}, u32[]{:S(2)}, u32[]{:S(2)}) collective-permute-start(bf16[1,128]{1,0:T(2,128)(2,1)} %param.5), channel_id=1, source_target_pairs={{0,2},{2,0},{4,6},{6,4},{1,3},{3,1},{5,7},{7,5},{8,10},{10,8},{12,... | collective-permute-start | bytes 776 | tf_op jit(solution)/shard_map/ppermute | solution.py:25
  2.3 4.9 %collective-permute-start.1 = (bf16[1,128]{1,0:T(2,128)(2,1)}, bf16[1,128]{1,0:T(2,128)(2,1)S(1)}, u32[]{:S(2)}, u32[]{:S(2)}) collective-permute-start(bf16[1,128]{1,0:T(2,128)(2,1)} %param.5), channel_id=1, source_target_pairs={{0,6},{2,4},{4,2},{6,0},{1,7},{3,5},{5,3},{7,1},{8,14},{10,12},{12... | collective-permute-start | bytes 776 | tf_op jit(solution)/shard_map/ppermute | solution.py:25
  4.5 5.2 %collective-permute-start.2 = (bf16[1,128]{1,0:T(2,128)(2,1)}, bf16[1,128]{1,0:T(2,128)(2,1)S(1)}, u32[]{:S(2)}, u32[]{:S(2)}) collective-permute-start(bf16[1,128]{1,0:T(2,128)(2,1)} %param.5), channel_id=1, source_target_pairs={{0,4},{2,6},{4,0},{6,2},{1,5},{3,7},{5,1},{7,3},{8,12},{10,14},{12... | collective-permute-start | bytes 776 | tf_op jit(solution)/shard_map/ppermute | solution.py:25
  10.3 1.1 %collective-permute-start.3 = (bf16[4,128]{1,0:T(4,128)(2,1)S(1)}, bf16[4,128]{1,0:T(4,128)(2,1)S(1)}, u32[]{:S(2)}, u32[]{:S(2)}) collective-permute-start(bf16[4,128]{1,0:T(4,128)(2,1)S(1)} %pad_maximum_fusion.1), channel_id=1, source_target_pairs={{0,1},{1,0},{2,3},{3,2},{4,5},{5,4},{6,7},{7,6},{8,9},{9,8},{10,11... | collective-permute-start | bytes 3080 | tf_op jit(solution)/shard_map/ppermute | solution.py:25
  11.5 4.4 %copy-start.1 = (bf16[128,128]{1,0:T(8,128)(2,1)S(1)}, bf16[128,128]{1,0:T(8,128)(2,1)}, u32[]{:S(2)}) copy-start(bf16[128,128]{1,0:T(8,128)(2,1)} %param.6) | copy-start | bytes 98308
  15.3 19.1 %copy-start = (f32[64,128]{1,0:T(8,128)S(1)}, f32[64,128]{1,0:T(8,128)}, u32[]{:S(2)}) copy-start(f32[64,128]{1,0:T(8,128)} %factor_ref.1) | copy-start | bytes 98308
  15.7 7.1 %collective-permute-start.4 = (f32[4,4,64,128]{3,2,1,0:T(8,128)S(1)}, f32[4,4,64,128]{3,2,1,0:T(8,128)S(1)}, u32[]{:S(2)}, u32[]{:S(2)}) collective-permute-start(f32[4,4,64,128]{3,2,1,0:T(8,128)S(1)} %dynamic-slice_bitcast_fusion), channel_id=1, source_target_pairs={{0,1},{1,0},{2,3},{3,2},{4,5},{5,4},{6,7},{7,6},{8,9},{9,8},{10,11... | collective-permute-start | bytes 1572872 | tf_op jit(solution)/shard_map/ppermute | solution.py:25
  16.0 4.6 %collective-permute-start.11 = (bf16[128,128]{1,0:T(8,128)(2,1)S(1)}, bf16[128,128]{1,0:T(8,128)(2,1)S(1)}, u32[]{:S(2)}, u32[]{:S(2)}) collective-permute-start(bf16[128,128]{1,0:T(8,128)(2,1)S(1)} %copy-done.1), channel_id=1, source_target_pairs={{0,2},{2,0},{4,6},{6,4},{1,3},{3,1},{5,7},{7,5},{8,10},{10,8},{12,... | collective-permute-start | bytes 98312 | tf_op jit(solution)/shard_map/ppermute | solution.py:25
  16.6 6.1 %collective-permute-start.12 = (bf16[128,128]{1,0:T(8,128)(2,1)S(1)}, bf16[128,128]{1,0:T(8,128)(2,1)S(1)}, u32[]{:S(2)}, u32[]{:S(2)}) collective-permute-start(bf16[128,128]{1,0:T(8,128)(2,1)S(1)} %copy-done.1), channel_id=1, source_target_pairs={{0,6},{2,4},{4,2},{6,0},{1,7},{3,5},{5,3},{7,1},{8,14},{10,12},{12... | collective-permute-start | bytes 98312 | tf_op jit(solution)/shard_map/ppermute | solution.py:25
  17.2 7.1 %collective-permute-start.13 = (bf16[128,128]{1,0:T(8,128)(2,1)S(1)}, bf16[128,128]{1,0:T(8,128)(2,1)S(1)}, u32[]{:S(2)}, u32[]{:S(2)}) collective-permute-start(bf16[128,128]{1,0:T(8,128)(2,1)S(1)} %copy-done.1), channel_id=1, source_target_pairs={{0,4},{2,6},{4,0},{6,2},{1,5},{3,7},{5,1},{7,3},{8,12},{10,14},{12... | collective-permute-start | bytes 98312 | tf_op jit(solution)/shard_map/ppermute | solution.py:25
  20.1 11.6 %collective-permute-start.15 = (bf16[8,128]{1,0:T(8,128)(2,1)S(1)}, bf16[8,128]{1,0:T(8,128)(2,1)S(1)}, u32[]{:S(2)}, u32[]{:S(2)}) collective-permute-start(bf16[8,128]{1,0:T(8,128)(2,1)S(1)} %get-tuple-element.12), channel_id=1, source_target_pairs={{0,8},{8,0},{16,24},{24,16},{1,9},{9,1},{17,25},{25,17},{2,10},{10... | collective-permute-start | bytes 6152 | tf_op jit(solution)/shard_map/ppermute | solution.py:25
  20.6 13.0 %collective-permute-start.16 = (bf16[8,128]{1,0:T(8,128)(2,1)S(1)}, bf16[8,128]{1,0:T(8,128)(2,1)S(1)}, u32[]{:S(2)}, u32[]{:S(2)}) collective-permute-start(bf16[8,128]{1,0:T(8,128)(2,1)S(1)} %get-tuple-element.12), channel_id=1, source_target_pairs={{0,24},{8,16},{16,8},{24,0},{1,25},{9,17},{17,9},{25,1},{2,26},{10... | collective-permute-start | bytes 6152 | tf_op jit(solution)/shard_map/ppermute | solution.py:25
  23.0 4.9 %collective-permute-start.5 = (f16[4,64,128]{2,1,0:T(8,128)(2,1)S(1)}, f16[4,64,128]{2,1,0:T(8,128)(2,1)S(1)}, u32[]{:S(2)}, u32[]{:S(2)}) collective-permute-start(f16[4,64,128]{2,1,0:T(8,128)(2,1)S(1)} %get-tuple-element.16), channel_id=1, source_target_pairs={{0,2},{2,0},{4,6},{6,4},{1,3},{3,1},{5,7},{7,5},{8,10},{10,8},{12,... | collective-permute-start | bytes 196616 | tf_op jit(solution)/shard_map/ppermute | solution.py:25
  23.7 5.6 %collective-permute-start.6 = (f16[4,64,128]{2,1,0:T(8,128)(2,1)S(1)}, f16[4,64,128]{2,1,0:T(8,128)(2,1)S(1)}, u32[]{:S(2)}, u32[]{:S(2)}) collective-permute-start(f16[4,64,128]{2,1,0:T(8,128)(2,1)S(1)} %get-tuple-element.18), channel_id=1, source_target_pairs={{0,6},{2,4},{4,2},{6,0},{1,7},{3,5},{5,3},{7,1},{8,14},{10,12},{12... | collective-permute-start | bytes 196616 | tf_op jit(solution)/shard_map/ppermute | solution.py:25
  24.3 5.8 %collective-permute-start.7 = (f16[4,64,128]{2,1,0:T(8,128)(2,1)S(1)}, f16[4,64,128]{2,1,0:T(8,128)(2,1)S(1)}, u32[]{:S(2)}, u32[]{:S(2)}) collective-permute-start(f16[4,64,128]{2,1,0:T(8,128)(2,1)S(1)} %get-tuple-element.17), channel_id=1, source_target_pairs={{0,4},{2,6},{4,0},{6,2},{1,5},{3,7},{5,1},{7,3},{8,12},{10,14},{12... | collective-permute-start | bytes 196616 | tf_op jit(solution)/shard_map/ppermute | solution.py:25
  27.9 6.5 %collective-permute-start.17 = (bf16[8,128]{1,0:T(8,128)(2,1)S(1)}, bf16[8,128]{1,0:T(8,128)(2,1)S(1)}, u32[]{:S(2)}, u32[]{:S(2)}) collective-permute-start(bf16[8,128]{1,0:T(8,128)(2,1)S(1)} %get-tuple-element.12), channel_id=1, source_target_pairs={{0,16},{8,24},{16,0},{24,8},{1,17},{9,25},{17,1},{25,9},{2,18},{10... | collective-permute-start | bytes 6152 | tf_op jit(solution)/shard_map/ppermute | solution.py:25
  29.3 5.1 %collective-permute-start.14 = (bf16[512,128]{1,0:T(8,128)(2,1)S(1)}, bf16[512,128]{1,0:T(8,128)(2,1)S(1)}, u32[]{:S(2)}, u32[]{:S(2)}) collective-permute-start(bf16[512,128]{1,0:T(8,128)(2,1)S(1)} %constant_dynamic-update-slice_fusion.own_ref), channel_id=1, source_target_pairs={{0,1},{1,0},{2,3},{3,2},{4,5},{5,4},{6,7},{7,6},{8,9},{9,8},{10,11... | collective-permute-start | bytes 393224 | tf_op jit(solution)/shard_map/ppermute | solution.py:25
  30.2 5.5 %collective-permute-start.10 = (f32[64,128]{1,0:T(8,128)S(1)}, f32[64,128]{1,0:T(8,128)S(1)}, u32[]{:S(2)}, u32[]{:S(2)}) collective-permute-start(f32[64,128]{1,0:T(8,128)S(1)} %get-tuple-element.19), channel_id=1, source_target_pairs={{0,16},{8,24},{16,0},{24,8},{1,17},{9,25},{17,1},{25,9},{2,18},{10... | collective-permute-start | bytes 98312 | tf_op jit(solution)/shard_map/ppermute | solution.py:25
  31.7 4.1 %collective-permute-start.8 = (f32[64,128]{1,0:T(8,128)S(1)}, f32[64,128]{1,0:T(8,128)S(1)}, u32[]{:S(2)}, u32[]{:S(2)}) collective-permute-start(f32[64,128]{1,0:T(8,128)S(1)} %get-tuple-element.21), channel_id=1, source_target_pairs={{0,8},{8,0},{16,24},{24,16},{1,9},{9,1},{17,25},{25,17},{2,10},{10... | collective-permute-start | bytes 98312 | tf_op jit(solution)/shard_map/ppermute | solution.py:25
  33.6 3.9 %collective-permute-start.9 = (f32[64,128]{1,0:T(8,128)S(1)}, f32[64,128]{1,0:T(8,128)S(1)}, u32[]{:S(2)}, u32[]{:S(2)}) collective-permute-start(f32[64,128]{1,0:T(8,128)S(1)} %get-tuple-element.20), channel_id=1, source_target_pairs={{0,24},{8,16},{16,8},{24,0},{1,25},{9,17},{17,9},{25,1},{2,26},{10... | collective-permute-start | bytes 98312 | tf_op jit(solution)/shard_map/ppermute | solution.py:25
  39.0 1.2 %collective-permute-start.18 = (f32[1,128]{1,0:T(1,128)S(1)}, f32[1,128]{1,0:T(1,128)S(1)}, u32[]{:S(2)}, u32[]{:S(2)}) collective-permute-start(f32[1,128]{1,0:T(1,128)S(1)} %get-tuple-element.11), channel_id=1, source_target_pairs={{0,1},{1,0},{2,3},{3,2},{4,5},{5,4},{6,7},{7,6},{8,9},{9,8},{10,11... | collective-permute-start | bytes 1544 | tf_op jit(solution)/shard_map/ppermute | solution.py:25
  66.4 0.6 copy-start.2

commit v2 on v1

v2 whole, which is shorter than its diff:
```python
import jax
import jax.numpy as jnp
from jax import lax
from jax.experimental import pallas as pl
from jax.experimental.pallas import tpu as pltpu
from jax.sharding import Mesh, PartitionSpec as P

f32, bf16, f16 = jnp.float32, jnp.bfloat16, jnp.float16
DOWN_C, DOWN_X, DOWN_Y = 1.0 / 4, 1.0 / 8, 1.0 / 32
NEAR = (2, 1, 3)
CHUNKS = 16
UP_U = 1024.0


def on_vmem(kernel, outs, *args, scratch=()):
    place = pl.BlockSpec(memory_space=pltpu.VMEM)
    return pl.pallas_call(
        kernel,
        out_shape=outs,
        in_specs=[place] * len(args),
        out_specs=jax.tree.map(lambda _: place, outs),
        scratch_shapes=scratch,
        compiler_params=pltpu.CompilerParams(vmem_limit_bytes=32 * 2**20),
    )(*args)


def swap(value, axis, distance):
    count = lax.axis_size(axis)
    return lax.ppermute(value, axis, [(i, i ^ distance) for i in range(count)])


def flatten_kernel(spectrogram_ref, other_ref, mine_ref, done_ref, buffer_ref, sem_ref):
    core = lax.axis_index("c")
    rows = spectrogram_ref.shape[0]
    chunk = other_ref.shape[0] // CHUNKS
    copies = []
    for side in range(2):
        for i in range(CHUNKS):
            offset = pl.multiple_of((2 * i + (core if side else 1 - core)) * chunk, chunk)
            copy = pltpu.make_async_copy(
                spectrogram_ref.at[pl.ds(offset, chunk)], buffer_ref.at[side, i], sem_ref.at[side, i]
            )
            copy.start()
            copies.append((side, i, copy))
    for side, i, copy in copies:
        copy.wait()
        out = mine_ref if side else other_ref
        out[chunk * i : chunk * (i + 1), :] = buffer_ref[side, i].reshape(chunk, out.shape[1])
    done_ref[...] = jnp.zeros_like(done_ref)


def lead_kernel(freq_ref, factor_ref, window_ref, out_ref, freq_out_ref, freq_buffer, factor_buffer, window_buffer, sem_ref):
    copies = [
        pltpu.make_async_copy(freq_ref, freq_buffer, sem_ref.at[0]),
        pltpu.make_async_copy(factor_ref, factor_buffer, sem_ref.at[1]),
        pltpu.make_async_copy(window_ref, window_buffer, sem_ref.at[2]),
    ]
    for copy in copies:
        copy.start()
    for copy in copies:
        copy.wait()
    freqs, rows = freq_ref.shape[0], factor_ref.shape[0]
    freq = freq_buffer[...]
    freq_out_ref[...] = freq
    out_ref[:freqs, :] = freq.astype(f32)
    out_ref[freqs : freqs + rows, :] = factor_buffer[...] * UP_U
    out_ref[freqs + rows :, :] = window_buffer[...].astype(f32)


def differ(part):
    lane = lax.broadcasted_iota(jnp.int32, part.shape, 1)
    return jnp.where(lane == 0, part, part - part[:, :1])


def other_kernel(flat_ref, block_ref, freq_ref, part_ref, khatri_rao_ref):
    freqs = freq_ref.shape[0]
    factor = freq_ref[...].astype(f32)
    for j in range(block_ref.shape[0]):
        khatri_rao_ref[freqs * j : freqs * (j + 1), :] = (block_ref[j : j + 1, :] * factor).astype(bf16)
    part_ref[...] = differ(jnp.dot(flat_ref[...], khatri_rao_ref[...], preferred_element_type=f32))


def mine_kernel(flat_ref, khatri_rao_ref, part_ref):
    part_ref[...] = differ(jnp.dot(flat_ref[...], khatri_rao_ref[...], preferred_element_type=f32))


def gram_of(block):
    return lax.dot_general(block, block, (((0,), (0,)), ((), ())), preferred_element_type=f32)


def gram_kernel(own_ref, far_ref, w0_ref, w1_ref, w2_ref, w3_ref, factor_ref, lower_ref, upper_ref, inverse_ref):
    rank = own_ref.shape[-1]

    def paired(blocks):
        own, two, one, three = (gram_of(v) for v in blocks)
        return (own + two) + (one + three)

    step = own_ref.shape[0] // 4
    freq = [paired([ref[step * i : step * (i + 1), :] for i in range(4)]) for ref in (own_ref, far_ref)]
    gram = (freq[0] + freq[1]) * paired([w[...] for w in (w0_ref, w1_ref, w2_ref, w3_ref)])
    row = lax.broadcasted_iota(jnp.int32, (rank, rank), 0)
    col = lax.broadcasted_iota(jnp.int32, (rank, rank), 1)
    inverse = 1.0 / jnp.sum(jnp.where(row == col, gram, 0.0), axis=1, keepdims=True)
    lower_ref[...] = jnp.where(row > col, gram, 0.0) * inverse
    upper = jnp.where(row < col, gram, 0.0) * inverse
    upper_ref[...] = lax.dot_general(
        upper,
        factor_ref[...],
        (((1,), (1,)), ((), ())),
        precision=lax.Precision.HIGHEST,
        preferred_element_type=f32,
    )
    inverse_ref[...] = jnp.broadcast_to(inverse, inverse_ref.shape)


def sweep_kernel(mttkrp_ref, lower_ref, upper_ref, inverse_ref, out_ref, square_ref):
    coded = mttkrp_ref[...].T * (1.0 / DOWN_Y)
    rank, rows = coded.shape
    row = lax.broadcasted_iota(jnp.int32, (rank, rows), 0)
    mttkrp = jnp.where(row == 0, coded, coded + coded[:1, :])
    start = mttkrp * inverse_ref[...] - upper_ref[...]
    parts = [start[8 * i : 8 * i + 8] for i in range(rank // 8)]
    for j in range(rank):
        block, lane = divmod(j, 8)
        fresh = jnp.maximum(parts[block], 0.0)[lane : lane + 1, :]
        fresh = jnp.broadcast_to(fresh, (8, rows))
        for i in range(block, rank // 8):
            column = jnp.broadcast_to(lower_ref[8 * i : 8 * i + 8, j : j + 1], (8, rows))
            parts[i] = parts[i] - column * fresh
    updated = jnp.maximum(jnp.concatenate(parts, axis=0), 0.0).T
    out_ref[...] = updated
    square_ref[...] = jnp.sum(updated * updated, axis=0, keepdims=True)


def body(spectrogram, window_factor, freq_factor, channel_factor):
    chan_rows, win_rows, freq_rows = spectrogram.shape
    rows, rank = channel_factor.shape
    xs, ys = lax.axis_size("x"), lax.axis_size("y")
    x, y, c = lax.axis_index("x"), lax.axis_index("y"), lax.axis_index("c")
    ux, uy = x.astype(jnp.uint32), y.astype(jnp.uint32)
    xs_near = [ux ^ jnp.uint32(k) for k in NEAR]
    own_slots = [2 * (y ^ k) + c for k in (0,) + NEAR]
    far_slots = [2 * (y ^ k) + 1 - c for k in (0,) + NEAR]
    from_near = [[(y ^ i) == k for k in NEAR] for i in range(ys)]
    uy_rows = uy * jnp.uint32(rows)

    lead = jnp.concatenate([freq_factor.astype(f32), channel_factor * UP_U, window_factor.astype(f32)], axis=0)
    lead = lax.optimization_barrier(lead)
    place = pl.BlockSpec(memory_space=pltpu.VMEM)
    high = lead.astype(f16)
    scaled = lead[freq_rows:-1]
    low = (scaled - scaled.astype(f16).astype(f32)).astype(f16)
    first = jnp.concatenate([high, low], axis=0)
    first, ux, xs_near, own_slots, far_slots, from_near, uy_rows = lax.optimization_barrier(
        (first, ux, xs_near, own_slots, far_slots, from_near, uy_rows)
    )
    first = [first] + [swap(first, "y", k) for k in NEAR]
    last = freq_rows + rows
    line = jnp.concatenate([v[last : last + 1] for v in first], axis=0)
    freqs = jnp.concatenate([v[:freq_rows] for v in first], axis=0).astype(bf16)
    olds = [v[freq_rows:last].astype(f32) + v[last + 1 :].astype(f32) for v in first]
    width = win_rows * freq_rows
    half = jax.ShapeDtypeStruct((chan_rows // 2, width), bf16)
    place = pl.BlockSpec(memory_space=pltpu.VMEM)
    flat_other, flat_mine, done = pl.pallas_call(
        flatten_kernel,
        out_shape=(half, half, jax.ShapeDtypeStruct((8, rank), f32)),
        in_specs=[pl.BlockSpec(memory_space=pl.ANY)],
        out_specs=(place, place, place),
        scratch_shapes=[
            pltpu.VMEM((2, CHUNKS, rows, win_rows, freq_rows), bf16),
            pltpu.SemaphoreType.DMA((2, CHUNKS)),
        ],
        compiler_params=pltpu.CompilerParams(vmem_limit_bytes=48 * 2**20),
        cost_estimate=pl.CostEstimate(flops=0, bytes_accessed=chan_rows * width * 4, transcendentals=0),
    )(spectrogram)
    line, freqs, done = lax.optimization_barrier((line, freqs, done))
    pair = swap(line, "c", 1)
    slot = jnp.arange(win_rows)[:, None]
    block = jnp.zeros((win_rows, rank), f32)
    for i in range(ys):
        block = jnp.where(slot == own_slots[i], line[i : i + 1].astype(f32), block)
        block = jnp.where(slot == far_slots[i], pair[i : i + 1].astype(f32), block)
    half = jax.ShapeDtypeStruct((chan_rows // 2, rank), f32)
    other, khatri_rao = on_vmem(
        other_kernel, (half, jax.ShapeDtypeStruct((width, rank), bf16)), flat_other, block, freq_factor
    )
    mine = on_vmem(mine_kernel, half, flat_mine, khatri_rao)

    far = swap((other * DOWN_C).astype(f16), "c", 1).astype(f32)
    part = (mine + far * (1.0 / DOWN_C)).reshape(xs, ys * rows, rank)
    total = lax.dynamic_index_in_dim(part, ux, 0, keepdims=False)
    small = (part * DOWN_X).astype(f16)
    small, freqs = lax.optimization_barrier((small, freqs))
    far, windows = 0.0, [block.astype(bf16)]
    for k, place_x in zip(NEAR, xs_near):
        piece = lax.dynamic_index_in_dim(small, place_x, 0, keepdims=False)
        piece = swap(jnp.concatenate([piece, block.astype(f16)], axis=0), "x", k)
        far = far + piece[: ys * rows].astype(f32)
        windows.append(piece[ys * rows :].astype(bf16))
    total = total + far * (1.0 / DOWN_X)

    freqs_far = swap(freqs, "c", 1)
    total, freqs_far = lax.optimization_barrier((total, freqs_far))
    ordered = []
    for i in range(ys):
        old = olds[0]
        for v, here in zip(olds[1:], from_near[i]):
            old = jnp.where(here, v, old)
        ordered.append(old)
    like = jax.ShapeDtypeStruct((rank, ys * rows), f32)
    lower, upper, inverse = on_vmem(
        gram_kernel,
        (jax.ShapeDtypeStruct((rank, rank), f32), like, like),
        freqs,
        freqs_far,
        *windows,
        jnp.concatenate(ordered, axis=0) * (1.0 / UP_U),
    )

    small = (total * DOWN_Y).astype(f16)
    p0, p2, p1, p3 = [small] + [swap(small, "y", k) for k in NEAR]
    mttkrp = (p1.astype(f32) + p3.astype(f32)) + (p0.astype(f32) + p2.astype(f32))
    updated, squares = on_vmem(
        sweep_kernel,
        (jax.ShapeDtypeStruct((ys * rows, rank), f32), jax.ShapeDtypeStruct((1, rank), f32)),
        mttkrp,
        lower,
        upper,
        inverse,
    )
    updated = lax.dynamic_slice_in_dim(updated, uy_rows, rows, 0)
    squares = squares + swap(squares, "c", 1)
    lines = xs * lax.axis_size("z")
    updated, squares = lax.optimization_barrier((updated, squares))
    squares = lax.all_to_all(
        jnp.broadcast_to(squares, (lines, rank)), ("z", "x"), 0, 0, tiled=True
    ).sum(axis=0)
    column_scale = jnp.sqrt(squares / (lines * 2 * ys * rows) + 1e-06)
    return (updated / column_scale[None, :], column_scale)


def solution(mesh):
    chan, win, freq = mesh.devices.shape
    fine = Mesh(mesh.devices.reshape(chan, win, freq // 2, 2), ("z", "x", "y", "c"))
    placed = (
        P("z", "x", ("y", "c")),
        P(("x", "y", "c"), None),
        P(("y", "c"), None),
        P(("z", "x", "y", "c"), None),
    )
    return jax.shard_map(
        body,
        mesh=fine,
        in_specs=placed,
        out_specs=(P(("z", "x", "y", "c"), None), P()),
        check_vma=False,
    )
```

time: 67.9 us -> 56.1 us (0.83)
  starting transfers between devices: 21.5 us -> 13.3 us
  blocking collectives: 26.1 us -> 19.7 us
  Pallas kernels: 2.12 us -> 7.06 us
  matrix products: 3.71 us -> 0 us
  waiting for transfers between devices: 9.11 us -> 10.4 us
  other arithmetic: 2.31 us -> 3.57 us
  local copies, waits for them, and re-layouts: 1.38 us -> 0.15 us
    ppermute x19 -> x13, starting transfers between devices: 21.5 us -> 13.3 us  [swap(): return lax.ppermute(value, axis, [(i, i ^ distance) for i in range(count)])]
    all_to_all x1, blocking collectives: 26.1 us -> 19.7 us  [body(): lax.all_to_all(jnp.broadcast_to(squares, (lines, rank)), ('z', 'x'), 0, 0...]
    dot_general x1 -> x0, matrix products: 3.71 us -> none  [body(): part = jnp.dot(flat, khatri_rao, preferred_element_type=f32)]
    pallas_call x0 -> x1, Pallas kernels: none -> 3.23 us  [body(): pl.pallas_call(flatten_kernel, out_shape=(half, half, jax.ShapeDtypeStruc...]
    pallas_call x2 -> x4, Pallas kernels: 2.12 us -> 3.84 us  [on_vmem(): pl.pallas_call(kernel, out_shape=outs, in_specs=[place] * len(args), out_...]
    convert_element_type x2 -> x13, other arithmetic: 0.19 us -> 1.71 us  [the longest x1 0.77 us: body(): freq_factor.astype(f32)]
    ppermute x19 -> x13, waiting for transfers between devices: 9.11 us -> 10.4 us  [swap(): return lax.ppermute(value, axis, [(i, i ^ distance) for i in range(count)])]
    convert_element_type x1 -> x0, local copies, waits for them, and re-layouts: 0.85 us -> none  [body(): product = block[:, None, :] * freq_factor.astype(f32)[None, :, :]]
  transfers between devices with their start and end apart: 19 -> 13, of which waited for: 9 -> 9; matrix products, arithmetic and copies ran while one was open for 3% -> 1% of each run, Pallas kernels for 1% -> 8%
where the time goes in v2:
time: 56.1 us; the launch traced here: 55.1 us
  blocking collectives  19.7 us (35%)
  starting transfers between devices  13.3 us (24%)
  waiting for transfers between devices  10.4 us (19%)
  Pallas kernels  7.06 us (13%)
  other arithmetic  3.57 us (6%)
  between operations  1 us (2%)
    all_to_all x1, blocking collectives, body(): lax.all_to_all(jnp.broadcast_to(squares, (lines, rank)), ('z', 'x'), 0, 0...  19.7 us
    ppermute x13, starting transfers between devices, swap(): return lax.ppermute(value, axis, [(i, i ^ distance) for i in range(count)])  13.3 us
    ppermute x13, waiting for transfers between devices, swap(): return lax.ppermute(value, axis, [(i, i ^ distance) for i in range(count)])  10.4 us
    pallas_call x4, Pallas kernels, on_vmem(): pl.pallas_call(kernel, out_shape=outs, in_specs=[place] * len(args), out_...  3.84 us
    pallas_call x1, Pallas kernels, body(): pl.pallas_call(flatten_kernel, out_shape=(half, half, jax.ShapeDtypeStruc...  3.23 us
  transfers between devices with their start and end apart: 13, of which 9 were waited for; matrix products, arithmetic and copies ran while one was open for 1% of the time, Pallas kernels for 8%

profile of v2, /device:TPU:2, one launch (start us, length us, event | category | flops | bytes accessed | tf_op | source)
XLA Modules:
  0.0 55.1 jit_solution(10096425159554868718)
XLA Ops:
  0.7 0.8 %convert_element_type.109 = f32[128,128]{1,0:T(8,128)S(1)} convert(bf16[128,128]{1,0:T(8,128)(2,1)} %freq_ref.1) | non-fusion elementwise | flops 16384 | bytes 98304 | tf_op jit(solution)/shard_map/convert_element_type | solution.py:147
  1.4 0.8 %broadcast_multiply_fusion = f32[64,128]{1,0:T(8,128)S(1)} fusion(f32[64,128]{1,0:T(8,128)} %param.7), kind=kLoop, calls=%fused_computation.27 | loop fusion | flops 8192 | bytes 65536 | tf_op jit(solution)/shard_map/mul | solution.py:147
  2.2 0.7 %convert_element_type.110 = f32[1,128]{1,0:T(1,128)S(1)} convert(bf16[1,128]{1,0:T(2,128)(2,1)} %param.5) | non-fusion elementwise | flops 128 | bytes 768 | tf_op jit(solution)/shard_map/convert_element_type | solution.py:147
  2.9 3.3 %collective-permute-start = (f16[257,128]{1,0:T(8,128)(2,1)S(1)}, f16[257,128]{1,0:T(8,128)(2,1)S(1)}, u32[]{:S(2)}, u32[]{:S(2)}) collective-permute-start(f16[257,128]{1,0:T(8,128)(2,1)S(1)} %pad_maximum_fusion.4), channel_id=1, source_target_pairs={{0,4},{2,6},{4,0},{6,2},{1,5},{3,7},{5,1},{7,3},{8,12},{10,14},{12... | collective-permute-start | bytes 197384 | tf_op jit(solution)/shard_map/ppermute | solution.py:29
  6.2 0.7 %collective-permute-start.1 = (f16[257,128]{1,0:T(8,128)(2,1)S(1)}, f16[257,128]{1,0:T(8,128)(2,1)S(1)}, u32[]{:S(2)}, u32[]{:S(2)}) collective-permute-start(f16[257,128]{1,0:T(8,128)(2,1)S(1)} %pad_maximum_fusion.4), channel_id=1, source_target_pairs={{0,2},{2,0},{4,6},{6,4},{1,3},{3,1},{5,7},{7,5},{8,10},{10,8},{12,... | collective-permute-start | bytes 197384 | tf_op jit(solution)/shard_map/ppermute | solution.py:29
  6.9 0.4 collective-permute-start.2
  7.3 3.2 %shard_map.59 = (bf16[1024,1024]{1,0:T(8,128)(2,1)S(1)}, bf16[1024,1024]{1,0:T(8,128)(2,1)S(1)}, f32[8,128]{1,0:T(8,128)}) custom-call(bf16[2048,8,128]{2,1,0:T(8,128)(2,1)} %spectrogram_ref.1), custom_call_target="tpu_custom_call" | custom-call | bytes 8388608 | tf_op jit(solution)/shard_map/pallas_call | solution.py:165
  10.7 1.7 %collective-permute-done.2 = f16[257,128]{1,0:T(8,128)(2,1)S(1)} collective-permute-done((f16[257,128]{1,0:T(8,128)(2,1)S(1)}, f16[257,128]{1,0:T(8,128)(2,1)S(1)}, u32[]{:S(2)}, u32[]{:S(2)}) %collective-permute-start.2) | collective-permute-done | bytes 65824 | tf_op jit(solution)/shard_map/ppermute | solution.py:29
  12.5 0.1 collective-permute-start.3
  12.7 1.0 %collective-permute-done.3 = f16[4,128]{1,0:T(4,128)(2,1)S(1)} collective-permute-done((f16[4,128]{1,0:T(4,128)(2,1)S(1)}, f16[4,128]{1,0:T(4,128)(2,1)S(1)}, u32[]{:S(2)}, u32[]{:S(2)}) %collective-permute-start.3) | collective-permute-done | bytes 1056 | tf_op jit(solution)/shard_map/ppermute | solution.py:29
  13.8 0.1 fusion
  13.8 0.8 %shard_map.60 = (f32[1024,128]{1,0:T(8,128)S(1)}, bf16[1024,128]{1,0:T(8,128)(2,1)S(1)}) custom-call(bf16[1024,1024]{1,0:T(8,128)(2,1)S(1)} %get-tuple-element.46.flat_ref, f32[8,128]{1,0:T(8,128)S(1)} %get-tuple-element.89.block_ref, bf16[128,128]{1,0:T(8,128)(2,1)S(1)} %copy-done), custom_call_target="tpu_custom_call" | custom-call | tf_op jit(solution)/shard_map/pallas_call | solution.py:17
  14.7 0.3 collective-permute-start.4
  15.1 0.8 %shard_map.61 = f32[1024,128]{1,0:T(8,128)S(1)} custom-call(bf16[1024,1024]{1,0:T(8,128)(2,1)S(1)} %get-tuple-element.45.flat_ref, bf16[1024,128]{1,0:T(8,128)(2,1)S(1)} %get-tuple-element.57.khatri_rao_ref), custom_call_target="tpu_custom_call" | custom-call | tf_op jit(solution)/shard_map/pallas_call | solution.py:17
  15.9 0.5 collective-permute-done.4
  16.6 1.6 %collective-permute-start.7 = (f16[264,128]{1,0:T(8,128)(2,1)S(1)}, f16[264,128]{1,0:T(8,128)(2,1)S(1)}, u32[]{:S(2)}, u32[]{:S(2)}) collective-permute-start(f16[264,128]{1,0:T(8,128)(2,1)S(1)} %get-tuple-element.95), channel_id=1, source_target_pairs={{0,24},{8,16},{16,8},{24,0},{1,25},{9,17},{17,9},{25,1},{2,26},{10... | collective-permute-start | bytes 202760 | tf_op jit(solution)/shard_map/ppermute | solution.py:29
  18.2 1.2 %collective-permute-start.5 = (f16[264,128]{1,0:T(8,128)(2,1)S(1)}, f16[264,128]{1,0:T(8,128)(2,1)S(1)}, u32[]{:S(2)}, u32[]{:S(2)}) collective-permute-start(f16[264,128]{1,0:T(8,128)(2,1)S(1)} %get-tuple-element.93), channel_id=1, source_target_pairs={{0,16},{8,24},{16,0},{24,8},{1,17},{9,25},{17,1},{25,9},{2,18},{10... | collective-permute-start | bytes 202760 | tf_op jit(solution)/shard_map/ppermute | solution.py:29
  19.4 1.5 %collective-permute-start.6 = (f16[264,128]{1,0:T(8,128)(2,1)S(1)}, f16[264,128]{1,0:T(8,128)(2,1)S(1)}, u32[]{:S(2)}, u32[]{:S(2)}) collective-permute-start(f16[264,128]{1,0:T(8,128)(2,1)S(1)} %get-tuple-element.94), channel_id=1, source_target_pairs={{0,8},{8,0},{16,24},{24,16},{1,9},{9,1},{17,25},{25,17},{2,10},{10... | collective-permute-start | bytes 202760 | tf_op jit(solution)/shard_map/ppermute | solution.py:29
  20.9 0.1 collective-permute-done.7
  21.0 3.7 %collective-permute-done.5 = f16[264,128]{1,0:T(8,128)(2,1)S(1)} collective-permute-done((f16[264,128]{1,0:T(8,128)(2,1)S(1)}, f16[264,128]{1,0:T(8,128)(2,1)S(1)}, u32[]{:S(2)}, u32[]{:S(2)}) %collective-permute-start.5) | collective-permute-done | bytes 67616 | tf_op jit(solution)/shard_map/ppermute | solution.py:29
  24.7 1.2 %collective-permute-start.10 = (f16[256,128]{1,0:T(8,128)(2,1)S(1)}, f16[256,128]{1,0:T(8,128)(2,1)S(1)}, u32[]{:S(2)}, u32[]{:S(2)}) collective-permute-start(f16[256,128]{1,0:T(8,128)(2,1)S(1)} %multiply_convert_fusion.2), channel_id=1, source_target_pairs={{0,6},{2,4},{4,2},{6,0},{1,7},{3,5},{5,3},{7,1},{8,14},{10,12},{12... | collective-permute-start | bytes 196616 | tf_op jit(solution)/shard_map/ppermute | solution.py:29
  26.0 1.1 %collective-permute-start.11 = (f16[256,128]{1,0:T(8,128)(2,1)S(1)}, f16[256,128]{1,0:T(8,128)(2,1)S(1)}, u32[]{:S(2)}, u32[]{:S(2)}) collective-permute-start(f16[256,128]{1,0:T(8,128)(2,1)S(1)} %multiply_convert_fusion.2), channel_id=1, source_target_pairs={{0,4},{2,6},{4,0},{6,2},{1,5},{3,7},{5,1},{7,3},{8,12},{10,14},{12... | collective-permute-start | bytes 196616 | tf_op jit(solution)/shard_map/ppermute | solution.py:29
  27.0 1.9 %collective-permute-start.9 = (f16[256,128]{1,0:T(8,128)(2,1)S(1)}, f16[256,128]{1,0:T(8,128)(2,1)S(1)}, u32[]{:S(2)}, u32[]{:S(2)}) collective-permute-start(f16[256,128]{1,0:T(8,128)(2,1)S(1)} %multiply_convert_fusion.2), channel_id=1, source_target_pairs={{0,2},{2,0},{4,6},{6,4},{1,3},{3,1},{5,7},{7,5},{8,10},{10,8},{12,... | collective-permute-start | bytes 196616 | tf_op jit(solution)/shard_map/ppermute | solution.py:29
  28.9 0.7 %shard_map.62 = (f32[128,128]{1,0:T(8,128)S(1)}, f32[128,256]{1,0:T(8,128)S(1)}, f32[128,256]{1,0:T(8,128)S(1)}) custom-call(bf16[512,128]{1,0:T(8,128)(2,1)S(1)} %maximum_convert_fusion.own_ref, bf16[512,128]{1,0:T(8,128)(2,1)S(1)} %collective-permute-done.8.far_ref, bf16[8,128]{1,0:T(8,128)(2,1)S(1)} %get-tuple-element.88.w0_ref, ...), custom_call_target="tpu_custom_call" | custom-call | tf_op jit(solution)/shard_map/pallas_call | solution.py:17
  29.6 0.9 %collective-permute-done.10 = f16[256,128]{1,0:T(8,128)(2,1)S(1)} collective-permute-done((f16[256,128]{1,0:T(8,128)(2,1)S(1)}, f16[256,128]{1,0:T(8,128)(2,1)S(1)}, u32[]{:S(2)}, u32[]{:S(2)}) %collective-permute-start.10) | collective-permute-done | bytes 65568 | tf_op jit(solution)/shard_map/ppermute | solution.py:29
  30.5 1.2 %collective-permute-done.11 = f16[256,128]{1,0:T(8,128)(2,1)S(1)} collective-permute-done((f16[256,128]{1,0:T(8,128)(2,1)S(1)}, f16[256,128]{1,0:T(8,128)(2,1)S(1)}, u32[]{:S(2)}, u32[]{:S(2)}) %collective-permute-start.11) | collective-permute-done | bytes 65568 | tf_op jit(solution)/shard_map/ppermute | solution.py:29
  31.8 0.1 collective-permute-done.9
  31.9 1.6 %shard_map.63 = (f32[256,128]{1,0:T(8,128)S(1)}, f32[1,128]{1,0:T(1,128)S(1)}) custom-call(f32[256,128]{1,0:T(8,128)S(1)} %add_add_fusion.mttkrp_ref, f32[128,128]{1,0:T(8,128)S(1)} %get-tuple-element.80.lower_ref, f32[128,256]{1,0:T(8,128)S(1)} %get-tuple-element.81.upper_ref, f32[128,256]{1,0:T(8,128)S(1)} %get-tuple-element.82.inverse_ref), custom_call_target="tpu_custom_call" | custom-call | tf_op jit(solution)/shard_map/pallas_call | solution.py:17
  33.5 0.1 collective-permute-start.12
  33.6 1.1 %collective-permute-done.12 = f32[1,128]{1,0:T(1,128)S(1)} collective-permute-done((f32[1,128]{1,0:T(1,128)S(1)}, f32[1,128]{1,0:T(1,128)S(1)}, u32[]{:S(2)}, u32[]{:S(2)}) %collective-permute-start.12) | collective-permute-done | bytes 544 | tf_op jit(solution)/shard_map/ppermute | solution.py:29
  34.7 19.7 %all_to_all.6 = f32[32,1,128]{2,1,0:T(1,128)S(1)} all-to-all(f32[32,1,128]{2,1,0:T(1,128)S(1)} %broadcast_in_dim.169), channel_id=1, replica_groups=mesh['z'=8,'x'=4,'y'=4,'c'=2] {'z','x'}, dimensions={0} | all-to-all | bytes 32768 | tf_op jit(solution)/shard_map/all_to_all | solution.py:236
  54.5 0.6 %broadcast_divide_fusion = f32[64,128]{1,0:T(8,128)} fusion(f32[64,128]{1,0:T(8,128)S(1)} %constant_dynamic-slice_fusion, f32[128]{0:T(128)S(1)} %add_sqrt_fusion), kind=kLoop, calls=%fused_computation.26 | loop fusion | flops 8192 | bytes 66048 | tf_op jit(solution)/shard_map/div | solution.py:240
  (51 shorter events, 0.8 us)
Async XLA Ops:
  2.9 7.7 %collective-permute-start = (f16[257,128]{1,0:T(8,128)(2,1)S(1)}, f16[257,128]{1,0:T(8,128)(2,1)S(1)}, u32[]{:S(2)}, u32[]{:S(2)}) collective-permute-start(f16[257,128]{1,0:T(8,128)(2,1)S(1)} %pad_maximum_fusion.4), channel_id=1, source_target_pairs={{0,4},{2,6},{4,0},{6,2},{1,5},{3,7},{5,1},{7,3},{8,12},{10,14},{12... | collective-permute-start | bytes 197384 | tf_op jit(solution)/shard_map/ppermute | solution.py:29
  6.2 4.4 %collective-permute-start.1 = (f16[257,128]{1,0:T(8,128)(2,1)S(1)}, f16[257,128]{1,0:T(8,128)(2,1)S(1)}, u32[]{:S(2)}, u32[]{:S(2)}) collective-permute-start(f16[257,128]{1,0:T(8,128)(2,1)S(1)} %pad_maximum_fusion.4), channel_id=1, source_target_pairs={{0,2},{2,0},{4,6},{6,4},{1,3},{3,1},{5,7},{7,5},{8,10},{10,8},{12,... | collective-permute-start | bytes 197384 | tf_op jit(solution)/shard_map/ppermute | solution.py:29
  6.9 5.5 %collective-permute-start.2 = (f16[257,128]{1,0:T(8,128)(2,1)S(1)}, f16[257,128]{1,0:T(8,128)(2,1)S(1)}, u32[]{:S(2)}, u32[]{:S(2)}) collective-permute-start(f16[257,128]{1,0:T(8,128)(2,1)S(1)} %pad_maximum_fusion.4), channel_id=1, source_target_pairs={{0,6},{2,4},{4,2},{6,0},{1,7},{3,5},{5,3},{7,1},{8,14},{10,12},{12... | collective-permute-start | bytes 197384 | tf_op jit(solution)/shard_map/ppermute | solution.py:29
  7.3 6.5 %copy-start = (bf16[128,128]{1,0:T(8,128)(2,1)S(1)}, bf16[128,128]{1,0:T(8,128)(2,1)}, u32[]{:S(2)}) copy-start(bf16[128,128]{1,0:T(8,128)(2,1)} %freq_ref.1) | copy-start | bytes 98308
  12.5 1.2 %collective-permute-start.3 = (f16[4,128]{1,0:T(4,128)(2,1)S(1)}, f16[4,128]{1,0:T(4,128)(2,1)S(1)}, u32[]{:S(2)}, u32[]{:S(2)}) collective-permute-start(f16[4,128]{1,0:T(4,128)(2,1)S(1)} %pad_maximum_fusion.5), channel_id=1, source_target_pairs={{0,1},{1,0},{2,3},{3,2},{4,5},{5,4},{6,7},{7,6},{8,9},{9,8},{10,11... | collective-permute-start | bytes 3080 | tf_op jit(solution)/shard_map/ppermute | solution.py:29
  14.7 1.6 %collective-permute-start.4 = (f16[1024,128]{1,0:T(8,128)(2,1)S(1)}, f16[1024,128]{1,0:T(8,128)(2,1)S(1)}, u32[]{:S(2)}, u32[]{:S(2)}) collective-permute-start(f16[1024,128]{1,0:T(8,128)(2,1)S(1)} %multiply_convert_fusion.1), channel_id=1, source_target_pairs={{0,1},{1,0},{2,3},{3,2},{4,5},{5,4},{6,7},{7,6},{8,9},{9,8},{10,11... | collective-permute-start | bytes 786440 | tf_op jit(solution)/shard_map/ppermute | solution.py:29
  16.6 4.4 %collective-permute-start.7 = (f16[264,128]{1,0:T(8,128)(2,1)S(1)}, f16[264,128]{1,0:T(8,128)(2,1)S(1)}, u32[]{:S(2)}, u32[]{:S(2)}) collective-permute-start(f16[264,128]{1,0:T(8,128)(2,1)S(1)} %get-tuple-element.95), channel_id=1, source_target_pairs={{0,24},{8,16},{16,8},{24,0},{1,25},{9,17},{17,9},{25,1},{2,26},{10... | collective-permute-start | bytes 202760 | tf_op jit(solution)/shard_map/ppermute | solution.py:29
  18.2 6.5 %collective-permute-start.5 = (f16[264,128]{1,0:T(8,128)(2,1)S(1)}, f16[264,128]{1,0:T(8,128)(2,1)S(1)}, u32[]{:S(2)}, u32[]{:S(2)}) collective-permute-start(f16[264,128]{1,0:T(8,128)(2,1)S(1)} %get-tuple-element.93), channel_id=1, source_target_pairs={{0,16},{8,24},{16,0},{24,8},{1,17},{9,25},{17,1},{25,9},{2,18},{10... | collective-permute-start | bytes 202760 | tf_op jit(solution)/shard_map/ppermute | solution.py:29
  19.4 5.3 %collective-permute-start.6 = (f16[264,128]{1,0:T(8,128)(2,1)S(1)}, f16[264,128]{1,0:T(8,128)(2,1)S(1)}, u32[]{:S(2)}, u32[]{:S(2)}) collective-permute-start(f16[264,128]{1,0:T(8,128)(2,1)S(1)} %get-tuple-element.94), channel_id=1, source_target_pairs={{0,8},{8,0},{16,24},{24,16},{1,9},{9,1},{17,25},{25,17},{2,10},{10... | collective-permute-start | bytes 202760 | tf_op jit(solution)/shard_map/ppermute | solution.py:29
  20.9 3.8 %collective-permute-start.8 = (bf16[512,128]{1,0:T(8,128)(2,1)S(1)}, bf16[512,128]{1,0:T(8,128)(2,1)S(1)}, u32[]{:S(2)}, u32[]{:S(2)}) collective-permute-start(bf16[512,128]{1,0:T(8,128)(2,1)S(1)} %maximum_convert_fusion.own_ref), channel_id=1, source_target_pairs={{0,1},{1,0},{2,3},{3,2},{4,5},{5,4},{6,7},{7,6},{8,9},{9,8},{10,11... | collective-permute-start | bytes 393224 | tf_op jit(solution)/shard_map/ppermute | solution.py:29
  24.7 5.8 %collective-permute-start.10 = (f16[256,128]{1,0:T(8,128)(2,1)S(1)}, f16[256,128]{1,0:T(8,128)(2,1)S(1)}, u32[]{:S(2)}, u32[]{:S(2)}) collective-permute-start(f16[256,128]{1,0:T(8,128)(2,1)S(1)} %multiply_convert_fusion.2), channel_id=1, source_target_pairs={{0,6},{2,4},{4,2},{6,0},{1,7},{3,5},{5,3},{7,1},{8,14},{10,12},{12... | collective-permute-start | bytes 196616 | tf_op jit(solution)/shard_map/ppermute | solution.py:29
  26.0 5.8 %collective-permute-start.11 = (f16[256,128]{1,0:T(8,128)(2,1)S(1)}, f16[256,128]{1,0:T(8,128)(2,1)S(1)}, u32[]{:S(2)}, u32[]{:S(2)}) collective-permute-start(f16[256,128]{1,0:T(8,128)(2,1)S(1)} %multiply_convert_fusion.2), channel_id=1, source_target_pairs={{0,4},{2,6},{4,0},{6,2},{1,5},{3,7},{5,1},{7,3},{8,12},{10,14},{12... | collective-permute-start | bytes 196616 | tf_op jit(solution)/shard_map/ppermute | solution.py:29
  27.0 4.8 %collective-permute-start.9 = (f16[256,128]{1,0:T(8,128)(2,1)S(1)}, f16[256,128]{1,0:T(8,128)(2,1)S(1)}, u32[]{:S(2)}, u32[]{:S(2)}) collective-permute-start(f16[256,128]{1,0:T(8,128)(2,1)S(1)} %multiply_convert_fusion.2), channel_id=1, source_target_pairs={{0,2},{2,0},{4,6},{6,4},{1,3},{3,1},{5,7},{7,5},{8,10},{10,8},{12,... | collective-permute-start | bytes 196616 | tf_op jit(solution)/shard_map/ppermute | solution.py:29
  33.5 1.2 %collective-permute-start.12 = (f32[1,128]{1,0:T(1,128)S(1)}, f32[1,128]{1,0:T(1,128)S(1)}, u32[]{:S(2)}, u32[]{:S(2)}) collective-permute-start(f32[1,128]{1,0:T(1,128)S(1)} %get-tuple-element.85), channel_id=1, source_target_pairs={{0,1},{1,0},{2,3},{3,2},{4,5},{5,4},{6,7},{7,6},{8,9},{9,8},{10,11... | collective-permute-start | bytes 1544 | tf_op jit(solution)/shard_map/ppermute | solution.py:29
  54.5 0.6 %copy-start.1 = (f32[128]{0:T(128)}, f32[128]{0:T(128)S(1)}, u32[]{:S(2)}) copy-start(f32[128]{0:T(128)S(1)} %add_sqrt_fusion) | copy-start | bytes 1540

commit v3 on v2

--- a/solution.py
+++ b/solution.py
@@ -8,8 +8,8 @@
 f32, bf16, f16 = jnp.float32, jnp.bfloat16, jnp.float16
 DOWN_C, DOWN_X, DOWN_Y = 1.0 / 4, 1.0 / 8, 1.0 / 32
 NEAR = (2, 1, 3)
+LEAD = (1, 3, 2)
 CHUNKS = 16
-UP_U = 1024.0
 
 
 def on_vmem(kernel, outs, *args, scratch=()):
@@ -29,7 +29,7 @@
     return lax.ppermute(value, axis, [(i, i ^ distance) for i in range(count)])
 
 
-def flatten_kernel(spectrogram_ref, other_ref, mine_ref, done_ref, buffer_ref, sem_ref):
+def flatten_kernel(spectrogram_ref, other_ref, mine_ref, buffer_ref, sem_ref):
     core = lax.axis_index("c")
     rows = spectrogram_ref.shape[0]
     chunk = other_ref.shape[0] // CHUNKS
@@ -46,25 +46,6 @@
         copy.wait()
         out = mine_ref if side else other_ref
         out[chunk * i : chunk * (i + 1), :] = buffer_ref[side, i].reshape(chunk, out.shape[1])
-    done_ref[...] = jnp.zeros_like(done_ref)
-
-
-def lead_kernel(freq_ref, factor_ref, window_ref, out_ref, freq_out_ref, freq_buffer, factor_buffer, window_buffer, sem_ref):
-    copies = [
-        pltpu.make_async_copy(freq_ref, freq_buffer, sem_ref.at[0]),
-        pltpu.make_async_copy(factor_ref, factor_buffer, sem_ref.at[1]),
-        pltpu.make_async_copy(window_ref, window_buffer, sem_ref.at[2]),
-    ]
-    for copy in copies:
-        copy.start()
-    for copy in copies:
-        copy.wait()
-    freqs, rows = freq_ref.shape[0], factor_ref.shape[0]
-    freq = freq_buffer[...]
-    freq_out_ref[...] = freq
-    out_ref[:freqs, :] = freq.astype(f32)
-    out_ref[freqs : freqs + rows, :] = factor_buffer[...] * UP_U
-    out_ref[freqs + rows :, :] = window_buffer[...].astype(f32)
 
 
 def differ(part):
@@ -88,16 +69,15 @@
     return lax.dot_general(block, block, (((0,), (0,)), ((), ())), preferred_element_type=f32)
 
 
-def gram_kernel(own_ref, far_ref, w0_ref, w1_ref, w2_ref, w3_ref, factor_ref, lower_ref, upper_ref, inverse_ref):
+def gram_kernel(own_ref, far_ref, w0_ref, w2_ref, w1_ref, w3_ref, factor_ref, lower_ref, upper_ref, inverse_ref):
     rank = own_ref.shape[-1]
 
-    def paired(blocks):
-        own, two, one, three = (gram_of(v) for v in blocks)
-        return (own + two) + (one + three)
+    def paired(own, one, three, two):
+        return (gram_of(own) + gram_of(two)) + (gram_of(one) + gram_of(three))
 
     step = own_ref.shape[0] // 4
-    freq = [paired([ref[step * i : step * (i + 1), :] for i in range(4)]) for ref in (own_ref, far_ref)]
-    gram = (freq[0] + freq[1]) * paired([w[...] for w in (w0_ref, w1_ref, w2_ref, w3_ref)])
+    freq = [paired(*[ref[step * i : step * (i + 1), :] for i in range(4)]) for ref in (own_ref, far_ref)]
+    gram = (freq[0] + freq[1]) * paired(w0_ref[...], w1_ref[...], w3_ref[...], w2_ref[...])
     row = lax.broadcasted_iota(jnp.int32, (rank, rank), 0)
     col = lax.broadcasted_iota(jnp.int32, (rank, rank), 1)
     inverse = 1.0 / jnp.sum(jnp.where(row == col, gram, 0.0), axis=1, keepdims=True)
@@ -139,34 +119,31 @@
     x, y, c = lax.axis_index("x"), lax.axis_index("y"), lax.axis_index("c")
     ux, uy = x.astype(jnp.uint32), y.astype(jnp.uint32)
     xs_near = [ux ^ jnp.uint32(k) for k in NEAR]
-    own_slots = [2 * (y ^ k) + c for k in (0,) + NEAR]
-    far_slots = [2 * (y ^ k) + 1 - c for k in (0,) + NEAR]
-    from_near = [[(y ^ i) == k for k in NEAR] for i in range(ys)]
+    own_slots = [2 * (y ^ k) + c for k in (0,) + LEAD]
+    far_slots = [2 * (y ^ k) + 1 - c for k in (0,) + LEAD]
+    from_near = [[(y ^ i) == k for k in LEAD] for i in range(ys)]
     uy_rows = uy * jnp.uint32(rows)
 
-    lead = jnp.concatenate([freq_factor.astype(f32), channel_factor * UP_U, window_factor.astype(f32)], axis=0)
-    lead = lax.optimization_barrier(lead)
     place = pl.BlockSpec(memory_space=pltpu.VMEM)
-    high = lead.astype(f16)
-    scaled = lead[freq_rows:-1]
-    low = (scaled - scaled.astype(f16).astype(f32)).astype(f16)
-    first = jnp.concatenate([high, low], axis=0)
+    high = channel_factor.astype(bf16)
+    low = (channel_factor - high.astype(f32)).astype(bf16)
+    first = jnp.concatenate([freq_factor, high, window_factor, low], axis=0)
     first, ux, xs_near, own_slots, far_slots, from_near, uy_rows = lax.optimization_barrier(
         (first, ux, xs_near, own_slots, far_slots, from_near, uy_rows)
     )
-    first = [first] + [swap(first, "y", k) for k in NEAR]
+    first = [first] + [swap(first, "y", k) for k in LEAD]
     last = freq_rows + rows
     line = jnp.concatenate([v[last : last + 1] for v in first], axis=0)
-    freqs = jnp.concatenate([v[:freq_rows] for v in first], axis=0).astype(bf16)
+    freqs = jnp.concatenate([v[:freq_rows] for v in first], axis=0)
     olds = [v[freq_rows:last].astype(f32) + v[last + 1 :].astype(f32) for v in first]
     width = win_rows * freq_rows
     half = jax.ShapeDtypeStruct((chan_rows // 2, width), bf16)
     place = pl.BlockSpec(memory_space=pltpu.VMEM)
-    flat_other, flat_mine, done = pl.pallas_call(
+    flat_other, flat_mine = pl.pallas_call(
         flatten_kernel,
-        out_shape=(half, half, jax.ShapeDtypeStruct((8, rank), f32)),
+        out_shape=(half, half),
         in_specs=[pl.BlockSpec(memory_space=pl.ANY)],
-        out_specs=(place, place, place),
+        out_specs=(place, place),
         scratch_shapes=[
             pltpu.VMEM((2, CHUNKS, rows, win_rows, freq_rows), bf16),
             pltpu.SemaphoreType.DMA((2, CHUNKS)),
@@ -174,7 +151,7 @@
         compiler_params=pltpu.CompilerParams(vmem_limit_bytes=48 * 2**20),
         cost_estimate=pl.CostEstimate(flops=0, bytes_accessed=chan_rows * width * 4, transcendentals=0),
     )(spectrogram)
-    line, freqs, done = lax.optimization_barrier((line, freqs, done))
+    line, freqs, flat_other, flat_mine = lax.optimization_barrier((line, freqs, flat_other, flat_mine))
     pair = swap(line, "c", 1)
     slot = jnp.arange(win_rows)[:, None]
     block = jnp.zeros((win_rows, rank), f32)
@@ -192,12 +169,14 @@
     total = lax.dynamic_index_in_dim(part, ux, 0, keepdims=False)
     small = (part * DOWN_X).astype(f16)
     small, freqs = lax.optimization_barrier((small, freqs))
-    far, windows = 0.0, [block.astype(bf16)]
-    for k, place_x in zip(NEAR, xs_near):
-        piece = lax.dynamic_index_in_dim(small, place_x, 0, keepdims=False)
-        piece = swap(jnp.concatenate([piece, block.astype(f16)], axis=0), "x", k)
-        far = far + piece[: ys * rows].astype(f32)
-        windows.append(piece[ys * rows :].astype(bf16))
+    pieces = [
+        jnp.concatenate([lax.dynamic_index_in_dim(small, i, 0, keepdims=False), block.astype(f16)], axis=0)
+        for i in xs_near
+    ]
+    pieces = [swap(v, "x", k) for v, k in zip(pieces, NEAR)]
+    windows = [block.astype(bf16)] + [v[ys * rows :].astype(bf16) for v in pieces]
+    two, one, three = (v[: ys * rows].astype(f32) for v in pieces)
+    far = two + (one + three)
     total = total + far * (1.0 / DOWN_X)
 
     freqs_far = swap(freqs, "c", 1)
@@ -215,12 +194,12 @@
         freqs,
         freqs_far,
         *windows,
-        jnp.concatenate(ordered, axis=0) * (1.0 / UP_U),
+        jnp.concatenate(ordered, axis=0),
     )
 
     small = (total * DOWN_Y).astype(f16)
-    p0, p2, p1, p3 = [small] + [swap(small, "y", k) for k in NEAR]
-    mttkrp = (p1.astype(f32) + p3.astype(f32)) + (p0.astype(f32) + p2.astype(f32))
+    two, one, three = (v.astype(f32) for v in [swap(small, "y", k) for k in NEAR])
+    mttkrp = (one + three) + (small.astype(f32) + two)
     updated, squares = on_vmem(
         sweep_kernel,
         (jax.ShapeDtypeStruct((ys * rows, rank), f32), jax.ShapeDtypeStruct((1, rank), f32)),
@@ -233,8 +212,9 @@
     squares = squares + swap(squares, "c", 1)
     lines = xs * lax.axis_size("z")
     updated, squares = lax.optimization_barrier((updated, squares))
+    order = [[(i + lines * 11 // 16) % lines for i in range(lines)]]
     squares = lax.all_to_all(
-        jnp.broadcast_to(squares, (lines, rank)), ("z", "x"), 0, 0, tiled=True
+        jnp.broadcast_to(squares, (lines, rank)), ("z", "x"), 0, 0, tiled=True, axis_index_groups=order
     ).sum(axis=0)
     column_scale = jnp.sqrt(squares / (lines * 2 * ys * rows) + 1e-06)
     return (updated / column_scale[None, :], column_scale)

time: 56.1 us -> 51.1 us (0.911); the launches traced: 55.1 us -> 50.8 us
  blocking collectives: 19.7 us -> 16.3 us
  waiting for transfers between devices: 10.4 us -> 11.3 us
  starting transfers between devices: 13.3 us -> 12.6 us
  other arithmetic: 3.57 us -> 2.92 us
    all_to_all x1, blocking collectives: 19.7 us -> 16.3 us  [body(): lax.all_to_all(jnp.broadcast_to(squares, (lines, rank)), ('z', 'x'), 0, 0...]
    ppermute x13, waiting for transfers between devices: 10.4 us -> 11.3 us  [swap(): return lax.ppermute(value, axis, [(i, i ^ distance) for i in range(count)])]
    mul x2 -> x0, other arithmetic: 0.77 us -> none  [the longest x1 0.76 us: body(): channel_factor * UP_U]
    concatenate x3 -> x4, other arithmetic: 0.1 us -> 0.86 us  [the longest x1 0.78 us: body(): first = jnp.concatenate([freq_factor, high, window_factor, low], axis=0)]
    convert_element_type x10 -> x6, other arithmetic: 1.58 us -> 0.94 us  [the longest x1 0.84 us: body(): low = (channel_factor - high.astype(f32)).astype(bf16)]
    ppermute x13, starting transfers between devices: 13.3 us -> 12.6 us  [swap(): return lax.ppermute(value, axis, [(i, i ^ distance) for i in range(count)])]
where the time goes in v3:
time: 51.1 us; the launch traced here: 50.8 us
  blocking collectives  16.3 us (32%)
  starting transfers between devices  12.6 us (25%)
  waiting for transfers between devices  11.3 us (22%)
  Pallas kernels  6.52 us (13%)
  other arithmetic  2.92 us (6%)
  between operations  0.95 us (2%)
    all_to_all x1, blocking collectives, body(): lax.all_to_all(jnp.broadcast_to(squares, (lines, rank)), ('z', 'x'), 0, 0...  16.3 us
    ppermute x13, starting transfers between devices, swap(): return lax.ppermute(value, axis, [(i, i ^ distance) for i in range(count)])  12.6 us
    ppermute x13, waiting for transfers between devices, swap(): return lax.ppermute(value, axis, [(i, i ^ distance) for i in range(count)])  11.3 us
    pallas_call x4, Pallas kernels, on_vmem(): pl.pallas_call(kernel, out_shape=outs, in_specs=[place] * len(args), out_...  3.84 us
    pallas_call x1, Pallas kernels, body(): pl.pallas_call(flatten_kernel, out_shape=(half, half), in_specs=[pl.Block...  2.68 us
  transfers between devices with their start and end apart: 13, of which 9 were waited for; matrix products, arithmetic and copies ran while one was open for 1% of the time, Pallas kernels for 8%

profile of v3, /device:TPU:2, one launch (start us, length us, event | category | flops | bytes accessed | tf_op | source)
XLA Modules:
  0.0 50.8 jit_solution(4519914989201290933)
XLA Ops:
  0.7 0.8 %subtract_convert_fusion = (bf16[64,128]{1,0:T(8,128)(2,1)S(1)}, bf16[64,128]{1,0:T(8,128)(2,1)S(1)}) fusion(f32[64,128]{1,0:T(8,128)} %param.7), kind=kLoop, calls=%fused_computation.23 | loop fusion | flops 32768 | bytes 65536 | tf_op jit(solution)/shard_map/convert_element_type | solution.py:129
  1.5 0.8 %pad_maximum_fusion.5 = bf16[257,128]{1,0:T(8,128)(2,1)S(1)} fusion(bf16[64,128]{1,0:T(8,128)(2,1)S(1)} %get-tuple-element.94, bf16[1,128]{1,0:T(2,128)(2,1)} %param.5, bf16[64,128]{1,0:T(8,128)(2,1)S(1)} %get-tuple-element.95, bf16[128,128]{1,0:T(8,128)(2,1)} %freq_ref.1), kind=kLoop, calls=%fused_computation.11 | loop fusion | flops 263168 | bytes 131584 | tf_op jit(solution)/shard_map/concatenate | solution.py:130
  2.3 3.3 %collective-permute-start.2 = (bf16[257,128]{1,0:T(8,128)(2,1)S(1)}, bf16[257,128]{1,0:T(8,128)(2,1)S(1)}, u32[]{:S(2)}, u32[]{:S(2)}) collective-permute-start(bf16[257,128]{1,0:T(8,128)(2,1)S(1)} %pad_maximum_fusion.5), channel_id=1, source_target_pairs={{0,4},{2,6},{4,0},{6,2},{1,5},{3,7},{5,1},{7,3},{8,12},{10,14},{12... | collective-permute-start | bytes 197384 | tf_op jit(solution)/shard_map/ppermute | solution.py:29
  5.6 1.1 %collective-permute-start.1 = (bf16[257,128]{1,0:T(8,128)(2,1)S(1)}, bf16[257,128]{1,0:T(8,128)(2,1)S(1)}, u32[]{:S(2)}, u32[]{:S(2)}) collective-permute-start(bf16[257,128]{1,0:T(8,128)(2,1)S(1)} %pad_maximum_fusion.5), channel_id=1, source_target_pairs={{0,6},{2,4},{4,2},{6,0},{1,7},{3,5},{5,3},{7,1},{8,14},{10,12},{12... | collective-permute-start | bytes 197384 | tf_op jit(solution)/shard_map/ppermute | solution.py:29
  6.7 2.7 %shard_map.59 = (bf16[1024,1024]{1,0:T(8,128)(2,1)S(1)}, bf16[1024,1024]{1,0:T(8,128)(2,1)S(1)}) custom-call(bf16[2048,8,128]{2,1,0:T(8,128)(2,1)} %spectrogram_ref.1), custom_call_target="tpu_custom_call" | custom-call | bytes 8388608 | tf_op jit(solution)/shard_map/pallas_call | solution.py:142
  9.4 1.6 %collective-permute-done.1 = bf16[257,128]{1,0:T(8,128)(2,1)S(1)} collective-permute-done((bf16[257,128]{1,0:T(8,128)(2,1)S(1)}, bf16[257,128]{1,0:T(8,128)(2,1)S(1)}, u32[]{:S(2)}, u32[]{:S(2)}) %collective-permute-start.1) | collective-permute-done | bytes 65824 | tf_op jit(solution)/shard_map/ppermute | solution.py:29
  11.2 0.1 collective-permute-start.3
  11.4 1.0 %collective-permute-done.3 = bf16[4,128]{1,0:T(4,128)(2,1)S(1)} collective-permute-done((bf16[4,128]{1,0:T(4,128)(2,1)S(1)}, bf16[4,128]{1,0:T(4,128)(2,1)S(1)}, u32[]{:S(2)}, u32[]{:S(2)}) %collective-permute-start.3) | collective-permute-done | bytes 1056 | tf_op jit(solution)/shard_map/ppermute | solution.py:29
  12.4 0.1 fusion
  12.5 0.8 %shard_map.60 = (f32[1024,128]{1,0:T(8,128)S(1)}, bf16[1024,128]{1,0:T(8,128)(2,1)S(1)}) custom-call(bf16[1024,1024]{1,0:T(8,128)(2,1)S(1)} %get-tuple-element.51.flat_ref, f32[8,128]{1,0:T(8,128)S(1)} %get-tuple-element.93.block_ref, bf16[128,128]{1,0:T(8,128)(2,1)S(1)} %copy-done), custom_call_target="tpu_custom_call" | custom-call | tf_op jit(solution)/shard_map/pallas_call | solution.py:17
  13.4 0.3 collective-permute-start.4
  13.7 0.8 %shard_map.61 = f32[1024,128]{1,0:T(8,128)S(1)} custom-call(bf16[1024,1024]{1,0:T(8,128)(2,1)S(1)} %get-tuple-element.50.flat_ref, bf16[1024,128]{1,0:T(8,128)(2,1)S(1)} %get-tuple-element.61.khatri_rao_ref), custom_call_target="tpu_custom_call" | custom-call | tf_op jit(solution)/shard_map/pallas_call | solution.py:17
  14.5 0.5 collective-permute-done.4
  15.0 0.1 multiply_add_fusion
  15.2 0.1 pad_maximum_fusion.4
  15.2 2.2 %collective-permute-start.5 = (f16[264,128]{1,0:T(8,128)(2,1)S(1)}, f16[264,128]{1,0:T(8,128)(2,1)S(1)}, u32[]{:S(2)}, u32[]{:S(2)}) collective-permute-start(f16[264,128]{1,0:T(8,128)(2,1)S(1)} %get-tuple-element.99), channel_id=1, source_target_pairs={{0,16},{8,24},{16,0},{24,8},{1,17},{9,25},{17,1},{25,9},{2,18},{10... | collective-permute-start | bytes 202760 | tf_op jit(solution)/shard_map/ppermute | solution.py:29
  17.5 1.5 %collective-permute-start.6 = (f16[264,128]{1,0:T(8,128)(2,1)S(1)}, f16[264,128]{1,0:T(8,128)(2,1)S(1)}, u32[]{:S(2)}, u32[]{:S(2)}) collective-permute-start(f16[264,128]{1,0:T(8,128)(2,1)S(1)} %get-tuple-element.100), channel_id=1, source_target_pairs={{0,8},{8,0},{16,24},{24,16},{1,9},{9,1},{17,25},{25,17},{2,10},{10... | collective-permute-start | bytes 202760 | tf_op jit(solution)/shard_map/ppermute | solution.py:29
  19.0 0.5 %collective-permute-start.7 = (f16[264,128]{1,0:T(8,128)(2,1)S(1)}, f16[264,128]{1,0:T(8,128)(2,1)S(1)}, u32[]{:S(2)}, u32[]{:S(2)}) collective-permute-start(f16[264,128]{1,0:T(8,128)(2,1)S(1)} %get-tuple-element.101), channel_id=1, source_target_pairs={{0,24},{8,16},{16,8},{24,0},{1,25},{9,17},{17,9},{25,1},{2,26},{10... | collective-permute-start | bytes 202760 | tf_op jit(solution)/shard_map/ppermute | solution.py:29
  19.5 2.4 %collective-permute-done.5 = f16[264,128]{1,0:T(8,128)(2,1)S(1)} collective-permute-done((f16[264,128]{1,0:T(8,128)(2,1)S(1)}, f16[264,128]{1,0:T(8,128)(2,1)S(1)}, u32[]{:S(2)}, u32[]{:S(2)}) %collective-permute-start.5) | collective-permute-done | bytes 67616 | tf_op jit(solution)/shard_map/ppermute | solution.py:29
  21.9 0.6 %collective-permute-done.6 = f16[264,128]{1,0:T(8,128)(2,1)S(1)} collective-permute-done((f16[264,128]{1,0:T(8,128)(2,1)S(1)}, f16[264,128]{1,0:T(8,128)(2,1)S(1)}, u32[]{:S(2)}, u32[]{:S(2)}) %collective-permute-start.6) | collective-permute-done | bytes 67616 | tf_op jit(solution)/shard_map/ppermute | solution.py:29
  22.5 0.7 %collective-permute-done.7 = f16[264,128]{1,0:T(8,128)(2,1)S(1)} collective-permute-done((f16[264,128]{1,0:T(8,128)(2,1)S(1)}, f16[264,128]{1,0:T(8,128)(2,1)S(1)}, u32[]{:S(2)}, u32[]{:S(2)}) %collective-permute-start.7) | collective-permute-done | bytes 67616 | tf_op jit(solution)/shard_map/ppermute | solution.py:29
  23.4 2.1 %collective-permute-start.11 = (f16[256,128]{1,0:T(8,128)(2,1)S(1)}, f16[256,128]{1,0:T(8,128)(2,1)S(1)}, u32[]{:S(2)}, u32[]{:S(2)}) collective-permute-start(f16[256,128]{1,0:T(8,128)(2,1)S(1)} %multiply_convert_fusion.2), channel_id=1, source_target_pairs={{0,4},{2,6},{4,0},{6,2},{1,5},{3,7},{5,1},{7,3},{8,12},{10,14},{12... | collective-permute-start | bytes 196616 | tf_op jit(solution)/shard_map/ppermute | solution.py:29
  25.5 1.1 %collective-permute-start.10 = (f16[256,128]{1,0:T(8,128)(2,1)S(1)}, f16[256,128]{1,0:T(8,128)(2,1)S(1)}, u32[]{:S(2)}, u32[]{:S(2)}) collective-permute-start(f16[256,128]{1,0:T(8,128)(2,1)S(1)} %multiply_convert_fusion.2), channel_id=1, source_target_pairs={{0,6},{2,4},{4,2},{6,0},{1,7},{3,5},{5,3},{7,1},{8,14},{10,12},{12... | collective-permute-start | bytes 196616 | tf_op jit(solution)/shard_map/ppermute | solution.py:29
  26.5 0.4 collective-permute-start.9
  26.9 0.7 %shard_map.62 = (f32[128,128]{1,0:T(8,128)S(1)}, f32[128,256]{1,0:T(8,128)S(1)}, f32[128,256]{1,0:T(8,128)S(1)}) custom-call(bf16[512,128]{1,0:T(8,128)(2,1)S(1)} %pad_maximum_fusion.own_ref, bf16[512,128]{1,0:T(8,128)(2,1)S(1)} %collective-permute-done.8.far_ref, bf16[8,128]{1,0:T(8,128)(2,1)S(1)} %get-tuple-element.92.w0_ref, ...), custom_call_target="tpu_custom_call" | custom-call | tf_op jit(solution)/shard_map/pallas_call | solution.py:17
  27.6 1.7 %collective-permute-done.11 = f16[256,128]{1,0:T(8,128)(2,1)S(1)} collective-permute-done((f16[256,128]{1,0:T(8,128)(2,1)S(1)}, f16[256,128]{1,0:T(8,128)(2,1)S(1)}, u32[]{:S(2)}, u32[]{:S(2)}) %collective-permute-start.11) | collective-permute-done | bytes 65568 | tf_op jit(solution)/shard_map/ppermute | solution.py:29
  29.3 1.6 %collective-permute-done.10 = f16[256,128]{1,0:T(8,128)(2,1)S(1)} collective-permute-done((f16[256,128]{1,0:T(8,128)(2,1)S(1)}, f16[256,128]{1,0:T(8,128)(2,1)S(1)}, u32[]{:S(2)}, u32[]{:S(2)}) %collective-permute-start.10) | collective-permute-done | bytes 65568 | tf_op jit(solution)/shard_map/ppermute | solution.py:29
  31.0 1.6 %shard_map.63 = (f32[256,128]{1,0:T(8,128)S(1)}, f32[1,128]{1,0:T(1,128)S(1)}) custom-call(f32[256,128]{1,0:T(8,128)S(1)} %add_add_fusion.mttkrp_ref, f32[128,128]{1,0:T(8,128)S(1)} %get-tuple-element.84.lower_ref, f32[128,256]{1,0:T(8,128)S(1)} %get-tuple-element.85.upper_ref, f32[128,256]{1,0:T(8,128)S(1)} %get-tuple-element.86.inverse_ref), custom_call_target="tpu_custom_call" | custom-call | tf_op jit(solution)/shard_map/pallas_call | solution.py:17
  32.6 0.1 collective-permute-start.12
  32.7 1.1 %collective-permute-done.12 = f32[1,128]{1,0:T(1,128)S(1)} collective-permute-done((f32[1,128]{1,0:T(1,128)S(1)}, f32[1,128]{1,0:T(1,128)S(1)}, u32[]{:S(2)}, u32[]{:S(2)}) %collective-permute-start.12) | collective-permute-done | bytes 544 | tf_op jit(solution)/shard_map/ppermute | solution.py:29
  33.8 16.3 %all_to_all.6 = f32[32,1,128]{2,1,0:T(1,128)S(1)} all-to-all(f32[32,1,128]{2,1,0:T(1,128)S(1)} %broadcast_in_dim.169), channel_id=1, replica_groups={{176,184,192,200,208,216,224,232,240,248,0,8,16,24,32,40,48,56,64,72,80..., dimensions={0} | all-to-all | bytes 32768 | tf_op jit(solution)/shard_map/all_to_all | solution.py:216
  50.2 0.6 %broadcast_divide_fusion = f32[64,128]{1,0:T(8,128)} fusion(f32[64,128]{1,0:T(8,128)S(1)} %constant_dynamic-slice_fusion, f32[128]{0:T(128)S(1)} %add_sqrt_fusion), kind=kLoop, calls=%fused_computation.24 | loop fusion | flops 8192 | bytes 66048 | tf_op jit(solution)/shard_map/div | solution.py:220
  (46 shorter events, 0.6 us)
Async XLA Ops:
  2.3 7.1 %collective-permute-start.2 = (bf16[257,128]{1,0:T(8,128)(2,1)S(1)}, bf16[257,128]{1,0:T(8,128)(2,1)S(1)}, u32[]{:S(2)}, u32[]{:S(2)}) collective-permute-start(bf16[257,128]{1,0:T(8,128)(2,1)S(1)} %pad_maximum_fusion.5), channel_id=1, source_target_pairs={{0,4},{2,6},{4,0},{6,2},{1,5},{3,7},{5,1},{7,3},{8,12},{10,14},{12... | collective-permute-start | bytes 197384 | tf_op jit(solution)/shard_map/ppermute | solution.py:29
  5.6 5.5 %collective-permute-start.1 = (bf16[257,128]{1,0:T(8,128)(2,1)S(1)}, bf16[257,128]{1,0:T(8,128)(2,1)S(1)}, u32[]{:S(2)}, u32[]{:S(2)}) collective-permute-start(bf16[257,128]{1,0:T(8,128)(2,1)S(1)} %pad_maximum_fusion.5), channel_id=1, source_target_pairs={{0,6},{2,4},{4,2},{6,0},{1,7},{3,5},{5,3},{7,1},{8,14},{10,12},{12... | collective-permute-start | bytes 197384 | tf_op jit(solution)/shard_map/ppermute | solution.py:29
  6.6 4.4 %collective-permute-start = (bf16[257,128]{1,0:T(8,128)(2,1)S(1)}, bf16[257,128]{1,0:T(8,128)(2,1)S(1)}, u32[]{:S(2)}, u32[]{:S(2)}) collective-permute-start(bf16[257,128]{1,0:T(8,128)(2,1)S(1)} %pad_maximum_fusion.5), channel_id=1, source_target_pairs={{0,2},{2,0},{4,6},{6,4},{1,3},{3,1},{5,7},{7,5},{8,10},{10,8},{12,... | collective-permute-start | bytes 197384 | tf_op jit(solution)/shard_map/ppermute | solution.py:29
  6.7 5.8 %copy-start = (bf16[128,128]{1,0:T(8,128)(2,1)S(1)}, bf16[128,128]{1,0:T(8,128)(2,1)}, u32[]{:S(2)}) copy-start(bf16[128,128]{1,0:T(8,128)(2,1)} %freq_ref.1) | copy-start | bytes 98308
  11.2 1.2 %collective-permute-start.3 = (bf16[4,128]{1,0:T(4,128)(2,1)S(1)}, bf16[4,128]{1,0:T(4,128)(2,1)S(1)}, u32[]{:S(2)}, u32[]{:S(2)}) collective-permute-start(bf16[4,128]{1,0:T(4,128)(2,1)S(1)} %pad_maximum_fusion.6), channel_id=1, source_target_pairs={{0,1},{1,0},{2,3},{3,2},{4,5},{5,4},{6,7},{7,6},{8,9},{9,8},{10,11... | collective-permute-start | bytes 3080 | tf_op jit(solution)/shard_map/ppermute | solution.py:29
  13.4 1.6 %collective-permute-start.4 = (f16[1024,128]{1,0:T(8,128)(2,1)S(1)}, f16[1024,128]{1,0:T(8,128)(2,1)S(1)}, u32[]{:S(2)}, u32[]{:S(2)}) collective-permute-start(f16[1024,128]{1,0:T(8,128)(2,1)S(1)} %multiply_convert_fusion.1), channel_id=1, source_target_pairs={{0,1},{1,0},{2,3},{3,2},{4,5},{5,4},{6,7},{7,6},{8,9},{9,8},{10,11... | collective-permute-start | bytes 786440 | tf_op jit(solution)/shard_map/ppermute | solution.py:29
  15.2 6.6 %collective-permute-start.5 = (f16[264,128]{1,0:T(8,128)(2,1)S(1)}, f16[264,128]{1,0:T(8,128)(2,1)S(1)}, u32[]{:S(2)}, u32[]{:S(2)}) collective-permute-start(f16[264,128]{1,0:T(8,128)(2,1)S(1)} %get-tuple-element.99), channel_id=1, source_target_pairs={{0,16},{8,24},{16,0},{24,8},{1,17},{9,25},{17,1},{25,9},{2,18},{10... | collective-permute-start | bytes 202760 | tf_op jit(solution)/shard_map/ppermute | solution.py:29
  17.5 5.1 %collective-permute-start.6 = (f16[264,128]{1,0:T(8,128)(2,1)S(1)}, f16[264,128]{1,0:T(8,128)(2,1)S(1)}, u32[]{:S(2)}, u32[]{:S(2)}) collective-permute-start(f16[264,128]{1,0:T(8,128)(2,1)S(1)} %get-tuple-element.100), channel_id=1, source_target_pairs={{0,8},{8,0},{16,24},{24,16},{1,9},{9,1},{17,25},{25,17},{2,10},{10... | collective-permute-start | bytes 202760 | tf_op jit(solution)/shard_map/ppermute | solution.py:29
  19.0 4.3 %collective-permute-start.7 = (f16[264,128]{1,0:T(8,128)(2,1)S(1)}, f16[264,128]{1,0:T(8,128)(2,1)S(1)}, u32[]{:S(2)}, u32[]{:S(2)}) collective-permute-start(f16[264,128]{1,0:T(8,128)(2,1)S(1)} %get-tuple-element.101), channel_id=1, source_target_pairs={{0,24},{8,16},{16,8},{24,0},{1,25},{9,17},{17,9},{25,1},{2,26},{10... | collective-permute-start | bytes 202760 | tf_op jit(solution)/shard_map/ppermute | solution.py:29
  19.5 3.8 %collective-permute-start.8 = (bf16[512,128]{1,0:T(8,128)(2,1)S(1)}, bf16[512,128]{1,0:T(8,128)(2,1)S(1)}, u32[]{:S(2)}, u32[]{:S(2)}) collective-permute-start(bf16[512,128]{1,0:T(8,128)(2,1)S(1)} %pad_maximum_fusion.own_ref), channel_id=1, source_target_pairs={{0,1},{1,0},{2,3},{3,2},{4,5},{5,4},{6,7},{7,6},{8,9},{9,8},{10,11... | collective-permute-start | bytes 393224 | tf_op jit(solution)/shard_map/ppermute | solution.py:29
  23.4 6.0 %collective-permute-start.11 = (f16[256,128]{1,0:T(8,128)(2,1)S(1)}, f16[256,128]{1,0:T(8,128)(2,1)S(1)}, u32[]{:S(2)}, u32[]{:S(2)}) collective-permute-start(f16[256,128]{1,0:T(8,128)(2,1)S(1)} %multiply_convert_fusion.2), channel_id=1, source_target_pairs={{0,4},{2,6},{4,0},{6,2},{1,5},{3,7},{5,1},{7,3},{8,12},{10,14},{12... | collective-permute-start | bytes 196616 | tf_op jit(solution)/shard_map/ppermute | solution.py:29
  25.5 5.5 %collective-permute-start.10 = (f16[256,128]{1,0:T(8,128)(2,1)S(1)}, f16[256,128]{1,0:T(8,128)(2,1)S(1)}, u32[]{:S(2)}, u32[]{:S(2)}) collective-permute-start(f16[256,128]{1,0:T(8,128)(2,1)S(1)} %multiply_convert_fusion.2), channel_id=1, source_target_pairs={{0,6},{2,4},{4,2},{6,0},{1,7},{3,5},{5,3},{7,1},{8,14},{10,12},{12... | collective-permute-start | bytes 196616 | tf_op jit(solution)/shard_map/ppermute | solution.py:29
  26.5 4.4 %collective-permute-start.9 = (f16[256,128]{1,0:T(8,128)(2,1)S(1)}, f16[256,128]{1,0:T(8,128)(2,1)S(1)}, u32[]{:S(2)}, u32[]{:S(2)}) collective-permute-start(f16[256,128]{1,0:T(8,128)(2,1)S(1)} %multiply_convert_fusion.2), channel_id=1, source_target_pairs={{0,2},{2,0},{4,6},{6,4},{1,3},{3,1},{5,7},{7,5},{8,10},{10,8},{12,... | collective-permute-start | bytes 196616 | tf_op jit(solution)/shard_map/ppermute | solution.py:29
  32.6 1.2 %collective-permute-start.12 = (f32[1,128]{1,0:T(1,128)S(1)}, f32[1,128]{1,0:T(1,128)S(1)}, u32[]{:S(2)}, u32[]{:S(2)}) collective-permute-start(f32[1,128]{1,0:T(1,128)S(1)} %get-tuple-element.89), channel_id=1, source_target_pairs={{0,1},{1,0},{2,3},{3,2},{4,5},{5,4},{6,7},{7,6},{8,9},{9,8},{10,11... | collective-permute-start | bytes 1544 | tf_op jit(solution)/shard_map/ppermute | solution.py:29
  50.2 0.6 %copy-start.1 = (f32[128]{0:T(128)}, f32[128]{0:T(128)S(1)}, u32[]{:S(2)}) copy-start(f32[128]{0:T(128)S(1)} %add_sqrt_fusion) | copy-start | bytes 1540

commit v4 on v3

--- a/solution.py
+++ b/solution.py
@@ -124,18 +124,21 @@
     from_near = [[(y ^ i) == k for k in LEAD] for i in range(ys)]
     uy_rows = uy * jnp.uint32(rows)
 
-    place = pl.BlockSpec(memory_space=pltpu.VMEM)
+    pair = swap(window_factor, "c", 1)
     high = channel_factor.astype(bf16)
     low = (channel_factor - high.astype(f32)).astype(bf16)
-    first = jnp.concatenate([freq_factor, high, window_factor, low], axis=0)
-    first, ux, xs_near, own_slots, far_slots, from_near, uy_rows = lax.optimization_barrier(
-        (first, ux, xs_near, own_slots, far_slots, from_near, uy_rows)
+    base = jnp.concatenate([freq_factor, window_factor], axis=0)
+    base, high, low = lax.optimization_barrier((base, high, low))
+    first = jnp.concatenate([base, high, low, pair], axis=0)
+    first, spectrogram, ux, xs_near, own_slots, far_slots, from_near, uy_rows = lax.optimization_barrier(
+        (first, spectrogram, ux, xs_near, own_slots, far_slots, from_near, uy_rows)
     )
     first = [first] + [swap(first, "y", k) for k in LEAD]
-    last = freq_rows + rows
-    line = jnp.concatenate([v[last : last + 1] for v in first], axis=0)
+    line = jnp.concatenate([v[freq_rows : freq_rows + 1] for v in first], axis=0)
+    pair = jnp.concatenate([v[-1:] for v in first], axis=0)
     freqs = jnp.concatenate([v[:freq_rows] for v in first], axis=0)
-    olds = [v[freq_rows:last].astype(f32) + v[last + 1 :].astype(f32) for v in first]
+    last = freq_rows + 1 + rows
+    olds = [v[freq_rows + 1 : last].astype(f32) + v[last:-1].astype(f32) for v in first]
     width = win_rows * freq_rows
     half = jax.ShapeDtypeStruct((chan_rows // 2, width), bf16)
     place = pl.BlockSpec(memory_space=pltpu.VMEM)
@@ -151,8 +154,7 @@
         compiler_params=pltpu.CompilerParams(vmem_limit_bytes=48 * 2**20),
         cost_estimate=pl.CostEstimate(flops=0, bytes_accessed=chan_rows * width * 4, transcendentals=0),
     )(spectrogram)
-    line, freqs, flat_other, flat_mine = lax.optimization_barrier((line, freqs, flat_other, flat_mine))
-    pair = swap(line, "c", 1)
+    line, pair, freqs, flat_other, flat_mine = lax.optimization_barrier((line, pair, freqs, flat_other, flat_mine))
     slot = jnp.arange(win_rows)[:, None]
     block = jnp.zeros((win_rows, rank), f32)
     for i in range(ys):

time: 51.1 us -> 50 us (0.978)
  waiting for transfers between devices: 11.3 us -> 10.4 us
    ppermute x13, waiting for transfers between devices: 11.3 us -> 10.4 us  [swap(): return lax.ppermute(value, axis, [(i, i ^ distance) for i in range(count)])]
  transfers between devices with their start and end apart: 13 -> 13, of which waited for: 9 -> 8; matrix products, arithmetic and copies ran while one was open for 1% -> 4% of each run, Pallas kernels for 8% -> 8%
where the time goes in v4:
time: 50 us; the launch traced here: 49.8 us
  blocking collectives  16.3 us (33%)
  starting transfers between devices  12.5 us (25%)
  waiting for transfers between devices  10.4 us (21%)
  Pallas kernels  6.51 us (13%)
  other arithmetic  2.98 us (6%)
  between operations  0.99 us (2%)
    all_to_all x1, blocking collectives, body(): lax.all_to_all(jnp.broadcast_to(squares, (lines, rank)), ('z', 'x'), 0, 0...  16.3 us
    ppermute x13, starting transfers between devices, swap(): return lax.ppermute(value, axis, [(i, i ^ distance) for i in range(count)])  12.5 us
    ppermute x13, waiting for transfers between devices, swap(): return lax.ppermute(value, axis, [(i, i ^ distance) for i in range(count)])  10.4 us
    pallas_call x4, Pallas kernels, on_vmem(): pl.pallas_call(kernel, out_shape=outs, in_specs=[place] * len(args), out_...  3.84 us
    pallas_call x1, Pallas kernels, body(): pl.pallas_call(flatten_kernel, out_shape=(half, half), in_specs=[pl.Block...  2.67 us
  transfers between devices with their start and end apart: 13, of which 8 were waited for; matrix products, arithmetic and copies ran while one was open for 4% of the time, Pallas kernels for 8%

profile of v4, /device:TPU:2, one launch (start us, length us, event | category | flops | bytes accessed | tf_op | source)
XLA Modules:
  0.0 49.8 jit_solution(13506801825249081558)
XLA Ops:
  0.6 0.1 collective-permute-start
  0.8 0.8 %subtract_convert_fusion = (bf16[64,128]{1,0:T(8,128)(2,1)S(1)}, bf16[64,128]{1,0:T(8,128)(2,1)S(1)}) fusion(f32[64,128]{1,0:T(8,128)} %param.7), kind=kLoop, calls=%fused_computation.24 | loop fusion | flops 32768 | bytes 65536 | tf_op jit(solution)/shard_map/convert_element_type | solution.py:129
  1.6 0.8 %pad_maximum_fusion.6 = bf16[129,128]{1,0:T(8,128)(2,1)S(1)} fusion(bf16[1,128]{1,0:T(2,128)(2,1)} %param.5, bf16[128,128]{1,0:T(8,128)(2,1)} %freq_ref.1), kind=kLoop, calls=%fused_computation.15 | loop fusion | flops 66048 | bytes 66048 | tf_op jit(solution)/shard_map/concatenate | solution.py:130
  2.5 3.3 %collective-permute-start.3 = (bf16[258,128]{1,0:T(8,128)(2,1)S(1)}, bf16[258,128]{1,0:T(8,128)(2,1)S(1)}, u32[]{:S(2)}, u32[]{:S(2)}) collective-permute-start(bf16[258,128]{1,0:T(8,128)(2,1)S(1)} %pad_maximum_fusion.5), channel_id=1, source_target_pairs={{0,4},{2,6},{4,0},{6,2},{1,5},{3,7},{5,1},{7,3},{8,12},{10,14},{12... | collective-permute-start | bytes 198152 | tf_op jit(solution)/shard_map/ppermute | solution.py:29
  5.8 1.1 %collective-permute-start.2 = (bf16[258,128]{1,0:T(8,128)(2,1)S(1)}, bf16[258,128]{1,0:T(8,128)(2,1)S(1)}, u32[]{:S(2)}, u32[]{:S(2)}) collective-permute-start(bf16[258,128]{1,0:T(8,128)(2,1)S(1)} %pad_maximum_fusion.5), channel_id=1, source_target_pairs={{0,6},{2,4},{4,2},{6,0},{1,7},{3,5},{5,3},{7,1},{8,14},{10,12},{12... | collective-permute-start | bytes 198152 | tf_op jit(solution)/shard_map/ppermute | solution.py:29
  6.8 2.7 %shard_map.59 = (bf16[1024,1024]{1,0:T(8,128)(2,1)S(1)}, bf16[1024,1024]{1,0:T(8,128)(2,1)S(1)}) custom-call(bf16[2048,8,128]{2,1,0:T(8,128)(2,1)} %spectrogram_ref), custom_call_target="tpu_custom_call" | custom-call | bytes 8388608 | tf_op jit(solution)/shard_map/pallas_call | solution.py:145
  9.6 1.7 %collective-permute-done.2 = bf16[258,128]{1,0:T(8,128)(2,1)S(1)} collective-permute-done((bf16[258,128]{1,0:T(8,128)(2,1)S(1)}, bf16[258,128]{1,0:T(8,128)(2,1)S(1)}, u32[]{:S(2)}, u32[]{:S(2)}) %collective-permute-start.2) | collective-permute-done | bytes 66080 | tf_op jit(solution)/shard_map/ppermute | solution.py:29
  11.4 0.1 fusion
  11.5 0.8 %shard_map.60 = (f32[1024,128]{1,0:T(8,128)S(1)}, bf16[1024,128]{1,0:T(8,128)(2,1)S(1)}) custom-call(bf16[1024,1024]{1,0:T(8,128)(2,1)S(1)} %get-tuple-element.60.flat_ref, f32[8,128]{1,0:T(8,128)S(1)} %get-tuple-element.103.block_ref, bf16[128,128]{1,0:T(8,128)(2,1)S(1)} %copy-done), custom_call_target="tpu_custom_call" | custom-call | tf_op jit(solution)/shard_map/pallas_call | solution.py:17
  12.3 0.1 collective-permute-start.4
  12.6 0.8 %shard_map.61 = f32[1024,128]{1,0:T(8,128)S(1)} custom-call(bf16[1024,1024]{1,0:T(8,128)(2,1)S(1)} %get-tuple-element.59.flat_ref, bf16[1024,128]{1,0:T(8,128)(2,1)S(1)} %get-tuple-element.71.khatri_rao_ref), custom_call_target="tpu_custom_call" | custom-call | tf_op jit(solution)/shard_map/pallas_call | solution.py:17
  13.4 0.5 %collective-permute-done.4 = f16[1024,128]{1,0:T(8,128)(2,1)S(1)} collective-permute-done((f16[1024,128]{1,0:T(8,128)(2,1)S(1)}, f16[1024,128]{1,0:T(8,128)(2,1)S(1)}, u32[]{:S(2)}, u32[]{:S(2)}) %collective-permute-start.4) | collective-permute-done | bytes 262176 | tf_op jit(solution)/shard_map/ppermute | solution.py:29
  14.0 0.1 multiply_add_fusion
  14.0 0.1 multiply_convert_fusion
  14.2 0.1 pad_maximum_fusion.4
  14.2 2.2 %collective-permute-start.5 = (f16[264,128]{1,0:T(8,128)(2,1)S(1)}, f16[264,128]{1,0:T(8,128)(2,1)S(1)}, u32[]{:S(2)}, u32[]{:S(2)}) collective-permute-start(f16[264,128]{1,0:T(8,128)(2,1)S(1)} %get-tuple-element.117), channel_id=1, source_target_pairs={{0,16},{8,24},{16,0},{24,8},{1,17},{9,25},{17,1},{25,9},{2,18},{10... | collective-permute-start | bytes 202760 | tf_op jit(solution)/shard_map/ppermute | solution.py:29
  16.4 1.5 %collective-permute-start.6 = (f16[264,128]{1,0:T(8,128)(2,1)S(1)}, f16[264,128]{1,0:T(8,128)(2,1)S(1)}, u32[]{:S(2)}, u32[]{:S(2)}) collective-permute-start(f16[264,128]{1,0:T(8,128)(2,1)S(1)} %get-tuple-element.118), channel_id=1, source_target_pairs={{0,8},{8,0},{16,24},{24,16},{1,9},{9,1},{17,25},{25,17},{2,10},{10... | collective-permute-start | bytes 202760 | tf_op jit(solution)/shard_map/ppermute | solution.py:29
  18.0 0.5 %collective-permute-start.7 = (f16[264,128]{1,0:T(8,128)(2,1)S(1)}, f16[264,128]{1,0:T(8,128)(2,1)S(1)}, u32[]{:S(2)}, u32[]{:S(2)}) collective-permute-start(f16[264,128]{1,0:T(8,128)(2,1)S(1)} %get-tuple-element.119), channel_id=1, source_target_pairs={{0,24},{8,16},{16,8},{24,0},{1,25},{9,17},{17,9},{25,1},{2,26},{10... | collective-permute-start | bytes 202760 | tf_op jit(solution)/shard_map/ppermute | solution.py:29
  18.5 2.3 %collective-permute-done.5 = f16[264,128]{1,0:T(8,128)(2,1)S(1)} collective-permute-done((f16[264,128]{1,0:T(8,128)(2,1)S(1)}, f16[264,128]{1,0:T(8,128)(2,1)S(1)}, u32[]{:S(2)}, u32[]{:S(2)}) %collective-permute-start.5) | collective-permute-done | bytes 67616 | tf_op jit(solution)/shard_map/ppermute | solution.py:29
  20.8 0.6 %collective-permute-done.6 = f16[264,128]{1,0:T(8,128)(2,1)S(1)} collective-permute-done((f16[264,128]{1,0:T(8,128)(2,1)S(1)}, f16[264,128]{1,0:T(8,128)(2,1)S(1)}, u32[]{:S(2)}, u32[]{:S(2)}) %collective-permute-start.6) | collective-permute-done | bytes 67616 | tf_op jit(solution)/shard_map/ppermute | solution.py:29
  21.5 0.8 %collective-permute-done.7 = f16[264,128]{1,0:T(8,128)(2,1)S(1)} collective-permute-done((f16[264,128]{1,0:T(8,128)(2,1)S(1)}, f16[264,128]{1,0:T(8,128)(2,1)S(1)}, u32[]{:S(2)}, u32[]{:S(2)}) %collective-permute-start.7) | collective-permute-done | bytes 67616 | tf_op jit(solution)/shard_map/ppermute | solution.py:29
  22.3 2.1 %collective-permute-start.11 = (f16[256,128]{1,0:T(8,128)(2,1)S(1)}, f16[256,128]{1,0:T(8,128)(2,1)S(1)}, u32[]{:S(2)}, u32[]{:S(2)}) collective-permute-start(f16[256,128]{1,0:T(8,128)(2,1)S(1)} %multiply_convert_fusion.2), channel_id=1, source_target_pairs={{0,4},{2,6},{4,0},{6,2},{1,5},{3,7},{5,1},{7,3},{8,12},{10,14},{12... | collective-permute-start | bytes 196616 | tf_op jit(solution)/shard_map/ppermute | solution.py:29
  24.4 1.1 %collective-permute-start.10 = (f16[256,128]{1,0:T(8,128)(2,1)S(1)}, f16[256,128]{1,0:T(8,128)(2,1)S(1)}, u32[]{:S(2)}, u32[]{:S(2)}) collective-permute-start(f16[256,128]{1,0:T(8,128)(2,1)S(1)} %multiply_convert_fusion.2), channel_id=1, source_target_pairs={{0,6},{2,4},{4,2},{6,0},{1,7},{3,5},{5,3},{7,1},{8,14},{10,12},{12... | collective-permute-start | bytes 196616 | tf_op jit(solution)/shard_map/ppermute | solution.py:29
  25.6 0.4 collective-permute-start.9
  25.9 0.7 %shard_map.62 = (f32[128,128]{1,0:T(8,128)S(1)}, f32[128,256]{1,0:T(8,128)S(1)}, f32[128,256]{1,0:T(8,128)S(1)}) custom-call(bf16[512,128]{1,0:T(8,128)(2,1)S(1)} %pad_maximum_fusion.own_ref, bf16[512,128]{1,0:T(8,128)(2,1)S(1)} %collective-permute-done.8.far_ref, bf16[8,128]{1,0:T(8,128)(2,1)S(1)} %get-tuple-element.102.w0_ref, ...), custom_call_target="tpu_custom_call" | custom-call | tf_op jit(solution)/shard_map/pallas_call | solution.py:17
  26.6 1.7 %collective-permute-done.11 = f16[256,128]{1,0:T(8,128)(2,1)S(1)} collective-permute-done((f16[256,128]{1,0:T(8,128)(2,1)S(1)}, f16[256,128]{1,0:T(8,128)(2,1)S(1)}, u32[]{:S(2)}, u32[]{:S(2)}) %collective-permute-start.11) | collective-permute-done | bytes 65568 | tf_op jit(solution)/shard_map/ppermute | solution.py:29
  28.3 1.6 %collective-permute-done.10 = f16[256,128]{1,0:T(8,128)(2,1)S(1)} collective-permute-done((f16[256,128]{1,0:T(8,128)(2,1)S(1)}, f16[256,128]{1,0:T(8,128)(2,1)S(1)}, u32[]{:S(2)}, u32[]{:S(2)}) %collective-permute-start.10) | collective-permute-done | bytes 65568 | tf_op jit(solution)/shard_map/ppermute | solution.py:29
  29.9 1.6 %shard_map.63 = (f32[256,128]{1,0:T(8,128)S(1)}, f32[1,128]{1,0:T(1,128)S(1)}) custom-call(f32[256,128]{1,0:T(8,128)S(1)} %add_add_fusion.mttkrp_ref, f32[128,128]{1,0:T(8,128)S(1)} %get-tuple-element.94.lower_ref, f32[128,256]{1,0:T(8,128)S(1)} %get-tuple-element.95.upper_ref, f32[128,256]{1,0:T(8,128)S(1)} %get-tuple-element.96.inverse_ref), custom_call_target="tpu_custom_call" | custom-call | tf_op jit(solution)/shard_map/pallas_call | solution.py:17
  31.5 0.1 collective-permute-start.12
  31.7 1.1 %collective-permute-done.12 = f32[1,128]{1,0:T(1,128)S(1)} collective-permute-done((f32[1,128]{1,0:T(1,128)S(1)}, f32[1,128]{1,0:T(1,128)S(1)}, u32[]{:S(2)}, u32[]{:S(2)}) %collective-permute-start.12) | collective-permute-done | bytes 544 | tf_op jit(solution)/shard_map/ppermute | solution.py:29
  32.8 16.3 %all_to_all.6 = f32[32,1,128]{2,1,0:T(1,128)S(1)} all-to-all(f32[32,1,128]{2,1,0:T(1,128)S(1)} %broadcast_in_dim.169), channel_id=1, replica_groups={{176,184,192,200,208,216,224,232,240,248,0,8,16,24,32,40,48,56,64,72,80..., dimensions={0} | all-to-all | bytes 32768 | tf_op jit(solution)/shard_map/all_to_all | solution.py:218
  49.1 0.6 %broadcast_divide_fusion = f32[64,128]{1,0:T(8,128)} fusion(f32[64,128]{1,0:T(8,128)S(1)} %constant_dynamic-slice_fusion, f32[128]{0:T(128)S(1)} %add_sqrt_fusion), kind=kLoop, calls=%fused_computation.25 | loop fusion | flops 8192 | bytes 66048 | tf_op jit(solution)/shard_map/div | solution.py:222
  (47 shorter events, 0.6 us)
Async XLA Ops:
  0.6 1.8 %collective-permute-start = (bf16[1,128]{1,0:T(2,128)(2,1)}, bf16[1,128]{1,0:T(2,128)(2,1)S(1)}, u32[]{:S(2)}, u32[]{:S(2)}) collective-permute-start(bf16[1,128]{1,0:T(2,128)(2,1)} %param.5), channel_id=1, source_target_pairs={{0,1},{1,0},{2,3},{3,2},{4,5},{5,4},{6,7},{7,6},{8,9},{9,8},{10,11... | collective-permute-start | bytes 776 | tf_op jit(solution)/shard_map/ppermute | solution.py:29
  2.5 9.0 %copy-start = (bf16[128,128]{1,0:T(8,128)(2,1)S(1)}, bf16[128,128]{1,0:T(8,128)(2,1)}, u32[]{:S(2)}) copy-start(bf16[128,128]{1,0:T(8,128)(2,1)} %freq_ref.1) | copy-start | bytes 98308
  2.5 7.1 %collective-permute-start.3 = (bf16[258,128]{1,0:T(8,128)(2,1)S(1)}, bf16[258,128]{1,0:T(8,128)(2,1)S(1)}, u32[]{:S(2)}, u32[]{:S(2)}) collective-permute-start(bf16[258,128]{1,0:T(8,128)(2,1)S(1)} %pad_maximum_fusion.5), channel_id=1, source_target_pairs={{0,4},{2,6},{4,0},{6,2},{1,5},{3,7},{5,1},{7,3},{8,12},{10,14},{12... | collective-permute-start | bytes 198152 | tf_op jit(solution)/shard_map/ppermute | solution.py:29
  5.8 5.5 %collective-permute-start.2 = (bf16[258,128]{1,0:T(8,128)(2,1)S(1)}, bf16[258,128]{1,0:T(8,128)(2,1)S(1)}, u32[]{:S(2)}, u32[]{:S(2)}) collective-permute-start(bf16[258,128]{1,0:T(8,128)(2,1)S(1)} %pad_maximum_fusion.5), channel_id=1, source_target_pairs={{0,6},{2,4},{4,2},{6,0},{1,7},{3,5},{5,3},{7,1},{8,14},{10,12},{12... | collective-permute-start | bytes 198152 | tf_op jit(solution)/shard_map/ppermute | solution.py:29
  6.8 4.4 %collective-permute-start.1 = (bf16[258,128]{1,0:T(8,128)(2,1)S(1)}, bf16[258,128]{1,0:T(8,128)(2,1)S(1)}, u32[]{:S(2)}, u32[]{:S(2)}) collective-permute-start(bf16[258,128]{1,0:T(8,128)(2,1)S(1)} %pad_maximum_fusion.5), channel_id=1, source_target_pairs={{0,2},{2,0},{4,6},{6,4},{1,3},{3,1},{5,7},{7,5},{8,10},{10,8},{12,... | collective-permute-start | bytes 198152 | tf_op jit(solution)/shard_map/ppermute | solution.py:29
  12.3 1.6 %collective-permute-start.4 = (f16[1024,128]{1,0:T(8,128)(2,1)S(1)}, f16[1024,128]{1,0:T(8,128)(2,1)S(1)}, u32[]{:S(2)}, u32[]{:S(2)}) collective-permute-start(f16[1024,128]{1,0:T(8,128)(2,1)S(1)} %multiply_convert_fusion.1), channel_id=1, source_target_pairs={{0,1},{1,0},{2,3},{3,2},{4,5},{5,4},{6,7},{7,6},{8,9},{9,8},{10,11... | collective-permute-start | bytes 786440 | tf_op jit(solution)/shard_map/ppermute | solution.py:29
  14.2 6.6 %collective-permute-start.5 = (f16[264,128]{1,0:T(8,128)(2,1)S(1)}, f16[264,128]{1,0:T(8,128)(2,1)S(1)}, u32[]{:S(2)}, u32[]{:S(2)}) collective-permute-start(f16[264,128]{1,0:T(8,128)(2,1)S(1)} %get-tuple-element.117), channel_id=1, source_target_pairs={{0,16},{8,24},{16,0},{24,8},{1,17},{9,25},{17,1},{25,9},{2,18},{10... | collective-permute-start | bytes 202760 | tf_op jit(solution)/shard_map/ppermute | solution.py:29
  16.4 5.0 %collective-permute-start.6 = (f16[264,128]{1,0:T(8,128)(2,1)S(1)}, f16[264,128]{1,0:T(8,128)(2,1)S(1)}, u32[]{:S(2)}, u32[]{:S(2)}) collective-permute-start(f16[264,128]{1,0:T(8,128)(2,1)S(1)} %get-tuple-element.118), channel_id=1, source_target_pairs={{0,8},{8,0},{16,24},{24,16},{1,9},{9,1},{17,25},{25,17},{2,10},{10... | collective-permute-start | bytes 202760 | tf_op jit(solution)/shard_map/ppermute | solution.py:29
  18.0 4.3 %collective-permute-start.7 = (f16[264,128]{1,0:T(8,128)(2,1)S(1)}, f16[264,128]{1,0:T(8,128)(2,1)S(1)}, u32[]{:S(2)}, u32[]{:S(2)}) collective-permute-start(f16[264,128]{1,0:T(8,128)(2,1)S(1)} %get-tuple-element.119), channel_id=1, source_target_pairs={{0,24},{8,16},{16,8},{24,0},{1,25},{9,17},{17,9},{25,1},{2,26},{10... | collective-permute-start | bytes 202760 | tf_op jit(solution)/shard_map/ppermute | solution.py:29
  18.5 3.8 %collective-permute-start.8 = (bf16[512,128]{1,0:T(8,128)(2,1)S(1)}, bf16[512,128]{1,0:T(8,128)(2,1)S(1)}, u32[]{:S(2)}, u32[]{:S(2)}) collective-permute-start(bf16[512,128]{1,0:T(8,128)(2,1)S(1)} %pad_maximum_fusion.own_ref), channel_id=1, source_target_pairs={{0,1},{1,0},{2,3},{3,2},{4,5},{5,4},{6,7},{7,6},{8,9},{9,8},{10,11... | collective-permute-start | bytes 393224 | tf_op jit(solution)/shard_map/ppermute | solution.py:29
  22.3 6.0 %collective-permute-start.11 = (f16[256,128]{1,0:T(8,128)(2,1)S(1)}, f16[256,128]{1,0:T(8,128)(2,1)S(1)}, u32[]{:S(2)}, u32[]{:S(2)}) collective-permute-start(f16[256,128]{1,0:T(8,128)(2,1)S(1)} %multiply_convert_fusion.2), channel_id=1, source_target_pairs={{0,4},{2,6},{4,0},{6,2},{1,5},{3,7},{5,1},{7,3},{8,12},{10,14},{12... | collective-permute-start | bytes 196616 | tf_op jit(solution)/shard_map/ppermute | solution.py:29
  24.4 5.5 %collective-permute-start.10 = (f16[256,128]{1,0:T(8,128)(2,1)S(1)}, f16[256,128]{1,0:T(8,128)(2,1)S(1)}, u32[]{:S(2)}, u32[]{:S(2)}) collective-permute-start(f16[256,128]{1,0:T(8,128)(2,1)S(1)} %multiply_convert_fusion.2), channel_id=1, source_target_pairs={{0,6},{2,4},{4,2},{6,0},{1,7},{3,5},{5,3},{7,1},{8,14},{10,12},{12... | collective-permute-start | bytes 196616 | tf_op jit(solution)/shard_map/ppermute | solution.py:29
  25.6 4.3 %collective-permute-start.9 = (f16[256,128]{1,0:T(8,128)(2,1)S(1)}, f16[256,128]{1,0:T(8,128)(2,1)S(1)}, u32[]{:S(2)}, u32[]{:S(2)}) collective-permute-start(f16[256,128]{1,0:T(8,128)(2,1)S(1)} %multiply_convert_fusion.2), channel_id=1, source_target_pairs={{0,2},{2,0},{4,6},{6,4},{1,3},{3,1},{5,7},{7,5},{8,10},{10,8},{12,... | collective-permute-start | bytes 196616 | tf_op jit(solution)/shard_map/ppermute | solution.py:29
  31.5 1.2 %collective-permute-start.12 = (f32[1,128]{1,0:T(1,128)S(1)}, f32[1,128]{1,0:T(1,128)S(1)}, u32[]{:S(2)}, u32[]{:S(2)}) collective-permute-start(f32[1,128]{1,0:T(1,128)S(1)} %get-tuple-element.99), channel_id=1, source_target_pairs={{0,1},{1,0},{2,3},{3,2},{4,5},{5,4},{6,7},{7,6},{8,9},{9,8},{10,11... | collective-permute-start | bytes 1544 | tf_op jit(solution)/shard_map/ppermute | solution.py:29
  49.1 0.6 %copy-start.1 = (f32[128]{0:T(128)}, f32[128]{0:T(128)S(1)}, u32[]{:S(2)}) copy-start(f32[128]{0:T(128)S(1)} %add_sqrt_fusion) | copy-start | bytes 1540

commit v5 on v4

--- a/solution.py
+++ b/solution.py
@@ -7,6 +7,7 @@
 
 f32, bf16, f16 = jnp.float32, jnp.bfloat16, jnp.float16
 DOWN_C, DOWN_X, DOWN_Y = 1.0 / 4, 1.0 / 8, 1.0 / 32
+UP_U = 1024.0
 NEAR = (2, 1, 3)
 LEAD = (1, 3, 2)
 CHUNKS = 16
@@ -48,6 +49,10 @@
         out[chunk * i : chunk * (i + 1), :] = buffer_ref[side, i].reshape(chunk, out.shape[1])
 
 
+def scale_kernel(factor_ref, out_ref):
+    out_ref[...] = factor_ref[...] * UP_U
+
+
 def differ(part):
     lane = lax.broadcasted_iota(jnp.int32, part.shape, 1)
     return jnp.where(lane == 0, part, part - part[:, :1])
@@ -125,20 +130,18 @@
     uy_rows = uy * jnp.uint32(rows)
 
     pair = swap(window_factor, "c", 1)
-    high = channel_factor.astype(bf16)
-    low = (channel_factor - high.astype(f32)).astype(bf16)
     base = jnp.concatenate([freq_factor, window_factor], axis=0)
-    base, high, low = lax.optimization_barrier((base, high, low))
-    first = jnp.concatenate([base, high, low, pair], axis=0)
+    base, factor = lax.optimization_barrier((base, channel_factor))
+    scaled = on_vmem(scale_kernel, jax.ShapeDtypeStruct(factor.shape, f32), factor).astype(f16)
+    first = jnp.concatenate([base.astype(f16), scaled, pair.astype(f16)], axis=0)
     first, spectrogram, ux, xs_near, own_slots, far_slots, from_near, uy_rows = lax.optimization_barrier(
         (first, spectrogram, ux, xs_near, own_slots, far_slots, from_near, uy_rows)
     )
     first = [first] + [swap(first, "y", k) for k in LEAD]
     line = jnp.concatenate([v[freq_rows : freq_rows + 1] for v in first], axis=0)
     pair = jnp.concatenate([v[-1:] for v in first], axis=0)
-    freqs = jnp.concatenate([v[:freq_rows] for v in first], axis=0)
-    last = freq_rows + 1 + rows
-    olds = [v[freq_rows + 1 : last].astype(f32) + v[last:-1].astype(f32) for v in first]
+    freqs = jnp.concatenate([v[:freq_rows] for v in first], axis=0).astype(bf16)
+    olds = [v[freq_rows + 1 : -1].astype(f32) for v in first]
     width = win_rows * freq_rows
     half = jax.ShapeDtypeStruct((chan_rows // 2, width), bf16)
     place = pl.BlockSpec(memory_space=pltpu.VMEM)
@@ -154,7 +157,7 @@
         compiler_params=pltpu.CompilerParams(vmem_limit_bytes=48 * 2**20),
         cost_estimate=pl.CostEstimate(flops=0, bytes_accessed=chan_rows * width * 4, transcendentals=0),
     )(spectrogram)
-    line, pair, freqs, flat_other, flat_mine = lax.optimization_barrier((line, pair, freqs, flat_other, flat_mine))
+    line, pair, flat_other, flat_mine = lax.optimization_barrier((line, pair, flat_other, flat_mine))
     slot = jnp.arange(win_rows)[:, None]
     block = jnp.zeros((win_rows, rank), f32)
     for i in range(ys):
@@ -196,7 +199,7 @@
         freqs,
         freqs_far,
         *windows,
-        jnp.concatenate(ordered, axis=0),
+        jnp.concatenate(ordered, axis=0) * (1.0 / UP_U),
     )
 
     small = (total * DOWN_Y).astype(f16)

time: 50 us -> 49.4 us (0.988)
  waiting for transfers between devices: 10.4 us -> 9.08 us
  other arithmetic: 2.98 us -> 2.1 us
  local copies, waits for them, and re-layouts: 0.13 us -> 0.92 us
  starting transfers between devices: 12.5 us -> 13.1 us
    ppermute x13, waiting for transfers between devices: 10.4 us -> 9.08 us  [swap(): return lax.ppermute(value, axis, [(i, i ^ distance) for i in range(count)])]
    convert_element_type x1 -> x4, other arithmetic: 0.84 us -> 0.07 us  [the longest x1 0.04 us: body(): freqs = jnp.concatenate([v[:freq_rows] for v in first], axis=0).astype(bf16)]
    unnamed x4 -> x6, local copies, waits for them, and re-layouts: 0.01 us -> 0.77 us
    ppermute x13, starting transfers between devices: 12.5 us -> 13.1 us  [swap(): return lax.ppermute(value, axis, [(i, i ^ distance) for i in range(count)])]
    pallas_call x4 -> x5, Pallas kernels: 3.84 us -> 3.84 us  [on_vmem(): pl.pallas_call(kernel, out_shape=outs, in_specs=[place] * len(args), out_...]
  transfers between devices with their start and end apart: 13 -> 13, of which waited for: 8 -> 8; matrix products, arithmetic and copies ran while one was open for 4% -> 2% of each run, Pallas kernels for 8% -> 8%
where the time goes in v5:
time: 49.4 us; the launch traced here: 49.1 us
  blocking collectives  16.4 us (33%)
  starting transfers between devices  13.1 us (27%)
  waiting for transfers between devices  9.08 us (18%)
  Pallas kernels  6.52 us (13%)
  other arithmetic  2.1 us (4%)
  between operations  1.01 us (2%)
  local copies, waits for them, and re-layouts  0.92 us (2%)
    all_to_all x1, blocking collectives, body(): lax.all_to_all(jnp.broadcast_to(squares, (lines, rank)), ('z', 'x'), 0, 0...  16.4 us
    ppermute x13, starting transfers between devices, swap(): return lax.ppermute(value, axis, [(i, i ^ distance) for i in range(count)])  13.1 us
    ppermute x13, waiting for transfers between devices, swap(): return lax.ppermute(value, axis, [(i, i ^ distance) for i in range(count)])  9.08 us
    pallas_call x5, Pallas kernels, on_vmem(): pl.pallas_call(kernel, out_shape=outs, in_specs=[place] * len(args), out_...  3.84 us
    pallas_call x1, Pallas kernels, body(): pl.pallas_call(flatten_kernel, out_shape=(half, half), in_specs=[pl.Block...  2.68 us
  transfers between devices with their start and end apart: 13, of which 8 were waited for; matrix products, arithmetic and copies ran while one was open for 2% of the time, Pallas kernels for 8%

profile of v5, /device:TPU:2, one launch (start us, length us, event | category | flops | bytes accessed | tf_op | source)
XLA Modules:
  0.0 49.1 jit_solution(13704778539172399138)
XLA Ops:
  0.6 0.1 collective-permute-start
  0.8 0.8 %pad_maximum_fusion.4 = bf16[129,128]{1,0:T(8,128)(2,1)S(1)} fusion(bf16[1,128]{1,0:T(2,128)(2,1)} %param.5, bf16[128,128]{1,0:T(8,128)(2,1)} %freq_ref.1), kind=kLoop, calls=%fused_computation.27 | loop fusion | flops 66048 | bytes 66048 | tf_op jit(solution)/shard_map/concatenate | solution.py:133
  1.6 0.8 %copy-done.1 = f32[64,128]{1,0:T(8,128)S(1)} copy-done((f32[64,128]{1,0:T(8,128)S(1)}, f32[64,128]{1,0:T(8,128)}, u32[]{:S(2)}) %copy-start.1) | copy-done | bytes 32792
  2.4 3.3 %collective-permute-start.3 = (f16[194,128]{1,0:T(8,128)(2,1)S(1)}, f16[194,128]{1,0:T(8,128)(2,1)S(1)}, u32[]{:S(2)}, u32[]{:S(2)}) collective-permute-start(f16[194,128]{1,0:T(8,128)(2,1)S(1)} %pad_maximum_fusion.3), channel_id=1, source_target_pairs={{0,4},{2,6},{4,0},{6,2},{1,5},{3,7},{5,1},{7,3},{8,12},{10,14},{12... | collective-permute-start | bytes 149000 | tf_op jit(solution)/shard_map/ppermute | solution.py:30
  5.7 1.1 %collective-permute-start.2 = (f16[194,128]{1,0:T(8,128)(2,1)S(1)}, f16[194,128]{1,0:T(8,128)(2,1)S(1)}, u32[]{:S(2)}, u32[]{:S(2)}) collective-permute-start(f16[194,128]{1,0:T(8,128)(2,1)S(1)} %pad_maximum_fusion.3), channel_id=1, source_target_pairs={{0,6},{2,4},{4,2},{6,0},{1,7},{3,5},{5,3},{7,1},{8,14},{10,12},{12... | collective-permute-start | bytes 149000 | tf_op jit(solution)/shard_map/ppermute | solution.py:30
  6.9 2.7 %shard_map.60 = (bf16[1024,1024]{1,0:T(8,128)(2,1)S(1)}, bf16[1024,1024]{1,0:T(8,128)(2,1)S(1)}) custom-call(bf16[2048,8,128]{2,1,0:T(8,128)(2,1)} %spectrogram_ref), custom_call_target="tpu_custom_call" | custom-call | bytes 8388608 | tf_op jit(solution)/shard_map/pallas_call | solution.py:148
  9.6 1.4 %collective-permute-done.2 = f16[194,128]{1,0:T(8,128)(2,1)S(1)} collective-permute-done((f16[194,128]{1,0:T(8,128)(2,1)S(1)}, f16[194,128]{1,0:T(8,128)(2,1)S(1)}, u32[]{:S(2)}, u32[]{:S(2)}) %collective-permute-start.2) | collective-permute-done | bytes 49696 | tf_op jit(solution)/shard_map/ppermute | solution.py:30
  11.1 0.1 fusion
  11.2 0.8 %shard_map.61 = (f32[1024,128]{1,0:T(8,128)S(1)}, bf16[1024,128]{1,0:T(8,128)(2,1)S(1)}) custom-call(bf16[1024,1024]{1,0:T(8,128)(2,1)S(1)} %get-tuple-element.57.flat_ref, f32[8,128]{1,0:T(8,128)S(1)} %get-tuple-element.99.block_ref, bf16[128,128]{1,0:T(8,128)(2,1)S(1)} %copy-done), custom_call_target="tpu_custom_call" | custom-call | tf_op jit(solution)/shard_map/pallas_call | solution.py:18
  12.1 0.1 collective-permute-start.4
  12.3 0.8 %shard_map.62 = f32[1024,128]{1,0:T(8,128)S(1)} custom-call(bf16[1024,1024]{1,0:T(8,128)(2,1)S(1)} %get-tuple-element.56.flat_ref, bf16[1024,128]{1,0:T(8,128)(2,1)S(1)} %get-tuple-element.68.khatri_rao_ref), custom_call_target="tpu_custom_call" | custom-call | tf_op jit(solution)/shard_map/pallas_call | solution.py:18
  13.1 0.6 %collective-permute-done.4 = f16[1024,128]{1,0:T(8,128)(2,1)S(1)} collective-permute-done((f16[1024,128]{1,0:T(8,128)(2,1)S(1)}, f16[1024,128]{1,0:T(8,128)(2,1)S(1)}, u32[]{:S(2)}, u32[]{:S(2)}) %collective-permute-start.4) | collective-permute-done | bytes 262176 | tf_op jit(solution)/shard_map/ppermute | solution.py:30
  13.7 0.1 multiply_add_fusion
  13.7 0.1 multiply_convert_fusion
  13.9 0.1 pad_maximum_fusion.2
  13.9 2.2 %collective-permute-start.5 = (f16[264,128]{1,0:T(8,128)(2,1)S(1)}, f16[264,128]{1,0:T(8,128)(2,1)S(1)}, u32[]{:S(2)}, u32[]{:S(2)}) collective-permute-start(f16[264,128]{1,0:T(8,128)(2,1)S(1)} %get-tuple-element.115), channel_id=1, source_target_pairs={{0,16},{8,24},{16,0},{24,8},{1,17},{9,25},{17,1},{25,9},{2,18},{10... | collective-permute-start | bytes 202760 | tf_op jit(solution)/shard_map/ppermute | solution.py:30
  16.2 0.1 collective-permute-start.7
  16.3 2.6 %collective-permute-start.6 = (f16[264,128]{1,0:T(8,128)(2,1)S(1)}, f16[264,128]{1,0:T(8,128)(2,1)S(1)}, u32[]{:S(2)}, u32[]{:S(2)}) collective-permute-start(f16[264,128]{1,0:T(8,128)(2,1)S(1)} %get-tuple-element.116), channel_id=1, source_target_pairs={{0,8},{8,0},{16,24},{24,16},{1,9},{9,1},{17,25},{25,17},{2,10},{10... | collective-permute-start | bytes 202760 | tf_op jit(solution)/shard_map/ppermute | solution.py:30
  18.8 1.0 %collective-permute-done.5 = f16[264,128]{1,0:T(8,128)(2,1)S(1)} collective-permute-done((f16[264,128]{1,0:T(8,128)(2,1)S(1)}, f16[264,128]{1,0:T(8,128)(2,1)S(1)}, u32[]{:S(2)}, u32[]{:S(2)}) %collective-permute-start.5) | collective-permute-done | bytes 67616 | tf_op jit(solution)/shard_map/ppermute | solution.py:30
  19.9 1.3 %collective-permute-done.7 = f16[264,128]{1,0:T(8,128)(2,1)S(1)} collective-permute-done((f16[264,128]{1,0:T(8,128)(2,1)S(1)}, f16[264,128]{1,0:T(8,128)(2,1)S(1)}, u32[]{:S(2)}, u32[]{:S(2)}) %collective-permute-start.7) | collective-permute-done | bytes 67616 | tf_op jit(solution)/shard_map/ppermute | solution.py:30
  21.2 0.1 collective-permute-done.6
  21.4 2.3 %collective-permute-start.11 = (f16[256,128]{1,0:T(8,128)(2,1)S(1)}, f16[256,128]{1,0:T(8,128)(2,1)S(1)}, u32[]{:S(2)}, u32[]{:S(2)}) collective-permute-start(f16[256,128]{1,0:T(8,128)(2,1)S(1)} %multiply_convert_fusion.2), channel_id=1, source_target_pairs={{0,4},{2,6},{4,0},{6,2},{1,5},{3,7},{5,1},{7,3},{8,12},{10,14},{12... | collective-permute-start | bytes 196616 | tf_op jit(solution)/shard_map/ppermute | solution.py:30
  23.7 1.1 %collective-permute-start.10 = (f16[256,128]{1,0:T(8,128)(2,1)S(1)}, f16[256,128]{1,0:T(8,128)(2,1)S(1)}, u32[]{:S(2)}, u32[]{:S(2)}) collective-permute-start(f16[256,128]{1,0:T(8,128)(2,1)S(1)} %multiply_convert_fusion.2), channel_id=1, source_target_pairs={{0,6},{2,4},{4,2},{6,0},{1,7},{3,5},{5,3},{7,1},{8,14},{10,12},{12... | collective-permute-start | bytes 196616 | tf_op jit(solution)/shard_map/ppermute | solution.py:30
  24.7 0.2 collective-permute-start.9
  25.0 0.7 %shard_map.63 = (f32[128,128]{1,0:T(8,128)S(1)}, f32[128,256]{1,0:T(8,128)S(1)}, f32[128,256]{1,0:T(8,128)S(1)}) custom-call(bf16[512,128]{1,0:T(8,128)(2,1)S(1)} %maximum_convert_fusion.own_ref, bf16[512,128]{1,0:T(8,128)(2,1)S(1)} %collective-permute-done.8.far_ref, bf16[8,128]{1,0:T(8,128)(2,1)S(1)} %get-tuple-element.98.w0_ref, ...), custom_call_target="tpu_custom_call" | custom-call | tf_op jit(solution)/shard_map/pallas_call | solution.py:18
  25.6 1.6 %collective-permute-done.11 = f16[256,128]{1,0:T(8,128)(2,1)S(1)} collective-permute-done((f16[256,128]{1,0:T(8,128)(2,1)S(1)}, f16[256,128]{1,0:T(8,128)(2,1)S(1)}, u32[]{:S(2)}, u32[]{:S(2)}) %collective-permute-start.11) | collective-permute-done | bytes 65568 | tf_op jit(solution)/shard_map/ppermute | solution.py:30
  27.3 1.9 %collective-permute-done.10 = f16[256,128]{1,0:T(8,128)(2,1)S(1)} collective-permute-done((f16[256,128]{1,0:T(8,128)(2,1)S(1)}, f16[256,128]{1,0:T(8,128)(2,1)S(1)}, u32[]{:S(2)}, u32[]{:S(2)}) %collective-permute-start.10) | collective-permute-done | bytes 65568 | tf_op jit(solution)/shard_map/ppermute | solution.py:30
  29.2 1.6 %shard_map.64 = (f32[256,128]{1,0:T(8,128)S(1)}, f32[1,128]{1,0:T(1,128)S(1)}) custom-call(f32[256,128]{1,0:T(8,128)S(1)} %add_add_fusion.mttkrp_ref, f32[128,128]{1,0:T(8,128)S(1)} %get-tuple-element.90.lower_ref, f32[128,256]{1,0:T(8,128)S(1)} %get-tuple-element.91.upper_ref, f32[128,256]{1,0:T(8,128)S(1)} %get-tuple-element.92.inverse_ref), custom_call_target="tpu_custom_call" | custom-call | tf_op jit(solution)/shard_map/pallas_call | solution.py:18
  30.8 0.1 collective-permute-start.12
  30.9 1.1 %collective-permute-done.12 = f32[1,128]{1,0:T(1,128)S(1)} collective-permute-done((f32[1,128]{1,0:T(1,128)S(1)}, f32[1,128]{1,0:T(1,128)S(1)}, u32[]{:S(2)}, u32[]{:S(2)}) %collective-permute-start.12) | collective-permute-done | bytes 544 | tf_op jit(solution)/shard_map/ppermute | solution.py:30
  32.0 16.4 %all_to_all.6 = f32[32,1,128]{2,1,0:T(1,128)S(1)} all-to-all(f32[32,1,128]{2,1,0:T(1,128)S(1)} %broadcast_in_dim.169), channel_id=1, replica_groups={{176,184,192,200,208,216,224,232,240,248,0,8,16,24,32,40,48,56,64,72,80..., dimensions={0} | all-to-all | bytes 32768 | tf_op jit(solution)/shard_map/all_to_all | solution.py:221
  48.5 0.6 %broadcast_divide_fusion = f32[64,128]{1,0:T(8,128)} fusion(f32[64,128]{1,0:T(8,128)S(1)} %constant_dynamic-slice_fusion, f32[128]{0:T(128)S(1)} %add_sqrt_fusion), kind=kLoop, calls=%fused_computation.28 | loop fusion | flops 8192 | bytes 66048 | tf_op jit(solution)/shard_map/div | solution.py:225
  (50 shorter events, 0.6 us)
Async XLA Ops:
  0.6 1.7 %collective-permute-start = (bf16[1,128]{1,0:T(2,128)(2,1)}, bf16[1,128]{1,0:T(2,128)(2,1)S(1)}, u32[]{:S(2)}, u32[]{:S(2)}) collective-permute-start(bf16[1,128]{1,0:T(2,128)(2,1)} %param.5), channel_id=1, source_target_pairs={{0,1},{1,0},{2,3},{3,2},{4,5},{5,4},{6,7},{7,6},{8,9},{9,8},{10,11... | collective-permute-start | bytes 776 | tf_op jit(solution)/shard_map/ppermute | solution.py:30
  1.6 0.8 %copy-start.1 = (f32[64,128]{1,0:T(8,128)S(1)}, f32[64,128]{1,0:T(8,128)}, u32[]{:S(2)}) copy-start(f32[64,128]{1,0:T(8,128)} %factor_ref) | copy-start | bytes 98308
  2.4 7.1 %collective-permute-start.3 = (f16[194,128]{1,0:T(8,128)(2,1)S(1)}, f16[194,128]{1,0:T(8,128)(2,1)S(1)}, u32[]{:S(2)}, u32[]{:S(2)}) collective-permute-start(f16[194,128]{1,0:T(8,128)(2,1)S(1)} %pad_maximum_fusion.3), channel_id=1, source_target_pairs={{0,4},{2,6},{4,0},{6,2},{1,5},{3,7},{5,1},{7,3},{8,12},{10,14},{12... | collective-permute-start | bytes 149000 | tf_op jit(solution)/shard_map/ppermute | solution.py:30
  5.7 5.3 %collective-permute-start.2 = (f16[194,128]{1,0:T(8,128)(2,1)S(1)}, f16[194,128]{1,0:T(8,128)(2,1)S(1)}, u32[]{:S(2)}, u32[]{:S(2)}) collective-permute-start(f16[194,128]{1,0:T(8,128)(2,1)S(1)} %pad_maximum_fusion.3), channel_id=1, source_target_pairs={{0,6},{2,4},{4,2},{6,0},{1,7},{3,5},{5,3},{7,1},{8,14},{10,12},{12... | collective-permute-start | bytes 149000 | tf_op jit(solution)/shard_map/ppermute | solution.py:30
  6.7 4.3 %collective-permute-start.1 = (f16[194,128]{1,0:T(8,128)(2,1)S(1)}, f16[194,128]{1,0:T(8,128)(2,1)S(1)}, u32[]{:S(2)}, u32[]{:S(2)}) collective-permute-start(f16[194,128]{1,0:T(8,128)(2,1)S(1)} %pad_maximum_fusion.3), channel_id=1, source_target_pairs={{0,2},{2,0},{4,6},{6,4},{1,3},{3,1},{5,7},{7,5},{8,10},{10,8},{12,... | collective-permute-start | bytes 149000 | tf_op jit(solution)/shard_map/ppermute | solution.py:30
  6.8 4.3 %copy-start = (bf16[128,128]{1,0:T(8,128)(2,1)S(1)}, bf16[128,128]{1,0:T(8,128)(2,1)}, u32[]{:S(2)}) copy-start(bf16[128,128]{1,0:T(8,128)(2,1)} %freq_ref.1) | copy-start | bytes 98308
  12.1 1.6 %collective-permute-start.4 = (f16[1024,128]{1,0:T(8,128)(2,1)S(1)}, f16[1024,128]{1,0:T(8,128)(2,1)S(1)}, u32[]{:S(2)}, u32[]{:S(2)}) collective-permute-start(f16[1024,128]{1,0:T(8,128)(2,1)S(1)} %multiply_convert_fusion.1), channel_id=1, source_target_pairs={{0,1},{1,0},{2,3},{3,2},{4,5},{5,4},{6,7},{7,6},{8,9},{9,8},{10,11... | collective-permute-start | bytes 786440 | tf_op jit(solution)/shard_map/ppermute | solution.py:30
  13.9 5.9 %collective-permute-start.5 = (f16[264,128]{1,0:T(8,128)(2,1)S(1)}, f16[264,128]{1,0:T(8,128)(2,1)S(1)}, u32[]{:S(2)}, u32[]{:S(2)}) collective-permute-start(f16[264,128]{1,0:T(8,128)(2,1)S(1)} %get-tuple-element.115), channel_id=1, source_target_pairs={{0,16},{8,24},{16,0},{24,8},{1,17},{9,25},{17,1},{25,9},{2,18},{10... | collective-permute-start | bytes 202760 | tf_op jit(solution)/shard_map/ppermute | solution.py:30
  16.2 5.0 %collective-permute-start.7 = (f16[264,128]{1,0:T(8,128)(2,1)S(1)}, f16[264,128]{1,0:T(8,128)(2,1)S(1)}, u32[]{:S(2)}, u32[]{:S(2)}) collective-permute-start(f16[264,128]{1,0:T(8,128)(2,1)S(1)} %get-tuple-element.117), channel_id=1, source_target_pairs={{0,24},{8,16},{16,8},{24,0},{1,25},{9,17},{17,9},{25,1},{2,26},{10... | collective-permute-start | bytes 202760 | tf_op jit(solution)/shard_map/ppermute | solution.py:30
  16.3 5.0 %collective-permute-start.6 = (f16[264,128]{1,0:T(8,128)(2,1)S(1)}, f16[264,128]{1,0:T(8,128)(2,1)S(1)}, u32[]{:S(2)}, u32[]{:S(2)}) collective-permute-start(f16[264,128]{1,0:T(8,128)(2,1)S(1)} %get-tuple-element.116), channel_id=1, source_target_pairs={{0,8},{8,0},{16,24},{24,16},{1,9},{9,1},{17,25},{25,17},{2,10},{10... | collective-permute-start | bytes 202760 | tf_op jit(solution)/shard_map/ppermute | solution.py:30
  18.8 2.5 %collective-permute-start.8 = (bf16[512,128]{1,0:T(8,128)(2,1)S(1)}, bf16[512,128]{1,0:T(8,128)(2,1)S(1)}, u32[]{:S(2)}, u32[]{:S(2)}) collective-permute-start(bf16[512,128]{1,0:T(8,128)(2,1)S(1)} %maximum_convert_fusion.own_ref), channel_id=1, source_target_pairs={{0,1},{1,0},{2,3},{3,2},{4,5},{5,4},{6,7},{7,6},{8,9},{9,8},{10,11... | collective-permute-start | bytes 393224 | tf_op jit(solution)/shard_map/ppermute | solution.py:30
  21.4 5.9 %collective-permute-start.11 = (f16[256,128]{1,0:T(8,128)(2,1)S(1)}, f16[256,128]{1,0:T(8,128)(2,1)S(1)}, u32[]{:S(2)}, u32[]{:S(2)}) collective-permute-start(f16[256,128]{1,0:T(8,128)(2,1)S(1)} %multiply_convert_fusion.2), channel_id=1, source_target_pairs={{0,4},{2,6},{4,0},{6,2},{1,5},{3,7},{5,1},{7,3},{8,12},{10,14},{12... | collective-permute-start | bytes 196616 | tf_op jit(solution)/shard_map/ppermute | solution.py:30
  23.7 5.5 %collective-permute-start.10 = (f16[256,128]{1,0:T(8,128)(2,1)S(1)}, f16[256,128]{1,0:T(8,128)(2,1)S(1)}, u32[]{:S(2)}, u32[]{:S(2)}) collective-permute-start(f16[256,128]{1,0:T(8,128)(2,1)S(1)} %multiply_convert_fusion.2), channel_id=1, source_target_pairs={{0,6},{2,4},{4,2},{6,0},{1,7},{3,5},{5,3},{7,1},{8,14},{10,12},{12... | collective-permute-start | bytes 196616 | tf_op jit(solution)/shard_map/ppermute | solution.py:30
  24.7 4.4 %collective-permute-start.9 = (f16[256,128]{1,0:T(8,128)(2,1)S(1)}, f16[256,128]{1,0:T(8,128)(2,1)S(1)}, u32[]{:S(2)}, u32[]{:S(2)}) collective-permute-start(f16[256,128]{1,0:T(8,128)(2,1)S(1)} %multiply_convert_fusion.2), channel_id=1, source_target_pairs={{0,2},{2,0},{4,6},{6,4},{1,3},{3,1},{5,7},{7,5},{8,10},{10,8},{12,... | collective-permute-start | bytes 196616 | tf_op jit(solution)/shard_map/ppermute | solution.py:30
  30.8 1.2 %collective-permute-start.12 = (f32[1,128]{1,0:T(1,128)S(1)}, f32[1,128]{1,0:T(1,128)S(1)}, u32[]{:S(2)}, u32[]{:S(2)}) collective-permute-start(f32[1,128]{1,0:T(1,128)S(1)} %get-tuple-element.95), channel_id=1, source_target_pairs={{0,1},{1,0},{2,3},{3,2},{4,5},{5,4},{6,7},{7,6},{8,9},{9,8},{10,11... | collective-permute-start | bytes 1544 | tf_op jit(solution)/shard_map/ppermute | solution.py:30
  48.5 0.6 %copy-start.2 = (f32[128]{0:T(128)}, f32[128]{0:T(128)S(1)}, u32[]{:S(2)}) copy-start(f32[128]{0:T(128)S(1)} %add_sqrt_fusion) | copy-start | bytes 1540

commit v6 on v5

--- a/solution.py
+++ b/solution.py
@@ -74,7 +74,7 @@
     return lax.dot_general(block, block, (((0,), (0,)), ((), ())), preferred_element_type=f32)
 
 
-def gram_kernel(own_ref, far_ref, w0_ref, w2_ref, w1_ref, w3_ref, factor_ref, lower_ref, upper_ref, inverse_ref):
+def gram_kernel(own_ref, far_ref, w0_ref, w2_ref, w1_ref, w3_ref, factor_ref, spread_ref, upper_ref, inverse_ref):
     rank = own_ref.shape[-1]
 
     def paired(own, one, three, two):
@@ -86,7 +86,10 @@
     row = lax.broadcasted_iota(jnp.int32, (rank, rank), 0)
     col = lax.broadcasted_iota(jnp.int32, (rank, rank), 1)
     inverse = 1.0 / jnp.sum(jnp.where(row == col, gram, 0.0), axis=1, keepdims=True)
-    lower_ref[...] = jnp.where(row > col, gram, 0.0) * inverse
+    lower = jnp.where(row > col, gram, 0.0) * inverse
+    for j in range(rank):
+        block = j // 8 * 8
+        spread_ref[j, block:, :] = jnp.broadcast_to(lower[block:, j : j + 1], (rank - block, rank))
     upper = jnp.where(row < col, gram, 0.0) * inverse
     upper_ref[...] = lax.dot_general(
         upper,
@@ -98,21 +101,25 @@
     inverse_ref[...] = jnp.broadcast_to(inverse, inverse_ref.shape)
 
 
-def sweep_kernel(mttkrp_ref, lower_ref, upper_ref, inverse_ref, out_ref, square_ref):
+def sweep_kernel(mttkrp_ref, spread_ref, upper_ref, inverse_ref, out_ref, square_ref):
     coded = mttkrp_ref[...].T * (1.0 / DOWN_Y)
     rank, rows = coded.shape
     row = lax.broadcasted_iota(jnp.int32, (rank, rows), 0)
     mttkrp = jnp.where(row == 0, coded, coded + coded[:1, :])
     start = mttkrp * inverse_ref[...] - upper_ref[...]
-    parts = [start[8 * i : 8 * i + 8] for i in range(rank // 8)]
+    groups = range(rows // rank)
+    parts = [[start[8 * i : 8 * i + 8, rank * g : rank * (g + 1)] for g in groups] for i in range(rank // 8)]
     for j in range(rank):
         block, lane = divmod(j, 8)
-        fresh = jnp.maximum(parts[block], 0.0)[lane : lane + 1, :]
-        fresh = jnp.broadcast_to(fresh, (8, rows))
+        fresh = [
+            jnp.broadcast_to(jnp.maximum(parts[block][g], 0.0)[lane : lane + 1, :], (8, rank)) for g in groups
+        ]
         for i in range(block, rank // 8):
-            column = jnp.broadcast_to(lower_ref[8 * i : 8 * i + 8, j : j + 1], (8, rows))
-            parts[i] = parts[i] - column * fresh
-    updated = jnp.maximum(jnp.concatenate(parts, axis=0), 0.0).T
+            column = spread_ref[j, 8 * i : 8 * i + 8, :]
+            for g in groups:
+                parts[i][g] = parts[i][g] - column * fresh[g]
+    final = jnp.concatenate([jnp.concatenate(p, axis=1) for p in parts], axis=0)
+    updated = jnp.maximum(final, 0.0).T
     out_ref[...] = updated
     square_ref[...] = jnp.sum(updated * updated, axis=0, keepdims=True)
 
@@ -193,9 +200,9 @@
             old = jnp.where(here, v, old)
         ordered.append(old)
     like = jax.ShapeDtypeStruct((rank, ys * rows), f32)
-    lower, upper, inverse = on_vmem(
+    spread, upper, inverse = on_vmem(
         gram_kernel,
-        (jax.ShapeDtypeStruct((rank, rank), f32), like, like),
+        (jax.ShapeDtypeStruct((rank, rank, rank), f32), like, like),
         freqs,
         freqs_far,
         *windows,
@@ -209,7 +216,7 @@
         sweep_kernel,
         (jax.ShapeDtypeStruct((ys * rows, rank), f32), jax.ShapeDtypeStruct((1, rank), f32)),
         mttkrp,
-        lower,
+        spread,
         upper,
         inverse,
     )

time: 49.4 us -> 49.4 us (level)
  Pallas kernels: 6.52 us -> 7.18 us
  starting transfers between devices: 13.1 us -> 12.5 us
    pallas_call x5, Pallas kernels: 3.84 us -> 4.51 us  [on_vmem(): pl.pallas_call(kernel, out_shape=outs, in_specs=[place] * len(args), out_...]
    ppermute x13, starting transfers between devices: 13.1 us -> 12.5 us  [swap(): return lax.ppermute(value, axis, [(i, i ^ distance) for i in range(count)])]
  transfers between devices with their start and end apart: 13 -> 13, of which waited for: 8 -> 8; matrix products, arithmetic and copies ran while one was open for 2% -> 2% of each run, Pallas kernels for 8% -> 11%
where the time goes in v6:
time: 49.4 us; the launch traced here: 49.2 us
  blocking collectives  16.3 us (33%)
  starting transfers between devices  12.5 us (25%)
  waiting for transfers between devices  9.12 us (18%)
  Pallas kernels  7.18 us (15%)
  other arithmetic  2.09 us (4%)
  between operations  0.99 us (2%)
  local copies, waits for them, and re-layouts  0.91 us (2%)
    all_to_all x1, blocking collectives, body(): lax.all_to_all(jnp.broadcast_to(squares, (lines, rank)), ('z', 'x'), 0, 0...  16.3 us
    ppermute x13, starting transfers between devices, swap(): return lax.ppermute(value, axis, [(i, i ^ distance) for i in range(count)])  12.5 us
    ppermute x13, waiting for transfers between devices, swap(): return lax.ppermute(value, axis, [(i, i ^ distance) for i in range(count)])  9.12 us
    pallas_call x5, Pallas kernels, on_vmem(): pl.pallas_call(kernel, out_shape=outs, in_specs=[place] * len(args), out_...  4.51 us
    pallas_call x1, Pallas kernels, body(): pl.pallas_call(flatten_kernel, out_shape=(half, half), in_specs=[pl.Block...  2.67 us
  transfers between devices with their start and end apart: 13, of which 8 were waited for; matrix products, arithmetic and copies ran while one was open for 2% of the time, Pallas kernels for 11%

profile of v6, /device:TPU:2, one launch (start us, length us, event | category | flops | bytes accessed | tf_op | source)
XLA Modules:
  0.0 49.2 jit_solution(5213872464939609460)
XLA Ops:
  0.6 0.1 collective-permute-start
  0.8 0.8 %pad_maximum_fusion.4 = bf16[129,128]{1,0:T(8,128)(2,1)S(1)} fusion(bf16[1,128]{1,0:T(2,128)(2,1)} %param.5, bf16[128,128]{1,0:T(8,128)(2,1)} %freq_ref.1), kind=kLoop, calls=%fused_computation.27 | loop fusion | flops 66048 | bytes 66048 | tf_op jit(solution)/shard_map/concatenate | solution.py:140
  1.6 0.7 %copy-done.1 = f32[64,128]{1,0:T(8,128)S(1)} copy-done((f32[64,128]{1,0:T(8,128)S(1)}, f32[64,128]{1,0:T(8,128)}, u32[]{:S(2)}) %copy-start.1) | copy-done | bytes 32792
  2.4 3.3 %collective-permute-start.3 = (f16[194,128]{1,0:T(8,128)(2,1)S(1)}, f16[194,128]{1,0:T(8,128)(2,1)S(1)}, u32[]{:S(2)}, u32[]{:S(2)}) collective-permute-start(f16[194,128]{1,0:T(8,128)(2,1)S(1)} %pad_maximum_fusion.3), channel_id=1, source_target_pairs={{0,4},{2,6},{4,0},{6,2},{1,5},{3,7},{5,1},{7,3},{8,12},{10,14},{12... | collective-permute-start | bytes 149000 | tf_op jit(solution)/shard_map/ppermute | solution.py:30
  5.8 1.1 %collective-permute-start.2 = (f16[194,128]{1,0:T(8,128)(2,1)S(1)}, f16[194,128]{1,0:T(8,128)(2,1)S(1)}, u32[]{:S(2)}, u32[]{:S(2)}) collective-permute-start(f16[194,128]{1,0:T(8,128)(2,1)S(1)} %pad_maximum_fusion.3), channel_id=1, source_target_pairs={{0,6},{2,4},{4,2},{6,0},{1,7},{3,5},{5,3},{7,1},{8,14},{10,12},{12... | collective-permute-start | bytes 149000 | tf_op jit(solution)/shard_map/ppermute | solution.py:30
  6.9 2.7 %shard_map.60 = (bf16[1024,1024]{1,0:T(8,128)(2,1)S(1)}, bf16[1024,1024]{1,0:T(8,128)(2,1)S(1)}) custom-call(bf16[2048,8,128]{2,1,0:T(8,128)(2,1)} %spectrogram_ref), custom_call_target="tpu_custom_call" | custom-call | bytes 8388608 | tf_op jit(solution)/shard_map/pallas_call | solution.py:155
  9.6 1.6 %collective-permute-done.2 = f16[194,128]{1,0:T(8,128)(2,1)S(1)} collective-permute-done((f16[194,128]{1,0:T(8,128)(2,1)S(1)}, f16[194,128]{1,0:T(8,128)(2,1)S(1)}, u32[]{:S(2)}, u32[]{:S(2)}) %collective-permute-start.2) | collective-permute-done | bytes 49696 | tf_op jit(solution)/shard_map/ppermute | solution.py:30
  11.3 0.1 fusion
  11.4 0.8 %shard_map.61 = (f32[1024,128]{1,0:T(8,128)S(1)}, bf16[1024,128]{1,0:T(8,128)(2,1)S(1)}) custom-call(bf16[1024,1024]{1,0:T(8,128)(2,1)S(1)} %get-tuple-element.57.flat_ref, f32[8,128]{1,0:T(8,128)S(1)} %get-tuple-element.99.block_ref, bf16[128,128]{1,0:T(8,128)(2,1)S(1)} %copy-done), custom_call_target="tpu_custom_call" | custom-call | tf_op jit(solution)/shard_map/pallas_call | solution.py:18
  12.2 0.1 collective-permute-start.4
  12.5 0.8 %shard_map.62 = f32[1024,128]{1,0:T(8,128)S(1)} custom-call(bf16[1024,1024]{1,0:T(8,128)(2,1)S(1)} %get-tuple-element.56.flat_ref, bf16[1024,128]{1,0:T(8,128)(2,1)S(1)} %get-tuple-element.68.khatri_rao_ref), custom_call_target="tpu_custom_call" | custom-call | tf_op jit(solution)/shard_map/pallas_call | solution.py:18
  13.3 0.6 %collective-permute-done.4 = f16[1024,128]{1,0:T(8,128)(2,1)S(1)} collective-permute-done((f16[1024,128]{1,0:T(8,128)(2,1)S(1)}, f16[1024,128]{1,0:T(8,128)(2,1)S(1)}, u32[]{:S(2)}, u32[]{:S(2)}) %collective-permute-start.4) | collective-permute-done | bytes 262176 | tf_op jit(solution)/shard_map/ppermute | solution.py:30
  13.8 0.1 multiply_add_fusion
  13.9 0.1 multiply_convert_fusion
  14.0 0.1 pad_maximum_fusion.2
  14.1 2.2 %collective-permute-start.5 = (f16[264,128]{1,0:T(8,128)(2,1)S(1)}, f16[264,128]{1,0:T(8,128)(2,1)S(1)}, u32[]{:S(2)}, u32[]{:S(2)}) collective-permute-start(f16[264,128]{1,0:T(8,128)(2,1)S(1)} %get-tuple-element.115), channel_id=1, source_target_pairs={{0,16},{8,24},{16,0},{24,8},{1,17},{9,25},{17,1},{25,9},{2,18},{10... | collective-permute-start | bytes 202760 | tf_op jit(solution)/shard_map/ppermute | solution.py:30
  16.3 1.5 %collective-permute-start.6 = (f16[264,128]{1,0:T(8,128)(2,1)S(1)}, f16[264,128]{1,0:T(8,128)(2,1)S(1)}, u32[]{:S(2)}, u32[]{:S(2)}) collective-permute-start(f16[264,128]{1,0:T(8,128)(2,1)S(1)} %get-tuple-element.116), channel_id=1, source_target_pairs={{0,8},{8,0},{16,24},{24,16},{1,9},{9,1},{17,25},{25,17},{2,10},{10... | collective-permute-start | bytes 202760 | tf_op jit(solution)/shard_map/ppermute | solution.py:30
  17.9 0.5 %collective-permute-start.7 = (f16[264,128]{1,0:T(8,128)(2,1)S(1)}, f16[264,128]{1,0:T(8,128)(2,1)S(1)}, u32[]{:S(2)}, u32[]{:S(2)}) collective-permute-start(f16[264,128]{1,0:T(8,128)(2,1)S(1)} %get-tuple-element.117), channel_id=1, source_target_pairs={{0,24},{8,16},{16,8},{24,0},{1,25},{9,17},{17,9},{25,1},{2,26},{10... | collective-permute-start | bytes 202760 | tf_op jit(solution)/shard_map/ppermute | solution.py:30
  18.4 2.3 %collective-permute-done.5 = f16[264,128]{1,0:T(8,128)(2,1)S(1)} collective-permute-done((f16[264,128]{1,0:T(8,128)(2,1)S(1)}, f16[264,128]{1,0:T(8,128)(2,1)S(1)}, u32[]{:S(2)}, u32[]{:S(2)}) %collective-permute-start.5) | collective-permute-done | bytes 67616 | tf_op jit(solution)/shard_map/ppermute | solution.py:30
  20.7 0.6 %collective-permute-done.6 = f16[264,128]{1,0:T(8,128)(2,1)S(1)} collective-permute-done((f16[264,128]{1,0:T(8,128)(2,1)S(1)}, f16[264,128]{1,0:T(8,128)(2,1)S(1)}, u32[]{:S(2)}, u32[]{:S(2)}) %collective-permute-start.6) | collective-permute-done | bytes 67616 | tf_op jit(solution)/shard_map/ppermute | solution.py:30
  21.3 0.8 %collective-permute-done.7 = f16[264,128]{1,0:T(8,128)(2,1)S(1)} collective-permute-done((f16[264,128]{1,0:T(8,128)(2,1)S(1)}, f16[264,128]{1,0:T(8,128)(2,1)S(1)}, u32[]{:S(2)}, u32[]{:S(2)}) %collective-permute-start.7) | collective-permute-done | bytes 67616 | tf_op jit(solution)/shard_map/ppermute | solution.py:30
  22.2 2.2 %collective-permute-start.11 = (f16[256,128]{1,0:T(8,128)(2,1)S(1)}, f16[256,128]{1,0:T(8,128)(2,1)S(1)}, u32[]{:S(2)}, u32[]{:S(2)}) collective-permute-start(f16[256,128]{1,0:T(8,128)(2,1)S(1)} %multiply_convert_fusion.2), channel_id=1, source_target_pairs={{0,4},{2,6},{4,0},{6,2},{1,5},{3,7},{5,1},{7,3},{8,12},{10,14},{12... | collective-permute-start | bytes 196616 | tf_op jit(solution)/shard_map/ppermute | solution.py:30
  24.4 1.1 %collective-permute-start.10 = (f16[256,128]{1,0:T(8,128)(2,1)S(1)}, f16[256,128]{1,0:T(8,128)(2,1)S(1)}, u32[]{:S(2)}, u32[]{:S(2)}) collective-permute-start(f16[256,128]{1,0:T(8,128)(2,1)S(1)} %multiply_convert_fusion.2), channel_id=1, source_target_pairs={{0,6},{2,4},{4,2},{6,0},{1,7},{3,5},{5,3},{7,1},{8,14},{10,12},{12... | collective-permute-start | bytes 196616 | tf_op jit(solution)/shard_map/ppermute | solution.py:30
  25.5 0.3 collective-permute-start.9
  25.8 1.9 %shard_map.63 = (f32[128,128,128]{2,1,0:T(8,128)S(1)}, f32[128,256]{1,0:T(8,128)S(1)}, f32[128,256]{1,0:T(8,128)S(1)}) custom-call(bf16[512,128]{1,0:T(8,128)(2,1)S(1)} %maximum_convert_fusion.own_ref, bf16[512,128]{1,0:T(8,128)(2,1)S(1)} %collective-permute-done.8.far_ref, bf16[8,128]{1,0:T(8,128)(2,1)S(1)} %get-tuple-element.98.w0_ref, ...), custom_call_target="tpu_custom_call" | custom-call | tf_op jit(solution)/shard_map/pallas_call | solution.py:18
  27.7 0.5 collective-permute-done.11
  28.2 1.7 %collective-permute-done.10 = f16[256,128]{1,0:T(8,128)(2,1)S(1)} collective-permute-done((f16[256,128]{1,0:T(8,128)(2,1)S(1)}, f16[256,128]{1,0:T(8,128)(2,1)S(1)}, u32[]{:S(2)}, u32[]{:S(2)}) %collective-permute-start.10) | collective-permute-done | bytes 65568 | tf_op jit(solution)/shard_map/ppermute | solution.py:30
  29.9 1.0 %shard_map.64 = (f32[256,128]{1,0:T(8,128)S(1)}, f32[1,128]{1,0:T(1,128)S(1)}) custom-call(f32[256,128]{1,0:T(8,128)S(1)} %add_add_fusion.mttkrp_ref, f32[128,128,128]{2,1,0:T(8,128)S(1)} %get-tuple-element.90.spread_ref, f32[128,256]{1,0:T(8,128)S(1)} %get-tuple-element.91.upper_ref, f32[128,256]{1,0:T(8,128)S(1)} %get-tuple-element.92.inverse_ref), custom_call_target="tpu_custom_call" | custom-call | tf_op jit(solution)/shard_map/pallas_call | solution.py:18
  30.9 0.1 collective-permute-start.12
  31.1 1.1 %collective-permute-done.12 = f32[1,128]{1,0:T(1,128)S(1)} collective-permute-done((f32[1,128]{1,0:T(1,128)S(1)}, f32[1,128]{1,0:T(1,128)S(1)}, u32[]{:S(2)}, u32[]{:S(2)}) %collective-permute-start.12) | collective-permute-done | bytes 544 | tf_op jit(solution)/shard_map/ppermute | solution.py:30
  32.2 16.3 %all_to_all.6 = f32[32,1,128]{2,1,0:T(1,128)S(1)} all-to-all(f32[32,1,128]{2,1,0:T(1,128)S(1)} %broadcast_in_dim.169), channel_id=1, replica_groups={{176,184,192,200,208,216,224,232,240,248,0,8,16,24,32,40,48,56,64,72,80..., dimensions={0} | all-to-all | bytes 32768 | tf_op jit(solution)/shard_map/all_to_all | solution.py:228
  48.5 0.6 %broadcast_divide_fusion = f32[64,128]{1,0:T(8,128)} fusion(f32[64,128]{1,0:T(8,128)S(1)} %constant_dynamic-slice_fusion, f32[128]{0:T(128)S(1)} %add_sqrt_fusion), kind=kLoop, calls=%fused_computation.28 | loop fusion | flops 8192 | bytes 66048 | tf_op jit(solution)/shard_map/div | solution.py:232
  (50 shorter events, 0.6 us)
Async XLA Ops:
  0.6 10.7 %copy-start = (bf16[128,128]{1,0:T(8,128)(2,1)S(1)}, bf16[128,128]{1,0:T(8,128)(2,1)}, u32[]{:S(2)}) copy-start(bf16[128,128]{1,0:T(8,128)(2,1)} %freq_ref.1) | copy-start | bytes 98308
  0.6 1.7 %collective-permute-start = (bf16[1,128]{1,0:T(2,128)(2,1)}, bf16[1,128]{1,0:T(2,128)(2,1)S(1)}, u32[]{:S(2)}, u32[]{:S(2)}) collective-permute-start(bf16[1,128]{1,0:T(2,128)(2,1)} %param.5), channel_id=1, source_target_pairs={{0,1},{1,0},{2,3},{3,2},{4,5},{5,4},{6,7},{7,6},{8,9},{9,8},{10,11... | collective-permute-start | bytes 776 | tf_op jit(solution)/shard_map/ppermute | solution.py:30
  1.6 0.8 %copy-start.1 = (f32[64,128]{1,0:T(8,128)S(1)}, f32[64,128]{1,0:T(8,128)}, u32[]{:S(2)}) copy-start(f32[64,128]{1,0:T(8,128)} %factor_ref) | copy-start | bytes 98308
  2.4 7.2 %collective-permute-start.3 = (f16[194,128]{1,0:T(8,128)(2,1)S(1)}, f16[194,128]{1,0:T(8,128)(2,1)S(1)}, u32[]{:S(2)}, u32[]{:S(2)}) collective-permute-start(f16[194,128]{1,0:T(8,128)(2,1)S(1)} %pad_maximum_fusion.3), channel_id=1, source_target_pairs={{0,4},{2,6},{4,0},{6,2},{1,5},{3,7},{5,1},{7,3},{8,12},{10,14},{12... | collective-permute-start | bytes 149000 | tf_op jit(solution)/shard_map/ppermute | solution.py:30
  5.8 5.4 %collective-permute-start.2 = (f16[194,128]{1,0:T(8,128)(2,1)S(1)}, f16[194,128]{1,0:T(8,128)(2,1)S(1)}, u32[]{:S(2)}, u32[]{:S(2)}) collective-permute-start(f16[194,128]{1,0:T(8,128)(2,1)S(1)} %pad_maximum_fusion.3), channel_id=1, source_target_pairs={{0,6},{2,4},{4,2},{6,0},{1,7},{3,5},{5,3},{7,1},{8,14},{10,12},{12... | collective-permute-start | bytes 149000 | tf_op jit(solution)/shard_map/ppermute | solution.py:30
  6.9 4.3 %collective-permute-start.1 = (f16[194,128]{1,0:T(8,128)(2,1)S(1)}, f16[194,128]{1,0:T(8,128)(2,1)S(1)}, u32[]{:S(2)}, u32[]{:S(2)}) collective-permute-start(f16[194,128]{1,0:T(8,128)(2,1)S(1)} %pad_maximum_fusion.3), channel_id=1, source_target_pairs={{0,2},{2,0},{4,6},{6,4},{1,3},{3,1},{5,7},{7,5},{8,10},{10,8},{12,... | collective-permute-start | bytes 149000 | tf_op jit(solution)/shard_map/ppermute | solution.py:30
  12.2 1.6 %collective-permute-start.4 = (f16[1024,128]{1,0:T(8,128)(2,1)S(1)}, f16[1024,128]{1,0:T(8,128)(2,1)S(1)}, u32[]{:S(2)}, u32[]{:S(2)}) collective-permute-start(f16[1024,128]{1,0:T(8,128)(2,1)S(1)} %multiply_convert_fusion.1), channel_id=1, source_target_pairs={{0,1},{1,0},{2,3},{3,2},{4,5},{5,4},{6,7},{7,6},{8,9},{9,8},{10,11... | collective-permute-start | bytes 786440 | tf_op jit(solution)/shard_map/ppermute | solution.py:30
  14.1 6.6 %collective-permute-start.5 = (f16[264,128]{1,0:T(8,128)(2,1)S(1)}, f16[264,128]{1,0:T(8,128)(2,1)S(1)}, u32[]{:S(2)}, u32[]{:S(2)}) collective-permute-start(f16[264,128]{1,0:T(8,128)(2,1)S(1)} %get-tuple-element.115), channel_id=1, source_target_pairs={{0,16},{8,24},{16,0},{24,8},{1,17},{9,25},{17,1},{25,9},{2,18},{10... | collective-permute-start | bytes 202760 | tf_op jit(solution)/shard_map/ppermute | solution.py:30
  16.3 5.0 %collective-permute-start.6 = (f16[264,128]{1,0:T(8,128)(2,1)S(1)}, f16[264,128]{1,0:T(8,128)(2,1)S(1)}, u32[]{:S(2)}, u32[]{:S(2)}) collective-permute-start(f16[264,128]{1,0:T(8,128)(2,1)S(1)} %get-tuple-element.116), channel_id=1, source_target_pairs={{0,8},{8,0},{16,24},{24,16},{1,9},{9,1},{17,25},{25,17},{2,10},{10... | collective-permute-start | bytes 202760 | tf_op jit(solution)/shard_map/ppermute | solution.py:30
  17.9 4.3 %collective-permute-start.7 = (f16[264,128]{1,0:T(8,128)(2,1)S(1)}, f16[264,128]{1,0:T(8,128)(2,1)S(1)}, u32[]{:S(2)}, u32[]{:S(2)}) collective-permute-start(f16[264,128]{1,0:T(8,128)(2,1)S(1)} %get-tuple-element.117), channel_id=1, source_target_pairs={{0,24},{8,16},{16,8},{24,0},{1,25},{9,17},{17,9},{25,1},{2,26},{10... | collective-permute-start | bytes 202760 | tf_op jit(solution)/shard_map/ppermute | solution.py:30
  18.4 3.8 %collective-permute-start.8 = (bf16[512,128]{1,0:T(8,128)(2,1)S(1)}, bf16[512,128]{1,0:T(8,128)(2,1)S(1)}, u32[]{:S(2)}, u32[]{:S(2)}) collective-permute-start(bf16[512,128]{1,0:T(8,128)(2,1)S(1)} %maximum_convert_fusion.own_ref), channel_id=1, source_target_pairs={{0,1},{1,0},{2,3},{3,2},{4,5},{5,4},{6,7},{7,6},{8,9},{9,8},{10,11... | collective-permute-start | bytes 393224 | tf_op jit(solution)/shard_map/ppermute | solution.py:30
  22.2 6.0 %collective-permute-start.11 = (f16[256,128]{1,0:T(8,128)(2,1)S(1)}, f16[256,128]{1,0:T(8,128)(2,1)S(1)}, u32[]{:S(2)}, u32[]{:S(2)}) collective-permute-start(f16[256,128]{1,0:T(8,128)(2,1)S(1)} %multiply_convert_fusion.2), channel_id=1, source_target_pairs={{0,4},{2,6},{4,0},{6,2},{1,5},{3,7},{5,1},{7,3},{8,12},{10,14},{12... | collective-permute-start | bytes 196616 | tf_op jit(solution)/shard_map/ppermute | solution.py:30
  24.4 5.5 %collective-permute-start.10 = (f16[256,128]{1,0:T(8,128)(2,1)S(1)}, f16[256,128]{1,0:T(8,128)(2,1)S(1)}, u32[]{:S(2)}, u32[]{:S(2)}) collective-permute-start(f16[256,128]{1,0:T(8,128)(2,1)S(1)} %multiply_convert_fusion.2), channel_id=1, source_target_pairs={{0,6},{2,4},{4,2},{6,0},{1,7},{3,5},{5,3},{7,1},{8,14},{10,12},{12... | collective-permute-start | bytes 196616 | tf_op jit(solution)/shard_map/ppermute | solution.py:30
  25.5 4.4 %collective-permute-start.9 = (f16[256,128]{1,0:T(8,128)(2,1)S(1)}, f16[256,128]{1,0:T(8,128)(2,1)S(1)}, u32[]{:S(2)}, u32[]{:S(2)}) collective-permute-start(f16[256,128]{1,0:T(8,128)(2,1)S(1)} %multiply_convert_fusion.2), channel_id=1, source_target_pairs={{0,2},{2,0},{4,6},{6,4},{1,3},{3,1},{5,7},{7,5},{8,10},{10,8},{12,... | collective-permute-start | bytes 196616 | tf_op jit(solution)/shard_map/ppermute | solution.py:30
  30.9 1.2 %collective-permute-start.12 = (f32[1,128]{1,0:T(1,128)S(1)}, f32[1,128]{1,0:T(1,128)S(1)}, u32[]{:S(2)}, u32[]{:S(2)}) collective-permute-start(f32[1,128]{1,0:T(1,128)S(1)} %get-tuple-element.95), channel_id=1, source_target_pairs={{0,1},{1,0},{2,3},{3,2},{4,5},{5,4},{6,7},{7,6},{8,9},{9,8},{10,11... | collective-permute-start | bytes 1544 | tf_op jit(solution)/shard_map/ppermute | solution.py:30
  48.5 0.6 %copy-start.2 = (f32[128]{0:T(128)}, f32[128]{0:T(128)S(1)}, u32[]{:S(2)}) copy-start(f32[128]{0:T(128)S(1)} %add_sqrt_fusion) | copy-start | bytes 1540

commit v7 on v6

--- a/solution.py
+++ b/solution.py
@@ -179,12 +179,10 @@
     far = swap((other * DOWN_C).astype(f16), "c", 1).astype(f32)
     part = (mine + far * (1.0 / DOWN_C)).reshape(xs, ys * rows, rank)
     total = lax.dynamic_index_in_dim(part, ux, 0, keepdims=False)
-    small = (part * DOWN_X).astype(f16)
+    joined = jnp.broadcast_to(block[None], (xs, win_rows, rank))
+    small = jnp.concatenate([(part * DOWN_X).astype(f16), joined.astype(f16)], axis=1)
     small, freqs = lax.optimization_barrier((small, freqs))
-    pieces = [
-        jnp.concatenate([lax.dynamic_index_in_dim(small, i, 0, keepdims=False), block.astype(f16)], axis=0)
-        for i in xs_near
-    ]
+    pieces = [lax.dynamic_index_in_dim(small, i, 0, keepdims=False) for i in xs_near]
     pieces = [swap(v, "x", k) for v, k in zip(pieces, NEAR)]
     windows = [block.astype(bf16)] + [v[ys * rows :].astype(bf16) for v in pieces]
     two, one, three = (v[: ys * rows].astype(f32) for v in pieces)

time: 49.4 us -> 48.9 us (0.990)
  waiting for transfers between devices: 9.12 us -> 7.84 us
  starting transfers between devices: 12.5 us -> 13.1 us
    ppermute x13, waiting for transfers between devices: 9.12 us -> 7.84 us  [swap(): return lax.ppermute(value, axis, [(i, i ^ distance) for i in range(count)])]
    ppermute x13, starting transfers between devices: 12.5 us -> 13.1 us  [swap(): return lax.ppermute(value, axis, [(i, i ^ distance) for i in range(count)])]
where the time goes in v7:
time: 48.9 us; the launch traced here: 48.6 us
  blocking collectives  16.4 us (34%)
  starting transfers between devices  13.1 us (27%)
  waiting for transfers between devices  7.84 us (16%)
  Pallas kernels  7.18 us (15%)
  other arithmetic  2.1 us (4%)
  between operations  1 us (2%)
  local copies, waits for them, and re-layouts  0.92 us (2%)
    all_to_all x1, blocking collectives, body(): lax.all_to_all(jnp.broadcast_to(squares, (lines, rank)), ('z', 'x'), 0, 0...  16.4 us
    ppermute x13, starting transfers between devices, swap(): return lax.ppermute(value, axis, [(i, i ^ distance) for i in range(count)])  13.1 us
    ppermute x13, waiting for transfers between devices, swap(): return lax.ppermute(value, axis, [(i, i ^ distance) for i in range(count)])  7.84 us
    pallas_call x5, Pallas kernels, on_vmem(): pl.pallas_call(kernel, out_shape=outs, in_specs=[place] * len(args), out_...  4.51 us
    pallas_call x1, Pallas kernels, body(): pl.pallas_call(flatten_kernel, out_shape=(half, half), in_specs=[pl.Block...  2.67 us
  transfers between devices with their start and end apart: 13, of which 8 were waited for; matrix products, arithmetic and copies ran while one was open for 2% of the time, Pallas kernels for 11%

profile of v7, /device:TPU:2, one launch (start us, length us, event | category | flops | bytes accessed | tf_op | source)
XLA Modules:
  0.0 48.6 jit_solution(15077471012038517291)
XLA Ops:
  0.6 0.1 collective-permute-start
  0.8 0.8 %pad_maximum_fusion.2 = bf16[129,128]{1,0:T(8,128)(2,1)S(1)} fusion(bf16[1,128]{1,0:T(2,128)(2,1)} %param.5, bf16[128,128]{1,0:T(8,128)(2,1)} %freq_ref.1), kind=kLoop, calls=%fused_computation.25 | loop fusion | flops 66048 | bytes 66048 | tf_op jit(solution)/shard_map/concatenate | solution.py:140
  1.6 0.7 %copy-done.1 = f32[64,128]{1,0:T(8,128)S(1)} copy-done((f32[64,128]{1,0:T(8,128)S(1)}, f32[64,128]{1,0:T(8,128)}, u32[]{:S(2)}) %copy-start.1) | copy-done | bytes 32792
  2.4 3.3 %collective-permute-start.3 = (f16[194,128]{1,0:T(8,128)(2,1)S(1)}, f16[194,128]{1,0:T(8,128)(2,1)S(1)}, u32[]{:S(2)}, u32[]{:S(2)}) collective-permute-start(f16[194,128]{1,0:T(8,128)(2,1)S(1)} %pad_maximum_fusion.1), channel_id=1, source_target_pairs={{0,4},{2,6},{4,0},{6,2},{1,5},{3,7},{5,1},{7,3},{8,12},{10,14},{12... | collective-permute-start | bytes 149000 | tf_op jit(solution)/shard_map/ppermute | solution.py:30
  5.8 1.1 %collective-permute-start.2 = (f16[194,128]{1,0:T(8,128)(2,1)S(1)}, f16[194,128]{1,0:T(8,128)(2,1)S(1)}, u32[]{:S(2)}, u32[]{:S(2)}) collective-permute-start(f16[194,128]{1,0:T(8,128)(2,1)S(1)} %pad_maximum_fusion.1), channel_id=1, source_target_pairs={{0,6},{2,4},{4,2},{6,0},{1,7},{3,5},{5,3},{7,1},{8,14},{10,12},{12... | collective-permute-start | bytes 149000 | tf_op jit(solution)/shard_map/ppermute | solution.py:30
  6.9 2.7 %shard_map.60 = (bf16[1024,1024]{1,0:T(8,128)(2,1)S(1)}, bf16[1024,1024]{1,0:T(8,128)(2,1)S(1)}) custom-call(bf16[2048,8,128]{2,1,0:T(8,128)(2,1)} %spectrogram_ref), custom_call_target="tpu_custom_call" | custom-call | bytes 8388608 | tf_op jit(solution)/shard_map/pallas_call | solution.py:155
  9.6 1.6 %collective-permute-done.2 = f16[194,128]{1,0:T(8,128)(2,1)S(1)} collective-permute-done((f16[194,128]{1,0:T(8,128)(2,1)S(1)}, f16[194,128]{1,0:T(8,128)(2,1)S(1)}, u32[]{:S(2)}, u32[]{:S(2)}) %collective-permute-start.2) | collective-permute-done | bytes 49696 | tf_op jit(solution)/shard_map/ppermute | solution.py:30
  11.3 0.1 fusion
  11.4 0.8 %shard_map.61 = (f32[1024,128]{1,0:T(8,128)S(1)}, bf16[1024,128]{1,0:T(8,128)(2,1)S(1)}) custom-call(bf16[1024,1024]{1,0:T(8,128)(2,1)S(1)} %get-tuple-element.57.flat_ref, f32[8,128]{1,0:T(8,128)S(1)} %get-tuple-element.99.block_ref, bf16[128,128]{1,0:T(8,128)(2,1)S(1)} %copy-done), custom_call_target="tpu_custom_call" | custom-call | tf_op jit(solution)/shard_map/pallas_call | solution.py:18
  12.2 0.1 collective-permute-start.4
  12.5 0.8 %shard_map.62 = f32[1024,128]{1,0:T(8,128)S(1)} custom-call(bf16[1024,1024]{1,0:T(8,128)(2,1)S(1)} %get-tuple-element.56.flat_ref, bf16[1024,128]{1,0:T(8,128)(2,1)S(1)} %get-tuple-element.68.khatri_rao_ref), custom_call_target="tpu_custom_call" | custom-call | tf_op jit(solution)/shard_map/pallas_call | solution.py:18
  13.3 0.6 %collective-permute-done.4 = f16[1024,128]{1,0:T(8,128)(2,1)S(1)} collective-permute-done((f16[1024,128]{1,0:T(8,128)(2,1)S(1)}, f16[1024,128]{1,0:T(8,128)(2,1)S(1)}, u32[]{:S(2)}, u32[]{:S(2)}) %collective-permute-start.4) | collective-permute-done | bytes 262176 | tf_op jit(solution)/shard_map/ppermute | solution.py:30
  13.8 0.1 multiply_add_fusion
  13.9 0.1 multiply_convert_fusion
  14.0 0.1 pad_maximum_fusion
  14.1 2.2 %collective-permute-start.5 = (f16[264,128]{1,0:T(8,128)(2,1)S(1)}, f16[264,128]{1,0:T(8,128)(2,1)S(1)}, u32[]{:S(2)}, u32[]{:S(2)}) collective-permute-start(f16[264,128]{1,0:T(8,128)(2,1)S(1)} %get-tuple-element.100), channel_id=1, source_target_pairs={{0,16},{8,24},{16,0},{24,8},{1,17},{9,25},{17,1},{25,9},{2,18},{10... | collective-permute-start | bytes 202760 | tf_op jit(solution)/shard_map/ppermute | solution.py:30
  16.4 0.1 collective-permute-start.7
  16.5 2.6 %collective-permute-start.6 = (f16[264,128]{1,0:T(8,128)(2,1)S(1)}, f16[264,128]{1,0:T(8,128)(2,1)S(1)}, u32[]{:S(2)}, u32[]{:S(2)}) collective-permute-start(f16[264,128]{1,0:T(8,128)(2,1)S(1)} %get-tuple-element.102), channel_id=1, source_target_pairs={{0,8},{8,0},{16,24},{24,16},{1,9},{9,1},{17,25},{25,17},{2,10},{10... | collective-permute-start | bytes 202760 | tf_op jit(solution)/shard_map/ppermute | solution.py:30
  19.0 1.0 %collective-permute-done.5 = f16[264,128]{1,0:T(8,128)(2,1)S(1)} collective-permute-done((f16[264,128]{1,0:T(8,128)(2,1)S(1)}, f16[264,128]{1,0:T(8,128)(2,1)S(1)}, u32[]{:S(2)}, u32[]{:S(2)}) %collective-permute-start.5) | collective-permute-done | bytes 67616 | tf_op jit(solution)/shard_map/ppermute | solution.py:30
  20.1 1.3 %collective-permute-done.7 = f16[264,128]{1,0:T(8,128)(2,1)S(1)} collective-permute-done((f16[264,128]{1,0:T(8,128)(2,1)S(1)}, f16[264,128]{1,0:T(8,128)(2,1)S(1)}, u32[]{:S(2)}, u32[]{:S(2)}) %collective-permute-start.7) | collective-permute-done | bytes 67616 | tf_op jit(solution)/shard_map/ppermute | solution.py:30
  21.4 0.1 collective-permute-done.6
  21.6 2.2 %collective-permute-start.11 = (f16[256,128]{1,0:T(8,128)(2,1)S(1)}, f16[256,128]{1,0:T(8,128)(2,1)S(1)}, u32[]{:S(2)}, u32[]{:S(2)}) collective-permute-start(f16[256,128]{1,0:T(8,128)(2,1)S(1)} %multiply_convert_fusion.2), channel_id=1, source_target_pairs={{0,4},{2,6},{4,0},{6,2},{1,5},{3,7},{5,1},{7,3},{8,12},{10,14},{12... | collective-permute-start | bytes 196616 | tf_op jit(solution)/shard_map/ppermute | solution.py:30
  23.8 1.1 %collective-permute-start.10 = (f16[256,128]{1,0:T(8,128)(2,1)S(1)}, f16[256,128]{1,0:T(8,128)(2,1)S(1)}, u32[]{:S(2)}, u32[]{:S(2)}) collective-permute-start(f16[256,128]{1,0:T(8,128)(2,1)S(1)} %multiply_convert_fusion.2), channel_id=1, source_target_pairs={{0,6},{2,4},{4,2},{6,0},{1,7},{3,5},{5,3},{7,1},{8,14},{10,12},{12... | collective-permute-start | bytes 196616 | tf_op jit(solution)/shard_map/ppermute | solution.py:30
  24.8 0.3 collective-permute-start.9
  25.2 1.9 %shard_map.63 = (f32[128,128,128]{2,1,0:T(8,128)S(1)}, f32[128,256]{1,0:T(8,128)S(1)}, f32[128,256]{1,0:T(8,128)S(1)}) custom-call(bf16[512,128]{1,0:T(8,128)(2,1)S(1)} %maximum_convert_fusion.own_ref, bf16[512,128]{1,0:T(8,128)(2,1)S(1)} %collective-permute-done.8.far_ref, bf16[8,128]{1,0:T(8,128)(2,1)S(1)} %get-tuple-element.98.w0_ref, ...), custom_call_target="tpu_custom_call" | custom-call | tf_op jit(solution)/shard_map/pallas_call | solution.py:18
  27.1 0.4 collective-permute-done.11
  27.5 1.8 %collective-permute-done.10 = f16[256,128]{1,0:T(8,128)(2,1)S(1)} collective-permute-done((f16[256,128]{1,0:T(8,128)(2,1)S(1)}, f16[256,128]{1,0:T(8,128)(2,1)S(1)}, u32[]{:S(2)}, u32[]{:S(2)}) %collective-permute-start.10) | collective-permute-done | bytes 65568 | tf_op jit(solution)/shard_map/ppermute | solution.py:30
  29.3 1.0 %shard_map.64 = (f32[256,128]{1,0:T(8,128)S(1)}, f32[1,128]{1,0:T(1,128)S(1)}) custom-call(f32[256,128]{1,0:T(8,128)S(1)} %add_add_fusion.mttkrp_ref, f32[128,128,128]{2,1,0:T(8,128)S(1)} %get-tuple-element.90.spread_ref, f32[128,256]{1,0:T(8,128)S(1)} %get-tuple-element.91.upper_ref, f32[128,256]{1,0:T(8,128)S(1)} %get-tuple-element.92.inverse_ref), custom_call_target="tpu_custom_call" | custom-call | tf_op jit(solution)/shard_map/pallas_call | solution.py:18
  30.3 0.1 collective-permute-start.12
  30.4 1.1 %collective-permute-done.12 = f32[1,128]{1,0:T(1,128)S(1)} collective-permute-done((f32[1,128]{1,0:T(1,128)S(1)}, f32[1,128]{1,0:T(1,128)S(1)}, u32[]{:S(2)}, u32[]{:S(2)}) %collective-permute-start.12) | collective-permute-done | bytes 544 | tf_op jit(solution)/shard_map/ppermute | solution.py:30
  31.5 16.4 %all_to_all.6 = f32[32,1,128]{2,1,0:T(1,128)S(1)} all-to-all(f32[32,1,128]{2,1,0:T(1,128)S(1)} %broadcast_in_dim.176), channel_id=1, replica_groups={{176,184,192,200,208,216,224,232,240,248,0,8,16,24,32,40,48,56,64,72,80..., dimensions={0} | all-to-all | bytes 32768 | tf_op jit(solution)/shard_map/all_to_all | solution.py:226
  48.0 0.6 %broadcast_divide_fusion = f32[64,128]{1,0:T(8,128)} fusion(f32[64,128]{1,0:T(8,128)S(1)} %constant_dynamic-slice_fusion, f32[128]{0:T(128)S(1)} %add_sqrt_fusion), kind=kLoop, calls=%fused_computation.26 | loop fusion | flops 8192 | bytes 66048 | tf_op jit(solution)/shard_map/div | solution.py:230
  (51 shorter events, 0.6 us)
Async XLA Ops:
  0.6 10.7 %copy-start = (bf16[128,128]{1,0:T(8,128)(2,1)S(1)}, bf16[128,128]{1,0:T(8,128)(2,1)}, u32[]{:S(2)}) copy-start(bf16[128,128]{1,0:T(8,128)(2,1)} %freq_ref.1) | copy-start | bytes 98308
  0.6 1.7 %collective-permute-start = (bf16[1,128]{1,0:T(2,128)(2,1)}, bf16[1,128]{1,0:T(2,128)(2,1)S(1)}, u32[]{:S(2)}, u32[]{:S(2)}) collective-permute-start(bf16[1,128]{1,0:T(2,128)(2,1)} %param.5), channel_id=1, source_target_pairs={{0,1},{1,0},{2,3},{3,2},{4,5},{5,4},{6,7},{7,6},{8,9},{9,8},{10,11... | collective-permute-start | bytes 776 | tf_op jit(solution)/shard_map/ppermute | solution.py:30
  1.6 0.8 %copy-start.1 = (f32[64,128]{1,0:T(8,128)S(1)}, f32[64,128]{1,0:T(8,128)}, u32[]{:S(2)}) copy-start(f32[64,128]{1,0:T(8,128)} %factor_ref) | copy-start | bytes 98308
  2.4 7.2 %collective-permute-start.3 = (f16[194,128]{1,0:T(8,128)(2,1)S(1)}, f16[194,128]{1,0:T(8,128)(2,1)S(1)}, u32[]{:S(2)}, u32[]{:S(2)}) collective-permute-start(f16[194,128]{1,0:T(8,128)(2,1)S(1)} %pad_maximum_fusion.1), channel_id=1, source_target_pairs={{0,4},{2,6},{4,0},{6,2},{1,5},{3,7},{5,1},{7,3},{8,12},{10,14},{12... | collective-permute-start | bytes 149000 | tf_op jit(solution)/shard_map/ppermute | solution.py:30
  5.8 5.4 %collective-permute-start.2 = (f16[194,128]{1,0:T(8,128)(2,1)S(1)}, f16[194,128]{1,0:T(8,128)(2,1)S(1)}, u32[]{:S(2)}, u32[]{:S(2)}) collective-permute-start(f16[194,128]{1,0:T(8,128)(2,1)S(1)} %pad_maximum_fusion.1), channel_id=1, source_target_pairs={{0,6},{2,4},{4,2},{6,0},{1,7},{3,5},{5,3},{7,1},{8,14},{10,12},{12... | collective-permute-start | bytes 149000 | tf_op jit(solution)/shard_map/ppermute | solution.py:30
  6.9 4.3 %collective-permute-start.1 = (f16[194,128]{1,0:T(8,128)(2,1)S(1)}, f16[194,128]{1,0:T(8,128)(2,1)S(1)}, u32[]{:S(2)}, u32[]{:S(2)}) collective-permute-start(f16[194,128]{1,0:T(8,128)(2,1)S(1)} %pad_maximum_fusion.1), channel_id=1, source_target_pairs={{0,2},{2,0},{4,6},{6,4},{1,3},{3,1},{5,7},{7,5},{8,10},{10,8},{12,... | collective-permute-start | bytes 149000 | tf_op jit(solution)/shard_map/ppermute | solution.py:30
  12.2 1.6 %collective-permute-start.4 = (f16[1024,128]{1,0:T(8,128)(2,1)S(1)}, f16[1024,128]{1,0:T(8,128)(2,1)S(1)}, u32[]{:S(2)}, u32[]{:S(2)}) collective-permute-start(f16[1024,128]{1,0:T(8,128)(2,1)S(1)} %multiply_convert_fusion.1), channel_id=1, source_target_pairs={{0,1},{1,0},{2,3},{3,2},{4,5},{5,4},{6,7},{7,6},{8,9},{9,8},{10,11... | collective-permute-start | bytes 786440 | tf_op jit(solution)/shard_map/ppermute | solution.py:30
  14.1 5.9 %collective-permute-start.5 = (f16[264,128]{1,0:T(8,128)(2,1)S(1)}, f16[264,128]{1,0:T(8,128)(2,1)S(1)}, u32[]{:S(2)}, u32[]{:S(2)}) collective-permute-start(f16[264,128]{1,0:T(8,128)(2,1)S(1)} %get-tuple-element.100), channel_id=1, source_target_pairs={{0,16},{8,24},{16,0},{24,8},{1,17},{9,25},{17,1},{25,9},{2,18},{10... | collective-permute-start | bytes 202760 | tf_op jit(solution)/shard_map/ppermute | solution.py:30
  16.4 5.0 %collective-permute-start.7 = (f16[264,128]{1,0:T(8,128)(2,1)S(1)}, f16[264,128]{1,0:T(8,128)(2,1)S(1)}, u32[]{:S(2)}, u32[]{:S(2)}) collective-permute-start(f16[264,128]{1,0:T(8,128)(2,1)S(1)} %get-tuple-element.101), channel_id=1, source_target_pairs={{0,24},{8,16},{16,8},{24,0},{1,25},{9,17},{17,9},{25,1},{2,26},{10... | collective-permute-start | bytes 202760 | tf_op jit(solution)/shard_map/ppermute | solution.py:30
  16.5 5.0 %collective-permute-start.6 = (f16[264,128]{1,0:T(8,128)(2,1)S(1)}, f16[264,128]{1,0:T(8,128)(2,1)S(1)}, u32[]{:S(2)}, u32[]{:S(2)}) collective-permute-start(f16[264,128]{1,0:T(8,128)(2,1)S(1)} %get-tuple-element.102), channel_id=1, source_target_pairs={{0,8},{8,0},{16,24},{24,16},{1,9},{9,1},{17,25},{25,17},{2,10},{10... | collective-permute-start | bytes 202760 | tf_op jit(solution)/shard_map/ppermute | solution.py:30
  19.0 2.5 %collective-permute-start.8 = (bf16[512,128]{1,0:T(8,128)(2,1)S(1)}, bf16[512,128]{1,0:T(8,128)(2,1)S(1)}, u32[]{:S(2)}, u32[]{:S(2)}) collective-permute-start(bf16[512,128]{1,0:T(8,128)(2,1)S(1)} %maximum_convert_fusion.own_ref), channel_id=1, source_target_pairs={{0,1},{1,0},{2,3},{3,2},{4,5},{5,4},{6,7},{7,6},{8,9},{9,8},{10,11... | collective-permute-start | bytes 393224 | tf_op jit(solution)/shard_map/ppermute | solution.py:30
  21.6 5.9 %collective-permute-start.11 = (f16[256,128]{1,0:T(8,128)(2,1)S(1)}, f16[256,128]{1,0:T(8,128)(2,1)S(1)}, u32[]{:S(2)}, u32[]{:S(2)}) collective-permute-start(f16[256,128]{1,0:T(8,128)(2,1)S(1)} %multiply_convert_fusion.2), channel_id=1, source_target_pairs={{0,4},{2,6},{4,0},{6,2},{1,5},{3,7},{5,1},{7,3},{8,12},{10,14},{12... | collective-permute-start | bytes 196616 | tf_op jit(solution)/shard_map/ppermute | solution.py:30
  23.8 5.5 %collective-permute-start.10 = (f16[256,128]{1,0:T(8,128)(2,1)S(1)}, f16[256,128]{1,0:T(8,128)(2,1)S(1)}, u32[]{:S(2)}, u32[]{:S(2)}) collective-permute-start(f16[256,128]{1,0:T(8,128)(2,1)S(1)} %multiply_convert_fusion.2), channel_id=1, source_target_pairs={{0,6},{2,4},{4,2},{6,0},{1,7},{3,5},{5,3},{7,1},{8,14},{10,12},{12... | collective-permute-start | bytes 196616 | tf_op jit(solution)/shard_map/ppermute | solution.py:30
  24.8 4.4 %collective-permute-start.9 = (f16[256,128]{1,0:T(8,128)(2,1)S(1)}, f16[256,128]{1,0:T(8,128)(2,1)S(1)}, u32[]{:S(2)}, u32[]{:S(2)}) collective-permute-start(f16[256,128]{1,0:T(8,128)(2,1)S(1)} %multiply_convert_fusion.2), channel_id=1, source_target_pairs={{0,2},{2,0},{4,6},{6,4},{1,3},{3,1},{5,7},{7,5},{8,10},{10,8},{12,... | collective-permute-start | bytes 196616 | tf_op jit(solution)/shard_map/ppermute | solution.py:30
  30.3 1.2 %collective-permute-start.12 = (f32[1,128]{1,0:T(1,128)S(1)}, f32[1,128]{1,0:T(1,128)S(1)}, u32[]{:S(2)}, u32[]{:S(2)}) collective-permute-start(f32[1,128]{1,0:T(1,128)S(1)} %get-tuple-element.95), channel_id=1, source_target_pairs={{0,1},{1,0},{2,3},{3,2},{4,5},{5,4},{6,7},{7,6},{8,9},{9,8},{10,11... | collective-permute-start | bytes 1544 | tf_op jit(solution)/shard_map/ppermute | solution.py:30
  48.0 0.6 %copy-start.2 = (f32[128]{0:T(128)}, f32[128]{0:T(128)S(1)}, u32[]{:S(2)}) copy-start(f32[128]{0:T(128)S(1)} %add_sqrt_fusion) | copy-start | bytes 1540
